TPU v7x, 256 devices: a whole 4x4x8 slice. The times are simulated.
256 devices in a mesh: row: 8 (over y, x_hi), col: 32 (over x_lo, z, core).
Axes of the slice: x: 4 (x_hi: 2, x_lo: 2; x = x_hi * 2 + x_lo), y: 4, z: 8, core: 2. Of those that a mesh axis runs over, the one named last changes fastest.
Arguments:
- pair: bfloat16 [1024, 1024, 128], P('row', 'col'), may hold values from -6 to 6
- layernorm_gain: float32 [128], replicated, may hold values from 0.25 to 1.75
- layernorm_bias: float32 [128], replicated, may hold values from -3 to 3
- proj_weight: bfloat16 [128, 512], replicated, may hold values from -0.5 to 0.5
- product_grad: bfloat16 [1024, 1024, 128], P('row', 'col'), may hold values from -0.1875 to 0.1875
Outputs:
- pairwise_gradient: bfloat16 [1024, 1024, 128], P('row', 'col')
- proj_grad: float32 [128, 512], replicated
- layernorm_gradient: float32 [2, 128], replicated
All inputs are finite; a program needn't handle non-finite values.
Results may differ from a plain program's by a relative error of at most 0.0072.
Values may be sent and summed in bfloat16 or wider, within the bound.
No kernel may reach another device: no remote copies, remote signals or barrier semaphores. Data moves between devices by JAX's collectives and lax.ppermute only.
A program may use at most 128 MiB of HBM per device.

v0:
```python
import jax
import jax.numpy as jnp
from jax import lax
from jax.sharding import PartitionSpec as P


def per_device(pair, layernorm_gain, layernorm_bias, proj_weight, product_grad):
    rows, cols, width = pair.shape
    hidden = proj_weight.shape[1] // 4
    total = rows * lax.axis_size("row")
    count = rows * cols
    flat = pair.reshape(count, width).astype(jnp.float32)
    row_mean = jnp.mean(flat, axis=1, keepdims=True)
    centred_input = flat - row_mean
    inverse_deviation = lax.rsqrt(
        jnp.mean(centred_input * centred_input, axis=1, keepdims=True) + 1e-05
    )
    standardized_input = centred_input * inverse_deviation
    normalized_input = (standardized_input * layernorm_gain + layernorm_bias).astype(jnp.bfloat16)
    proj_t = lax.dot_general(
        proj_weight, normalized_input, (((0,), (1,)), ((), ())), preferred_element_type=jnp.float32
    )
    pa, ga, pb, gb = (
        proj_t[:hidden],
        proj_t[hidden : 2 * hidden],
        proj_t[2 * hidden : 3 * hidden],
        proj_t[3 * hidden :],
    )
    sa = jax.nn.sigmoid(ga)
    sb = jax.nn.sigmoid(gb)
    left = (sa * pa).astype(jnp.bfloat16).reshape(hidden, rows, cols)
    right = (sb * pb).astype(jnp.bfloat16).reshape(hidden, rows, cols)
    grad_major = jnp.transpose(product_grad, (2, 0, 1))
    left_ch, right_ch, grad_ch = (
        lax.all_to_all(left, "col", split_axis=0, concat_axis=2, tiled=True),
        lax.all_to_all(right, "col", split_axis=0, concat_axis=2, tiled=True),
        lax.all_to_all(grad_major, "col", split_axis=0, concat_axis=2, tiled=True),
    )
    mine = lax.axis_index("row") * rows
    right_piece = lax.all_gather(right_ch, "row", axis=1, tiled=True)
    grad_piece = lax.all_gather(grad_ch, "row", axis=1, tiled=True)
    left_piece = lax.all_gather(left_ch, "row", axis=1, tiled=True)
    first = jnp.einsum("hij,hjk->hik", grad_ch, right_piece, preferred_element_type=jnp.float32)
    own_cols = lax.dynamic_slice_in_dim(grad_piece, mine, rows, 2)
    second = jnp.einsum("hij,hik->hjk", own_cols, left_piece, preferred_element_type=jnp.float32)
    left_back, right_back = (
        lax.all_to_all(first.astype(jnp.bfloat16), "col", split_axis=2, concat_axis=0, tiled=True),
        lax.all_to_all(second.astype(jnp.bfloat16), "col", split_axis=2, concat_axis=0, tiled=True),
    )
    left_back = left_back.reshape(hidden, count).astype(jnp.float32)
    right_back = right_back.reshape(hidden, count).astype(jnp.float32)
    dproj_t = jnp.concatenate(
        [
            left_back * sa,
            left_back * pa * sa * (1.0 - sa),
            right_back * sb,
            right_back * pb * sb * (1.0 - sb),
        ],
        axis=0,
    ).astype(jnp.bfloat16)
    normalized_gradient = lax.dot_general(
        dproj_t, proj_weight, (((0,), (1,)), ((), ())), preferred_element_type=jnp.float32
    )
    weight_term = lax.dot_general(
        normalized_input, dproj_t, (((0,), (1,)), ((), ())), preferred_element_type=jnp.float32
    )
    gain_product = jnp.sum(normalized_gradient * standardized_input, axis=0)
    bias_term = jnp.sum(normalized_gradient, axis=0)
    weight_sum, gain_sum, bias_sum = lax.psum(
        (weight_term, gain_product, bias_term), ("row", "col")
    )
    scaled_input = normalized_gradient * layernorm_gain
    pairwise_gradient = (
        scaled_input
        - jnp.mean(scaled_input, axis=1, keepdims=True)
        - standardized_input * jnp.mean(scaled_input * standardized_input, axis=1, keepdims=True)
    ) * inverse_deviation
    pairwise_gradient = pairwise_gradient.astype(jnp.bfloat16).reshape(rows, cols, width)
    return (pairwise_gradient, weight_sum / total, jnp.stack([gain_sum, bias_sum]) / total)


def solution(mesh):
    in_specs = (P("row", "col", None), P(), P(), P(), P("row", "col", None))
    out_specs = (P("row", "col", None), P(), P())
    return jax.shard_map(
        per_device, mesh=mesh, in_specs=in_specs, out_specs=out_specs, check_vma=False
    )
```

profile of v0, /device:TPU:1, one launch (start us, length us, event | category | flops | bytes accessed | tf_op | source)
XLA Modules:
  0.0 752.2 jit_solution(17001834974957036539)
XLA Ops:
  7.3 1.9 convert_reduce_fusion
  9.2 2.3 multiply_reduce_fusion.2
  11.7 1.3 add_convert_fusion
  15.3 3.2 copy-done.1
  19.1 1.5 copy.29
  20.6 37.3 %all_to_all.72 = bf16[128,128,32]{1,2,0:T(8,128)(2,1)S(1)} all-to-all(bf16[128,128,32]{1,2,0:T(8,128)(2,1)S(1)} %copy.29), channel_id=1, replica_groups=mesh['row'=8,'col'=32] {'col'}, dimensions={0} | all-to-all | bytes 2097152 | tf_op jit(solution)/shard_map/all_to_all | solution.py:36
  59.5 1.5 copy.31
  61.0 32.4 %all_to_all.73 = bf16[128,128,32]{1,2,0:T(8,128)(2,1)S(1)} all-to-all(bf16[128,128,32]{1,2,0:T(8,128)(2,1)S(1)} %bitcast.64), channel_id=1, replica_groups=mesh['row'=8,'col'=32] {'col'}, dimensions={0} | all-to-all | bytes 2097152 | tf_op jit(solution)/shard_map/all_to_all | solution.py:37
  94.6 89.7 %all-gather.4.cloned.1.call-done = bf16[4,1024,1024]{1,2,0:T(8,128)(2,1)} async-done(((bf16[4,128,1024]{1,2,0:T(8,128)(2,1)}), bf16[4,1024,1024]{1,2,0:T(8,128)(2,1)}) %all-gather.4.cloned.1.call-update) | async-done | bytes 8388624 | tf_op jit(solution)/shard_map/all_gather | solution.py:40
  184.3 5.9 fusion.7
  191.0 34.5 %all_to_all.74 = bf16[4,128,1024]{1,0,2:T(4,128)(2,1)S(1)} all-to-all(bf16[4,128,1024]{1,0,2:T(4,128)(2,1)S(1)} %copy.34), channel_id=1, replica_groups=mesh['row'=8,'col'=32] {'col'}, dimensions={2} | all-to-all | bytes 2097152 | tf_op jit(solution)/shard_map/all_to_all | solution.py:47
  225.5 4.1 copy.35
  229.6 6.3 reshape.76
  235.9 1.9 copy.36
  237.7 5.2 multiply_convert_fusion.5
  242.9 1.5 copy.38
  244.5 32.4 %all_to_all.75 = bf16[128,128,32]{1,2,0:T(8,128)(2,1)S(1)} all-to-all(bf16[128,128,32]{1,2,0:T(8,128)(2,1)S(1)} %copy.38), channel_id=1, replica_groups=mesh['row'=8,'col'=32] {'col'}, dimensions={0} | all-to-all | bytes 2097152 | tf_op jit(solution)/shard_map/all_to_all | solution.py:35
  276.9 1.3 copy.40
  278.3 45.1 %all-gather.6.cloned.1.call-done = bf16[4,1024,1024]{1,2,0:T(8,128)(2,1)} async-done(((bf16[4,128,1024]{1,2,0:T(8,128)(2,1)}), bf16[4,1024,1024]{1,2,0:T(8,128)(2,1)}) %all-gather.6.cloned.1.call-update) | async-done | bytes 8388624 | tf_op jit(solution)/shard_map/all_gather | solution.py:41
  323.4 112.9 %all-gather.8.cloned.1.call-done = bf16[4,1024,1024]{2,1,0:T(8,128)(2,1)} async-done(((bf16[4,128,1024]{2,1,0:T(8,128)(2,1)}), bf16[4,1024,1024]{2,1,0:T(8,128)(2,1)}) %all-gather.8.cloned.1.call-update) | async-done | bytes 8388624 | tf_op jit(solution)/shard_map/all_gather | solution.py:42
  436.4 5.0 convolution_convert_fusion
  442.1 34.4 %all_to_all.76 = bf16[4,128,1024]{1,0,2:T(4,128)(2,1)S(1)} all-to-all(bf16[4,128,1024]{1,0,2:T(4,128)(2,1)S(1)} %copy.41), channel_id=1, replica_groups=mesh['row'=8,'col'=32] {'col'}, dimensions={2} | all-to-all | bytes 2097152 | tf_op jit(solution)/shard_map/all_to_all | solution.py:48
  476.9 4.6 copy.43
  481.6 6.2 reshape.77
  487.8 1.9 copy.44
  489.6 3.9 multiply_convert_fusion.2
  493.6 2.3 multiply_reduce_fusion
  495.9 1.5 fusion.9
  497.4 3.3 multiply_convert_fusion
  500.6 75.7 %all-reduce = (f32[1,128]{1,0:T(1,128)S(1)}, f32[1,128]{1,0:T(1,128)S(1)}) all-reduce(f32[1,128]{1,0:T(1,128)S(1)} %bitcast.67, f32[1,128]{1,0:T(1,128)S(1)} %bitcast.66), channel_id=1, replica_groups=mesh['row'=8,'col'=32] {'row','col'}, use_global_device_ids=true, to_apply=%region_8.0 | all-reduce | flops 256 | bytes 2048 | tf_op jit(solution)/shard_map/psum | solution.py:69
  576.9 167.1 %all-reduce.3.cloned.1.call-done = f32[128,512]{1,0:T(8,128)} async-done(((f32[128,512]{1,0:T(8,128)}), f32[128,512]{1,0:T(8,128)}) %all-reduce.3.cloned.1.call-update) | async-done | bytes 262160 | tf_op jit(solution)/shard_map/psum | solution.py:69
  744.0 1.7 broadcast_multiply_fusion
  (42 shorter events, 8.5 us)
Async XLA Ops:
  7.2 6.9 copy-start
  7.2 4.5 copy-start.2
  7.2 4.5 copy-start.8
  7.2 4.5 copy-start.9
  7.2 177.1 %all-gather.4.cloned.1.call-start = ((), (), s32[]{:S(2)}) async-start(), calls=%async_computation.5 | async-start | bytes 9437184 | tf_op jit(solution)/shard_map/all_gather | solution.py:40
  13.0 1.0 copy-start.3
  15.3 3.2 copy-start.1
  57.9 1.6 copy-start.7
  59.0 264.4 %all-gather.6.cloned.1.call-start = ((), (), s32[]{:S(2)}) async-start(), calls=%async_computation.6 | async-start | bytes 9437184 | tf_op jit(solution)/shard_map/all_gather | solution.py:41
  94.5 341.9 %all-gather.8.cloned.1.call-start = ((), (), s32[]{:S(2)}) async-start(), calls=%async_computation.7 | async-start | bytes 9437184 | tf_op jit(solution)/shard_map/all_gather | solution.py:42
  278.3 465.7 %all-reduce.3.cloned.1.call-start = ((), (), s32[]{:S(2)}) async-start(), calls=%async_computation.8 | async-start | bytes 524288 | tf_op jit(solution)/shard_map/psum | solution.py:69
  489.6 3.9 copy-start.5
  489.6 3.9 copy-start.6
  493.6 2.3 copy-start.4
Sparse Core Ops, SparseCore 0:
  59.1 125.1 all-gather.3
  186.8 136.6 all-gather.5
  326.1 110.2 all-gather.7
  497.5 246.4 all-reduce.2
where the time goes:
time: 753 us; the launch traced here: 752 us
  waiting for transfers between devices  415 us (55%)
  blocking collectives  247 us (33%)
  local copies, waits for them, and re-layouts  39.6 us (5%)
  other arithmetic  21 us (3%)
  matrix products  15.9 us (2%)
  between operations  14 us (2%)
    psum x1, waiting for transfers between devices, per_device(): lax.psum((weight_term, gain_product, bias_term), ('row', 'col'))  167 us
    all_gather x1, waiting for transfers between devices, per_device(): left_piece = lax.all_gather(left_ch, 'row', axis=1, tiled=True)  113 us
    all_gather x1, waiting for transfers between devices, per_device(): right_piece = lax.all_gather(right_ch, 'row', axis=1, tiled=True)  89.7 us
    psum x1, blocking collectives, per_device(): lax.psum((weight_term, gain_product, bias_term), ('row', 'col'))  75.7 us
    all_gather x1, waiting for transfers between devices, per_device(): grad_piece = lax.all_gather(grad_ch, 'row', axis=1, tiled=True)  45.1 us
    all_to_all x1, blocking collectives, per_device(): lax.all_to_all(right, 'col', split_axis=0, concat_axis=2, tiled=True)  37.3 us
    all_to_all x1, blocking collectives, per_device(): lax.all_to_all(first.astype(jnp.bfloat16), 'col', split_axis=2, concat_ax...  34.5 us
    all_to_all x1, blocking collectives, per_device(): lax.all_to_all(second.astype(jnp.bfloat16), 'col', split_axis=2, concat_a...  34.4 us
  transfers between devices with their start and end apart: 4, of which 4 were waited for; matrix products, arithmetic and copies ran while one was open for 4% of the time, Pallas kernels for 0%

commit v1 on v0

v1 whole, which is shorter than its diff:
```python
import functools

import jax
import jax.numpy as jnp
from jax import lax
from jax.experimental import pallas as pl
from jax.experimental.pallas import tpu as pltpu
from jax.sharding import Mesh, PartitionSpec as P

PLANE = ("y", "xh", "xl", "c")
GROUPS = 32
SLABS = 8
STEP_ROWS = 16
VMEM_LIMIT = 48 * 1024 * 1024


def all_to_all(x, axes):
    return lax.all_to_all(x, axes, split_axis=0, concat_axis=0, tiled=True)


def shift(x, by):
    return lax.ppermute(x, "z", [(i, (i + by) % SLABS) for i in range(SLABS)])


def normalize(pair_ref, gain_ref, bias_ref):
    x = pair_ref[...].astype(jnp.float32)
    x = x.reshape(x.shape[0] * x.shape[1], x.shape[2])
    centred = x - jnp.mean(x, axis=1, keepdims=True)
    inverse = lax.rsqrt(jnp.mean(centred * centred, axis=1, keepdims=True) + 1e-05)
    xhat = centred * inverse
    normed = (xhat * gain_ref[...] + bias_ref[...]).astype(jnp.bfloat16)
    return xhat, inverse, normed


def project(normed, weight_ref):
    proj = jnp.dot(normed, weight_ref[...], preferred_element_type=jnp.float32)
    h = proj.shape[1] // 4
    return proj[:, :h], proj[:, h : 2 * h], proj[:, 2 * h : 3 * h], proj[:, 3 * h :]


def pre_kernel(pair_ref, gain_ref, bias_ref, weight_ref, left_ref, right_ref):
    _, _, normed = normalize(pair_ref, gain_ref, bias_ref)
    pa, ga, pb, gb = project(normed, weight_ref)
    left_ref[...] = (jax.nn.sigmoid(ga) * pa).astype(jnp.bfloat16).reshape(left_ref.shape)
    right_ref[...] = (jax.nn.sigmoid(gb) * pb).astype(jnp.bfloat16).reshape(right_ref.shape)


def pre(pair, gain, bias, weight):
    rows, cols, width = pair.shape
    tile = pl.BlockSpec((STEP_ROWS, cols, width), lambda i: (i, 0, 0))
    whole = lambda *shape: pl.BlockSpec(shape, lambda i: (0,) * len(shape))
    return pl.pallas_call(
        pre_kernel,
        grid=(rows // STEP_ROWS,),
        in_specs=[tile, whole(1, width), whole(1, width), whole(*weight.shape)],
        out_specs=[tile, tile],
        out_shape=[jax.ShapeDtypeStruct(pair.shape, jnp.bfloat16)] * 2,
        compiler_params=pltpu.CompilerParams(vmem_limit_bytes=VMEM_LIMIT),
        cost_estimate=pl.CostEstimate(
            flops=2 * rows * cols * width * 512, bytes_accessed=3 << 20, transcendentals=1 << 20
        ),
        name="gated_projections",
    )(pair, gain, bias, weight)


def post_kernel(
    pair_ref, left_ref, right_ref, gain_ref, bias_ref, weight_ref, weight_t_ref, grad_ref, total_ref
):
    step = pl.program_id(0)

    @pl.when(step == 0)
    def _():
        total_ref[...] = jnp.zeros_like(total_ref)

    xhat, inverse, normed = normalize(pair_ref, gain_ref, bias_ref)
    pa, ga, pb, gb = project(normed, weight_ref)
    width = xhat.shape[1]
    left = left_ref[...].astype(jnp.float32).reshape(xhat.shape)
    right = right_ref[...].astype(jnp.float32).reshape(xhat.shape)
    sa = jax.nn.sigmoid(ga)
    sb = jax.nn.sigmoid(gb)
    la = left * sa
    rb = right * sb
    dproj = jnp.concatenate(
        [
            la.astype(jnp.bfloat16),
            (la * pa * (1.0 - sa)).astype(jnp.bfloat16),
            rb.astype(jnp.bfloat16),
            (rb * pb * (1.0 - sb)).astype(jnp.bfloat16),
        ],
        axis=1,
    )
    dnormed = jnp.dot(dproj, weight_t_ref[...], preferred_element_type=jnp.float32)
    wgrad = lax.dot_general(
        normed, dproj, (((0,), (0,)), ((), ())), preferred_element_type=jnp.float32
    )
    for block in range(4):
        total_ref[block * width : (block + 1) * width, :] += wgrad[
            :, block * width : (block + 1) * width
        ]
    total_ref[4 * width : 4 * width + 1, :] += jnp.sum(dnormed * xhat, axis=0, keepdims=True)
    total_ref[4 * width + 8 : 4 * width + 9, :] += jnp.sum(dnormed, axis=0, keepdims=True)
    g = dnormed * gain_ref[...]
    grad = (
        g
        - jnp.mean(g, axis=1, keepdims=True)
        - xhat * jnp.mean(g * xhat, axis=1, keepdims=True)
    ) * inverse
    grad_ref[...] = grad.astype(jnp.bfloat16).reshape(grad_ref.shape)


def post(pair, left, right, gain, bias, weight, total_rows):
    rows, cols, width = pair.shape
    tile = pl.BlockSpec((STEP_ROWS, cols, width), lambda i: (i, 0, 0))
    whole = lambda *shape: pl.BlockSpec(shape, lambda i: (0,) * len(shape))
    return pl.pallas_call(
        post_kernel,
        grid=(rows // STEP_ROWS,),
        in_specs=[
            tile,
            tile,
            tile,
            whole(1, width),
            whole(1, width),
            whole(*weight.shape),
            whole(*weight.shape[::-1]),
        ],
        out_specs=[tile, whole(total_rows, width)],
        out_shape=[
            jax.ShapeDtypeStruct(pair.shape, jnp.bfloat16),
            jax.ShapeDtypeStruct((total_rows, width), jnp.float32),
        ],
        compiler_params=pltpu.CompilerParams(vmem_limit_bytes=VMEM_LIMIT),
        cost_estimate=pl.CostEstimate(
            flops=6 * rows * cols * width * 512, bytes_accessed=5 << 20, transcendentals=1 << 20
        ),
        name="input_gradients",
    )(pair, left, right, gain, bias, weight, weight.T)


def assemble(refs):
    pieces = [piece for ref in refs for piece in ref[:, 0]]
    across = [
        jnp.concatenate(pieces[4 * r : 4 * r + 4], axis=0) for r in range(len(pieces) // 4)
    ]
    return jnp.concatenate(across, axis=1)


def halves(a, b):
    return (
        jnp.concatenate([a[:, :64], b[:, :64]], axis=1),
        jnp.concatenate([a[:, 64:], b[:, 64:]], axis=1),
    )


def product_kernel(offsets, n_refs, finish, with_sums, slab_ref, left_ref, right_ref, *refs):
    block_refs = refs[:n_refs]
    rest = refs[n_refs:]
    if with_sums:
        sum_in, second_in, *rest = rest
    if finish:
        out_ref, by_slab, second = rest
    else:
        sum_out, second_out, by_slab, second = rest
    slab = slab_ref[0]
    left = assemble([left_ref])
    right = assemble([right_ref])
    for m in range(4):
        even, odd = halves(
            right[:, 128 * m : 128 * m + 128], right[:, 512 + 128 * m : 640 + 128 * m]
        )
        by_slab[2 * m] = even
        by_slab[2 * m + 1] = odd
    total = None
    if with_sums:
        total = sum_in[0]
        second[...] = second_in[0]
    at = 0
    for offset, parts in offsets:
        block = assemble(block_refs[at : at + parts])
        at += parts
        where = lax.rem(slab + offset, SLABS)
        term = jnp.dot(by_slab[where], block, preferred_element_type=jnp.float32)
        total = term if total is None else total + term
        second[where] = lax.dot_general(
            left, block, (((1,), (1,)), ((), ())), preferred_element_type=jnp.float32
        ).astype(jnp.bfloat16)
    if not finish:
        sum_out[0] = total
        second_out[0] = second[...]
        return
    first = total.astype(jnp.bfloat16)
    for r in range(8):
        for c in range(4):
            out_ref[4 * r + c, 0, 0] = first[32 * c : 32 * c + 32, 128 * r : 128 * r + 128]
    for m in range(4):
        low, high = halves(second[2 * m], second[2 * m + 1])
        for c in range(4):
            out_ref[4 * m + c, 1, 0] = low[32 * c : 32 * c + 32]
            out_ref[4 * (m + 4) + c, 1, 0] = high[32 * c : 32 * c + 32]


def products(slab, left, right, blocks, sums, finish):
    groups, channels, depth, width = left.shape
    arrays = [a for _, parts in blocks for a in parts]
    piece = lambda a: pl.BlockSpec((a.shape[0], 1, depth, width), lambda h: (0, h, 0, 0))
    sum_specs = [
        pl.BlockSpec((1, 128, 1024), lambda h: (h, 0, 0)),
        pl.BlockSpec((1, SLABS, 128, 128), lambda h: (h, 0, 0, 0)),
    ]
    sum_shapes = [
        jax.ShapeDtypeStruct((channels, 128, 1024), jnp.float32),
        jax.ShapeDtypeStruct((channels, SLABS, 128, 128), jnp.bfloat16),
    ]
    operands = [slab, left, right, *arrays] + (list(sums) if sums else [])
    aliases = {}
    if finish:
        out_specs = pl.BlockSpec((groups, 2, 1, depth, width), lambda h: (0, 0, h, 0, 0))
        out_shape = jax.ShapeDtypeStruct((groups, 2, channels, depth, width), jnp.bfloat16)
    else:
        out_specs, out_shape = sum_specs, sum_shapes
        if sums:
            aliases = {len(operands) - 2: 0, len(operands) - 1: 1}
    kernel = functools.partial(
        product_kernel,
        [(offset, len(parts)) for offset, parts in blocks],
        len(arrays),
        finish,
        bool(sums),
    )
    return pl.pallas_call(
        kernel,
        grid=(channels,),
        in_specs=[pl.BlockSpec(memory_space=pltpu.SMEM), piece(left), piece(right)]
        + [piece(a) for a in arrays]
        + (sum_specs if sums else []),
        out_specs=out_specs,
        out_shape=out_shape,
        scratch_shapes=[
            pltpu.VMEM((SLABS, 128, 128), jnp.bfloat16),
            pltpu.VMEM((SLABS, 128, 128), jnp.bfloat16),
        ],
        input_output_aliases=aliases,
        compiler_params=pltpu.CompilerParams(vmem_limit_bytes=VMEM_LIMIT),
        cost_estimate=pl.CostEstimate(
            flops=4 * channels * 128 * 128 * 1024 * len(blocks),
            bytes_accessed=(2 + len(blocks)) << 20,
            transcendentals=0,
        ),
        name="triangle_products",
    )(*operands)


def per_device(pair, layernorm_gain, layernorm_bias, proj_weight, product_grad):
    rows, cols, width = pair.shape
    split = lambda x: jnp.transpose(x, (2, 1, 0)).reshape(GROUPS, width // GROUPS, cols, rows)
    gain = layernorm_gain.reshape(1, width)
    bias = layernorm_bias.reshape(1, width)
    slab = lax.axis_index("z").astype(jnp.int32).reshape(1)

    own = all_to_all(split(product_grad), PLANE)
    up1, down1 = shift(own, 1), shift(own, -1)
    pair, own = lax.optimization_barrier((pair, own))
    left, right = pre(pair, gain, bias, proj_weight)
    left = all_to_all(split(left), PLANE)
    right, left, up1, down1 = lax.optimization_barrier((split(right), left, up1, down1))
    up2, down2 = shift(up1, 1), shift(down1, -1)
    right = all_to_all(right, PLANE)
    up2, down2, right = lax.optimization_barrier((up2, down2, right))
    up3, down3 = shift(up2, 1), shift(down2, -1)
    sums = products(
        slab, left, right,
        [(0, [own]), (7, [up1]), (1, [down1]), (6, [up2]), (2, [down2])], None, False,
    )
    up4, down4 = shift(up3[:16], 1), shift(down3[16:], -1)
    sums = products(slab, left, right, [(5, [up3]), (3, [down3])], sums, False)
    back = products(slab, left, right, [(4, [up4, down4])], sums, True)
    back = all_to_all(back, PLANE)

    join = lambda x: jnp.transpose(x.reshape(width, cols, rows), (2, 1, 0))
    total_rows = 24 * GROUPS
    pairwise_gradient, total = post(
        pair, join(back[:, 0]), join(back[:, 1]), gain, bias, proj_weight, total_rows
    )
    total = jnp.sum(all_to_all(total.reshape(GROUPS, 24, width), PLANE), axis=0)
    total = lax.psum(total, "z") / (rows * 8)
    total = all_to_all(jnp.broadcast_to(total[None], (GROUPS, 24, width)), PLANE)
    total = total.reshape(total_rows, width)
    proj_grad = jnp.transpose(total[: 4 * width].reshape(4, width, width), (1, 0, 2))
    proj_grad = proj_grad.reshape(width, 4 * width)
    layernorm_gradient = jnp.stack([total[4 * width], total[4 * width + 8]])
    return pairwise_gradient, proj_grad, layernorm_gradient


def solution(mesh):
    fine = Mesh(mesh.devices.reshape(4, 2, 2, 8, 2), ("y", "xh", "xl", "z", "c"))
    tiles = P(("y", "xh"), ("xl", "z", "c"), None)
    return jax.shard_map(
        per_device,
        mesh=fine,
        in_specs=(tiles, P(), P(), P(), tiles),
        out_specs=(tiles, P(), P()),
        check_vma=False,
    )
```

time: 753 us -> 248 us (0.33)
  waiting for transfers between devices: 415 us -> 66 us
  blocking collectives: 247 us -> 106 us
  Pallas kernels: 0 us -> 29.6 us
  starting transfers between devices: 0.16 us -> 23.9 us
  other arithmetic: 21 us -> 0.61 us
  local copies, waits for them, and re-layouts: 39.6 us -> 20.4 us
  matrix products: 15.9 us -> 0 us
  between operations: 14 us -> 0.78 us
    all_gather x3 -> x0, waiting for transfers between devices: 248 us -> none  [the longest x1 113 us: per_device(): left_piece = lax.all_gather(left_ch, 'row', axis=1, tiled=True)]
    psum x1 -> x0, waiting for transfers between devices: 167 us -> none  [per_device(): lax.psum((weight_term, gain_product, bias_term), ('row', 'col'))]
    all_to_all x5 -> x4, blocking collectives: 171 us -> 83.8 us  [all_to_all(): return lax.all_to_all(x, axes, split_axis=0, concat_axis=0, tiled=True)]
    psum x1, blocking collectives: 75.7 us -> 22.3 us  [per_device(): total = lax.psum(total, 'z') / (rows * 8)]
    all_to_all x0 -> x2, waiting for transfers between devices: none -> 42.7 us  [all_to_all(): return lax.all_to_all(x, axes, split_axis=0, concat_axis=0, tiled=True)]
    pallas_call x0 -> x5, Pallas kernels: none -> 29.6 us  [the longest x3 16.9 us: products(): pl.pallas_call(kernel, grid=(channels,), in_specs=[pl.BlockSpec(memory_sp...]
    convert_element_type x8 -> x0, local copies, waits for them, and re-layouts: 26.5 us -> none  [the longest x3 12.7 us: per_device(): right_back = right_back.reshape(hidden, count).astype(jnp.float32)]
    ppermute x0 -> x8, waiting for transfers between devices: none -> 23.2 us  [shift(): return lax.ppermute(x, 'z', [(i, (i + by) % SLABS) for i in range(SLABS)])]
  transfers between devices with their start and end apart: 4 -> 10, of which waited for: 4 -> 4; matrix products, arithmetic and copies ran while one was open for 4% -> 3% of each run, Pallas kernels for 0% -> 7%
where the time goes in v1:
time: 248 us; the launch traced here: 247 us
  blocking collectives  106 us (43%)
  waiting for transfers between devices  66 us (27%)
  Pallas kernels  29.6 us (12%)
  starting transfers between devices  23.9 us (10%)
  local copies, waits for them, and re-layouts  20.4 us (8%)
    all_to_all x4, blocking collectives, all_to_all(): return lax.all_to_all(x, axes, split_axis=0, concat_axis=0, tiled=True)  83.8 us
    all_to_all x2, waiting for transfers between devices, all_to_all(): return lax.all_to_all(x, axes, split_axis=0, concat_axis=0, tiled=True)  42.7 us
    ppermute x8, waiting for transfers between devices, shift(): return lax.ppermute(x, 'z', [(i, (i + by) % SLABS) for i in range(SLABS)])  23.2 us
    psum x1, blocking collectives, per_device(): total = lax.psum(total, 'z') / (rows * 8)  22.3 us
    pallas_call x3, Pallas kernels, products(): pl.pallas_call(kernel, grid=(channels,), in_specs=[pl.BlockSpec(memory_sp...  16.9 us
    ppermute x8, starting transfers between devices, shift(): return lax.ppermute(x, 'z', [(i, (i + by) % SLABS) for i in range(SLABS)])  12.8 us
    all_to_all x2, starting transfers between devices, all_to_all(): return lax.all_to_all(x, axes, split_axis=0, concat_axis=0, tiled=True)  11.1 us
    pallas_call x1, Pallas kernels, post(): pl.pallas_call(post_kernel, grid=(rows // STEP_ROWS,), in_specs=[tile, ti...  7.93 us
  transfers between devices with their start and end apart: 10, of which 4 were waited for; matrix products, arithmetic and copies ran while one was open for 3% of the time, Pallas kernels for 7%

profile of v1, /device:TPU:1, one launch (start us, length us, event | category | flops | bytes accessed | tf_op | source)
XLA Modules:
  0.0 247.4 jit_solution(1338935691456065343)
XLA Ops:
  0.7 2.5 %copy.17 = bf16[128,32,128]{2,1,0:T(8,128)(2,1)S(1)} copy(bf16[128,32,128]{0,1,2:T(8,128)(2,1)} %bitcast.40) | data formatting | bytes 2097152 | tf_op jit(solution)/shard_map/transpose | solution.py:256
  3.2 25.7 %all_to_all.30.refs_0_ = bf16[32,4,32,128]{3,2,1,0:T(8,128)(2,1)S(1)} all-to-all(bf16[32,4,32,128]{3,2,1,0:T(8,128)(2,1)S(1)} %bitcast.35), channel_id=1, replica_groups=mesh['y'=4,'xh'=2,'xl'=2,'z'=8,'c'=2] {'y','xh','xl','c'}, dimensions={0} | all-to-all | bytes 2097152 | tf_op jit(solution)/shard_map/all_to_all | solution.py:18
  28.9 1.6 collective-permute-start
  30.5 3.9 %collective-permute-start.1 = (bf16[32,4,32,128]{3,2,1,0:T(8,128)(2,1)S(1)}, bf16[32,4,32,128]{3,2,1,0:T(8,128)(2,1)}, u32[]{:S(2)}, u32[]{:S(2)}) collective-permute-start(bf16[32,4,32,128]{3,2,1,0:T(8,128)(2,1)S(1)} %all_to_all.30.refs_0_), channel_id=1, source_target_pairs={{0,14},{2,0},{4,2},{6,4},{8,6},{10,8},{12,10},{14,12},{1,15},{3,1}... | collective-permute-start | bytes 3145736 | tf_op jit(solution)/shard_map/ppermute | solution.py:22
  34.5 4.8 %gated_projections.1 = (bf16[128,32,128]{2,1,0:T(8,128)(2,1)S(1)}, bf16[128,32,128]{2,1,0:T(8,128)(2,1)S(1)}) custom-call(bf16[128,32,128]{2,1,0:T(8,128)(2,1)S(1)} %copy-done.5, f32[1,128]{1,0:T(1,128)S(1)} %bitcast.29, f32[1,128]{1,0:T(1,128)S(1)} %bitcast.31, bf16[128,512]{1,0:T(8,128)(2,1)S(1)} %copy-done.4), custom_call_target="tpu_custom_call" | custom-call | flops 536870912 | bytes 3145728 | tf_op jit(solution)/shard_map/gated_projections/pallas_call | solution.py:52
  39.3 2.3 copy.19
  41.6 4.3 %all-to-all-start.1 = ((bf16[32,4,32,128]{3,2,1,0:T(8,128)(2,1)}), bf16[32,4,32,128]{3,2,1,0:T(8,128)(2,1)S(1)}, u32[]{:S(2)}, u32[]{:S(2)}) async-start(bf16[32,4,32,128]{3,2,1,0:T(8,128)(2,1)} %bitcast.34), calls=%async_computation.1 | async-start | bytes 2097152 | tf_op jit(solution)/shard_map/all_to_all | solution.py:18
  45.9 2.3 copy.18
  48.2 15.0 %all-to-all-done.1.left_ref = bf16[32,4,32,128]{3,2,1,0:T(8,128)(2,1)S(1)} async-done(((bf16[32,4,32,128]{3,2,1,0:T(8,128)(2,1)}), bf16[32,4,32,128]{3,2,1,0:T(8,128)(2,1)S(1)}, u32[]{:S(2)}, u32[]{:S(2)}) %all-to-all-start.1) | async-done | bytes 1048608 | tf_op jit(solution)/shard_map/all_to_all | solution.py:18
  63.2 2.7 %collective-permute-start.3 = (bf16[32,4,32,128]{3,2,1,0:T(8,128)(2,1)}, bf16[32,4,32,128]{3,2,1,0:T(8,128)(2,1)S(1)}, u32[]{:S(2)}, u32[]{:S(2)}) collective-permute-start(bf16[32,4,32,128]{3,2,1,0:T(8,128)(2,1)} %collective-permute-done.1.refs_2_), channel_id=1, source_target_pairs={{0,14},{2,0},{4,2},{6,4},{8,6},{10,8},{12,10},{14,12},{1,15},{3,1}... | collective-permute-start | bytes 3145736 | tf_op jit(solution)/shard_map/ppermute | solution.py:22
  65.8 21.8 %all_to_all.31.right_ref = bf16[32,4,32,128]{3,2,1,0:T(8,128)(2,1)S(1)} all-to-all(bf16[32,4,32,128]{3,2,1,0:T(8,128)(2,1)} %bitcast.33), channel_id=1, replica_groups=mesh['y'=4,'xh'=2,'xl'=2,'z'=8,'c'=2] {'y','xh','xl','c'}, dimensions={0} | all-to-all | bytes 2097152 | tf_op jit(solution)/shard_map/all_to_all | solution.py:18
  87.7 1.3 collective-permute-done.2.refs_3_
  89.0 0.9 copy-done.9
  89.9 1.8 collective-permute-start.6
  91.7 22.0 %collective-permute-done.4.refs_0_ = bf16[32,4,32,128]{3,2,1,0:T(8,128)(2,1)S(1)} collective-permute-done((bf16[32,4,32,128]{3,2,1,0:T(8,128)(2,1)S(1)}, bf16[32,4,32,128]{3,2,1,0:T(8,128)(2,1)S(1)}, u32[]{:S(2)}, u32[]{:S(2)}) %collective-permute-start.4) | collective-permute-done | bytes 1048608 | tf_op jit(solution)/shard_map/ppermute | solution.py:22
  113.6 0.9 slice.28
  114.5 1.0 copy-done
  116.3 1.0 copy-done.2
  117.3 2.7 %collective-permute-start.7 = (bf16[16,4,32,128]{3,2,1,0:T(8,128)(2,1)}, bf16[16,4,32,128]{3,2,1,0:T(8,128)(2,1)}, u32[]{:S(2)}, u32[]{:S(2)}) collective-permute-start(bf16[16,4,32,128]{3,2,1,0:T(8,128)(2,1)} %slice.29), channel_id=1, source_target_pairs={{0,14},{2,0},{4,2},{6,4},{8,6},{10,8},{12,10},{14,12},{1,15},{3,1}... | collective-permute-start | bytes 1572872 | tf_op jit(solution)/shard_map/ppermute | solution.py:22
  120.0 6.6 %triangle_products.3 = (f32[4,128,1024]{2,1,0:T(8,128)}, bf16[4,8,128,128]{3,2,1,0:T(8,128)(2,1)S(1)}) custom-call(s32[1]{0:T(128)} %bitcast.2.slab_ref, bf16[32,4,32,128]{3,2,1,0:T(8,128)(2,1)S(1)} %all-to-all-done.1.left_ref, bf16[32,4,32,128]{3,2,1,0:T(8,128)(2,1)S(1)} %all_to_all.31.right_ref, bf16[32,4,32,128]{3,2,1,0:T(8,128)(2,1)S(1)} %all_to_all.30.refs_0_, ...), custom_call_target="tpu_custom_call" | custom-call | flops 1342177280 | bytes 7340032 | tf_op jit(solution)/shard_map/triangle_products/pallas_call | solution.py:231
  126.6 5.0 %triangle_products.4 = (f32[4,128,1024]{2,1,0:T(8,128)}, bf16[4,8,128,128]{3,2,1,0:T(8,128)(2,1)S(1)}) custom-call(s32[1]{0:T(128)} %bitcast.2.slab_ref, bf16[32,4,32,128]{3,2,1,0:T(8,128)(2,1)S(1)} %all-to-all-done.1.left_ref, bf16[32,4,32,128]{3,2,1,0:T(8,128)(2,1)S(1)} %all_to_all.31.right_ref, ...), custom_call_target="tpu_custom_call", output_to_operand_aliasing={{0}: (5, {}), {1}: (6, {})} | custom-call | flops 536870912 | bytes 4194304 | tf_op jit(solution)/shard_map/triangle_products/pallas_call | solution.py:231
  131.7 5.2 %triangle_products.5 = bf16[32,2,4,32,128]{4,3,2,1,0:T(8,128)(2,1)} custom-call(s32[1]{0:T(128)} %bitcast.2.slab_ref, bf16[32,4,32,128]{3,2,1,0:T(8,128)(2,1)S(1)} %all-to-all-done.1.left_ref, bf16[32,4,32,128]{3,2,1,0:T(8,128)(2,1)S(1)} %all_to_all.31.right_ref, bf16[16,4,32,128]{3,2,1,0:T(8,128)(2,1)} %collective-permute-done.5.refs_0_, ...), custom_call_target="tpu_custom_call" | custom-call | flops 268435456 | bytes 3145728 | tf_op jit(solution)/shard_map/triangle_products/pallas_call | solution.py:231
  136.9 6.9 %all-to-all-start.3 = ((bf16[32,2,4,32,128]{4,3,2,1,0:T(8,128)(2,1)}), bf16[32,2,4,32,128]{4,3,2,1,0:T(8,128)(2,1)S(1)}, u32[]{:S(2)}, u32[]{:S(2)}) async-start(bf16[32,2,4,32,128]{4,3,2,1,0:T(8,128)(2,1)} %triangle_products.5), calls=%async_computation.3 | async-start | bytes 4194304 | tf_op jit(solution)/shard_map/all_to_all | solution.py:18
  143.9 27.7 %all-to-all-done.3 = bf16[32,2,4,32,128]{4,3,2,1,0:T(8,128)(2,1)S(1)} async-done(((bf16[32,2,4,32,128]{4,3,2,1,0:T(8,128)(2,1)}), bf16[32,2,4,32,128]{4,3,2,1,0:T(8,128)(2,1)S(1)}, u32[]{:S(2)}, u32[]{:S(2)}) %all-to-all-start.3) | async-done | bytes 2097184 | tf_op jit(solution)/shard_map/all_to_all | solution.py:18
  171.6 1.7 fusion
  173.3 2.5 copy.20
  175.8 2.5 %copy.21 = bf16[128,32,128]{0,1,2:T(8,128)(2,1)S(1)} copy(bf16[128,32,128]{2,1,0:T(8,128)(2,1)} %bitcast.36) | data formatting | bytes 2097152 | tf_op jit(solution)/shard_map/reshape;squeeze | solution.py:280
  178.3 1.2 copy-done.6
  179.5 7.9 %input_gradients.1 = (bf16[128,32,128]{2,1,0:T(8,128)(2,1)}, f32[768,128]{1,0:T(8,128)S(1)}) custom-call(bf16[128,32,128]{2,1,0:T(8,128)(2,1)S(1)} %copy-done.6, bf16[128,32,128]{2,1,0:T(8,128)(2,1)S(1)} %bitcast.24, bf16[128,32,128]{2,1,0:T(8,128)(2,1)S(1)} %bitcast.25, f32[1,128]{1,0:T(1,128)S(1)} %bitcast.30, f32[1,128]{1,0:T(1,128)S(1)} %bitcast.32, ...), custom_call_target="tpu_custom_call" | custom-call | flops 1610612736 | bytes 5242880 | tf_op jit(solution)/shard_map/input_gradients/pallas_call | solution.py:116
  187.4 15.3 %all_to_all.32 = f32[32,24,128]{2,1,0:T(8,128)S(1)} all-to-all(f32[32,24,128]{2,1,0:T(8,128)S(1)} %bitcast.27), channel_id=1, replica_groups=mesh['y'=4,'xh'=2,'xl'=2,'z'=8,'c'=2] {'y','xh','xl','c'}, dimensions={0} | all-to-all | bytes 786432 | tf_op jit(solution)/shard_map/all_to_all | solution.py:18
  202.8 22.3 %psum.7 = f32[24,128]{1,0:T(8,128)S(1)} all-reduce(f32[24,128]{1,0:T(8,128)S(1)} %reduce_sum.9), channel_id=1, replica_groups=mesh['y'=4,'xh'=2,'xl'=2,'z'=8,'c'=2] {'z'}, use_global_device_ids=true, to_apply=%region_1.0 | all-reduce | flops 3072 | bytes 24576 | tf_op jit(solution)/shard_map/psum | solution.py:286
  225.1 21.0 %all_to_all.33 = f32[32,24,128]{2,1,0:T(8,128)S(1)} all-to-all(f32[32,24,128]{2,1,0:T(8,128)S(1)} %broadcast_in_dim.2), channel_id=1, replica_groups=mesh['y'=4,'xh'=2,'xl'=2,'z'=8,'c'=2] {'y','xh','xl','c'}, dimensions={0} | all-to-all | bytes 786432 | tf_op jit(solution)/shard_map/all_to_all | solution.py:18
  (36 shorter events, 2.5 us)
Async XLA Ops:
  0.6 33.9 %copy-start.4 = (bf16[128,512]{1,0:T(8,128)(2,1)S(1)}, bf16[128,512]{1,0:T(8,128)(2,1)}, u32[]{:S(2)}) copy-start(bf16[128,512]{1,0:T(8,128)(2,1)} %weight_ref.3) | copy-start | bytes 393220
  0.6 33.9 %copy-start.7 = (f32[128]{0:T(128)S(1)}, f32[128]{0:T(128)}, u32[]{:S(2)}) copy-start(f32[128]{0:T(128)} %param.6) | copy-start | bytes 1540
  0.7 33.8 %copy-start.8 = (f32[128]{0:T(128)S(1)}, f32[128]{0:T(128)}, u32[]{:S(2)}) copy-start(f32[128]{0:T(128)} %param.7) | copy-start | bytes 1540
  3.2 31.3 %copy-start.5 = (bf16[128,32,128]{2,1,0:T(8,128)(2,1)S(1)}, bf16[128,32,128]{2,1,0:T(8,128)(2,1)}, u32[]{:S(2)}) copy-start(bf16[128,32,128]{2,1,0:T(8,128)(2,1)} %pair_ref.1) | copy-start | bytes 3145732
  28.9 34.3 %collective-permute-start = (bf16[32,4,32,128]{3,2,1,0:T(8,128)(2,1)S(1)}, bf16[32,4,32,128]{3,2,1,0:T(8,128)(2,1)}, u32[]{:S(2)}, u32[]{:S(2)}) collective-permute-start(bf16[32,4,32,128]{3,2,1,0:T(8,128)(2,1)S(1)} %all_to_all.30.refs_0_), channel_id=1, source_target_pairs={{0,2},{2,4},{4,6},{6,8},{8,10},{10,12},{12,14},{14,0},{1,3},{3,5},... | collective-permute-start | bytes 3145736 | tf_op jit(solution)/shard_map/ppermute | solution.py:22
  30.5 32.6 %collective-permute-start.1 = (bf16[32,4,32,128]{3,2,1,0:T(8,128)(2,1)S(1)}, bf16[32,4,32,128]{3,2,1,0:T(8,128)(2,1)}, u32[]{:S(2)}, u32[]{:S(2)}) collective-permute-start(bf16[32,4,32,128]{3,2,1,0:T(8,128)(2,1)S(1)} %all_to_all.30.refs_0_), channel_id=1, source_target_pairs={{0,14},{2,0},{4,2},{6,4},{8,6},{10,8},{12,10},{14,12},{1,15},{3,1}... | collective-permute-start | bytes 3145736 | tf_op jit(solution)/shard_map/ppermute | solution.py:22
  41.6 21.6 %all-to-all-start.1 = ((bf16[32,4,32,128]{3,2,1,0:T(8,128)(2,1)}), bf16[32,4,32,128]{3,2,1,0:T(8,128)(2,1)S(1)}, u32[]{:S(2)}, u32[]{:S(2)}) async-start(bf16[32,4,32,128]{3,2,1,0:T(8,128)(2,1)} %bitcast.34), calls=%async_computation.1 | async-start | bytes 2097152 | tf_op jit(solution)/shard_map/all_to_all | solution.py:18
  63.2 25.8 %collective-permute-start.2 = (bf16[32,4,32,128]{3,2,1,0:T(8,128)(2,1)}, bf16[32,4,32,128]{3,2,1,0:T(8,128)(2,1)S(1)}, u32[]{:S(2)}, u32[]{:S(2)}) collective-permute-start(bf16[32,4,32,128]{3,2,1,0:T(8,128)(2,1)} %collective-permute-done.refs_1_), channel_id=1, source_target_pairs={{0,2},{2,4},{4,6},{6,8},{8,10},{10,12},{12,14},{14,0},{1,3},{3,5},... | collective-permute-start | bytes 3145736 | tf_op jit(solution)/shard_map/ppermute | solution.py:22
  63.2 25.8 %collective-permute-start.3 = (bf16[32,4,32,128]{3,2,1,0:T(8,128)(2,1)}, bf16[32,4,32,128]{3,2,1,0:T(8,128)(2,1)S(1)}, u32[]{:S(2)}, u32[]{:S(2)}) collective-permute-start(bf16[32,4,32,128]{3,2,1,0:T(8,128)(2,1)} %collective-permute-done.1.refs_2_), channel_id=1, source_target_pairs={{0,14},{2,0},{4,2},{6,4},{8,6},{10,8},{12,10},{14,12},{1,15},{3,1}... | collective-permute-start | bytes 3145736 | tf_op jit(solution)/shard_map/ppermute | solution.py:22
  88.9 1.0 copy-start.9
  88.9 27.4 %copy-start.10 = (bf16[32,4,32,128]{3,2,1,0:T(8,128)(2,1)}, bf16[32,4,32,128]{3,2,1,0:T(8,128)(2,1)S(1)}, u32[]{:S(2)}) copy-start(bf16[32,4,32,128]{3,2,1,0:T(8,128)(2,1)S(1)} %collective-permute-done.3.refs_4_) | copy-start | bytes 3145732
  88.9 24.7 %collective-permute-start.4 = (bf16[32,4,32,128]{3,2,1,0:T(8,128)(2,1)S(1)}, bf16[32,4,32,128]{3,2,1,0:T(8,128)(2,1)S(1)}, u32[]{:S(2)}, u32[]{:S(2)}) collective-permute-start(bf16[32,4,32,128]{3,2,1,0:T(8,128)(2,1)S(1)} %collective-permute-done.2.refs_3_), channel_id=1, source_target_pairs={{0,2},{2,4},{4,6},{6,8},{8,10},{10,12},{12,14},{14,0},{1,3},{3,5},... | collective-permute-start | bytes 3145736 | tf_op jit(solution)/shard_map/ppermute | solution.py:22
  89.9 25.6 %collective-permute-start.6 = (bf16[32,4,32,128]{3,2,1,0:T(8,128)(2,1)S(1)}, bf16[32,4,32,128]{3,2,1,0:T(8,128)(2,1)S(1)}, u32[]{:S(2)}, u32[]{:S(2)}) collective-permute-start(bf16[32,4,32,128]{3,2,1,0:T(8,128)(2,1)S(1)} %collective-permute-done.3.refs_4_), channel_id=1, source_target_pairs={{0,14},{2,0},{4,2},{6,4},{8,6},{10,8},{12,10},{14,12},{1,15},{3,1}... | collective-permute-start | bytes 3145736 | tf_op jit(solution)/shard_map/ppermute | solution.py:22
  114.5 1.0 copy-start
  115.5 16.2 %collective-permute-start.5 = (bf16[16,4,32,128]{3,2,1,0:T(8,128)(2,1)}, bf16[16,4,32,128]{3,2,1,0:T(8,128)(2,1)}, u32[]{:S(2)}, u32[]{:S(2)}) collective-permute-start(bf16[16,4,32,128]{3,2,1,0:T(8,128)(2,1)} %slice.28), channel_id=1, source_target_pairs={{0,2},{2,4},{4,6},{6,8},{8,10},{10,12},{12,14},{14,0},{1,3},{3,5},... | collective-permute-start | bytes 1572872 | tf_op jit(solution)/shard_map/ppermute | solution.py:22
  116.3 1.0 copy-start.2
  117.3 14.3 %collective-permute-start.7 = (bf16[16,4,32,128]{3,2,1,0:T(8,128)(2,1)}, bf16[16,4,32,128]{3,2,1,0:T(8,128)(2,1)}, u32[]{:S(2)}, u32[]{:S(2)}) collective-permute-start(bf16[16,4,32,128]{3,2,1,0:T(8,128)(2,1)} %slice.29), channel_id=1, source_target_pairs={{0,14},{2,0},{4,2},{6,4},{8,6},{10,8},{12,10},{14,12},{1,15},{3,1}... | collective-permute-start | bytes 1572872 | tf_op jit(solution)/shard_map/ppermute | solution.py:22
  120.0 6.6 %copy-start.1 = (bf16[32,4,32,128]{3,2,1,0:T(8,128)(2,1)S(1)}, bf16[32,4,32,128]{3,2,1,0:T(8,128)(2,1)}, u32[]{:S(2)}) copy-start(bf16[32,4,32,128]{3,2,1,0:T(8,128)(2,1)} %copy-done) | copy-start | bytes 3145732
  120.0 6.6 %copy-start.3 = (bf16[32,4,32,128]{3,2,1,0:T(8,128)(2,1)S(1)}, bf16[32,4,32,128]{3,2,1,0:T(8,128)(2,1)}, u32[]{:S(2)}) copy-start(bf16[32,4,32,128]{3,2,1,0:T(8,128)(2,1)} %copy-done.2) | copy-start | bytes 3145732
  136.9 34.7 %all-to-all-start.3 = ((bf16[32,2,4,32,128]{4,3,2,1,0:T(8,128)(2,1)}), bf16[32,2,4,32,128]{4,3,2,1,0:T(8,128)(2,1)S(1)}, u32[]{:S(2)}, u32[]{:S(2)}) async-start(bf16[32,2,4,32,128]{4,3,2,1,0:T(8,128)(2,1)} %triangle_products.5), calls=%async_computation.3 | async-start | bytes 4194304 | tf_op jit(solution)/shard_map/all_to_all | solution.py:18
  178.3 1.2 copy-start.6

commit v2 on v1

v2 whole, which is shorter than its diff:
```python
import functools

import jax
import jax.numpy as jnp
from jax import lax
from jax.experimental import pallas as pl
from jax.experimental.pallas import tpu as pltpu
from jax.sharding import Mesh, PartitionSpec as P

PLANE = ("y", "xh", "xl", "c")
GROUPS = 32
SLABS = 8
STEP_ROWS = 16
VMEM_LIMIT = 48 * 1024 * 1024


def all_to_all(x, axes):
    return lax.all_to_all(x, axes, split_axis=0, concat_axis=0, tiled=True)


def shift(x, by):
    return lax.ppermute(x, "z", [(i, (i + by) % SLABS) for i in range(SLABS)])


def normalize(pair_ref, gain_ref, bias_ref):
    x = pair_ref[...].astype(jnp.float32)
    x = x.reshape(x.shape[0] * x.shape[1], x.shape[2])
    centred = x - jnp.mean(x, axis=1, keepdims=True)
    inverse = lax.rsqrt(jnp.mean(centred * centred, axis=1, keepdims=True) + 1e-05)
    xhat = centred * inverse
    normed = (xhat * gain_ref[...] + bias_ref[...]).astype(jnp.bfloat16)
    return xhat, inverse, normed


def lane_order(transposed):
    source = lax.broadcasted_iota(jnp.int32, (128, 128), 1 if transposed else 0)
    lane = lax.broadcasted_iota(jnp.int32, (128, 128), 0 if transposed else 1)
    wanted = ((lane >> 1) & 1) * 64 + (lane >> 2) * 2 + (lane & 1)
    return jnp.where(source == wanted, 1.0, 0.0).astype(jnp.float32)


def pre_kernel(pair_ref, gain_ref, bias_ref, weight_ref, a_ref, b_ref, ordered_ref):
    @pl.when(pl.program_id(0) == 0)
    def _():
        order = lane_order(False).astype(jnp.bfloat16)
        for half in range(2):
            for kind in range(2):
                left = weight_ref[:, 128 * kind + 64 * half : 128 * kind + 64 * half + 64]
                right = weight_ref[:, 256 + 128 * kind + 64 * half : 320 + 128 * kind + 64 * half]
                at = 256 * half + 128 * kind
                ordered_ref[:, at : at + 128] = jnp.dot(
                    jnp.concatenate([left, right], axis=1),
                    order,
                    preferred_element_type=jnp.float32,
                ).astype(jnp.bfloat16)

    _, _, normed = normalize(pair_ref, gain_ref, bias_ref)
    proj = jnp.dot(normed, ordered_ref[...], preferred_element_type=jnp.float32)
    for half, ref in enumerate((a_ref, b_ref)):
        value = proj[:, 256 * half : 256 * half + 128]
        gate = proj[:, 256 * half + 128 : 256 * half + 256]
        ref[...] = (jax.nn.sigmoid(gate) * value).astype(jnp.bfloat16).reshape(ref.shape)


def pre(pair, gain, bias, weight):
    rows, cols, width = pair.shape
    tile = pl.BlockSpec((STEP_ROWS, cols, width), lambda i: (i, 0, 0))
    whole = lambda *shape: pl.BlockSpec(shape, lambda i: (0,) * len(shape))
    return pl.pallas_call(
        pre_kernel,
        grid=(rows // STEP_ROWS,),
        in_specs=[tile, whole(1, width), whole(1, width), whole(*weight.shape)],
        out_specs=[tile, tile, whole(*weight.shape)],
        out_shape=[jax.ShapeDtypeStruct(pair.shape, jnp.bfloat16)] * 2
        + [jax.ShapeDtypeStruct(weight.shape, jnp.bfloat16)],
        compiler_params=pltpu.CompilerParams(vmem_limit_bytes=VMEM_LIMIT),
        cost_estimate=pl.CostEstimate(
            flops=2 * rows * cols * width * 512, bytes_accessed=12 << 20, transcendentals=1 << 20
        ),
        name="gated_projections",
    )(pair, gain, bias, weight)


def post_kernel(
    pair_ref, a_ref, b_ref, gain_ref, bias_ref, ordered_ref, grad_ref, total_ref, wgrad_ref
):
    step = pl.program_id(0)

    @pl.when(step == 0)
    def _():
        total_ref[...] = jnp.zeros_like(total_ref)
        wgrad_ref[...] = jnp.zeros_like(wgrad_ref)

    xhat, inverse, normed = normalize(pair_ref, gain_ref, bias_ref)
    proj = jnp.dot(normed, ordered_ref[...], preferred_element_type=jnp.float32)
    width = xhat.shape[1]
    parts = []
    for half, ref in enumerate((a_ref, b_ref)):
        value = proj[:, 256 * half : 256 * half + 128]
        gate = jax.nn.sigmoid(proj[:, 256 * half + 128 : 256 * half + 256])
        gated = ref[...].astype(jnp.float32).reshape(xhat.shape) * gate
        parts.append(gated.astype(jnp.bfloat16))
        parts.append((gated * value * (1.0 - gate)).astype(jnp.bfloat16))
    dproj = jnp.concatenate(parts, axis=1)
    dnormed = lax.dot_general(
        dproj, ordered_ref[...], (((1,), (1,)), ((), ())), preferred_element_type=jnp.float32
    )
    wgrad_ref[...] += lax.dot_general(
        normed, dproj, (((0,), (0,)), ((), ())), preferred_element_type=jnp.float32
    )
    total_ref[4 * width : 4 * width + 1, :] += jnp.sum(dnormed * xhat, axis=0, keepdims=True)
    total_ref[4 * width + 8 : 4 * width + 9, :] += jnp.sum(dnormed, axis=0, keepdims=True)
    g = dnormed * gain_ref[...]
    grad = (
        g
        - jnp.mean(g, axis=1, keepdims=True)
        - xhat * jnp.mean(g * xhat, axis=1, keepdims=True)
    ) * inverse
    grad_ref[...] = grad.astype(jnp.bfloat16).reshape(grad_ref.shape)

    @pl.when(step == pl.num_programs(0) - 1)
    def _():
        order = lane_order(True)
        plain = [
            jnp.dot(
                wgrad_ref[:, 128 * n : 128 * n + 128],
                order,
                precision=lax.Precision.HIGHEST,
                preferred_element_type=jnp.float32,
            )
            for n in range(4)
        ]
        for side in range(2):
            for kind in range(2):
                at = (2 * side + kind) * width
                total_ref[at : at + width, :] = jnp.concatenate(
                    [plain[2 * half + kind][:, 64 * side : 64 * side + 64] for half in range(2)],
                    axis=1,
                )


def post(pair, a, b, gain, bias, ordered, total_rows):
    rows, cols, width = pair.shape
    tile = pl.BlockSpec((STEP_ROWS, cols, width), lambda i: (i, 0, 0))
    whole = lambda *shape: pl.BlockSpec(shape, lambda i: (0,) * len(shape))
    return pl.pallas_call(
        post_kernel,
        grid=(rows // STEP_ROWS,),
        in_specs=[tile, tile, tile, whole(1, width), whole(1, width), whole(*ordered.shape)],
        out_specs=[tile, whole(total_rows, width)],
        out_shape=[
            jax.ShapeDtypeStruct(pair.shape, jnp.bfloat16),
            jax.ShapeDtypeStruct((total_rows, width), jnp.float32),
        ],
        scratch_shapes=[pltpu.VMEM(ordered.shape, jnp.float32)],
        compiler_params=pltpu.CompilerParams(vmem_limit_bytes=VMEM_LIMIT),
        cost_estimate=pl.CostEstimate(
            flops=6 * rows * cols * width * 512, bytes_accessed=20 << 20, transcendentals=1 << 20
        ),
        name="input_gradients",
    )(pair, a, b, gain, bias, ordered)


def assemble(ref, at):
    return jnp.concatenate(
        [
            jnp.concatenate([ref[4 * r + c, at] for c in range(4)], axis=0)
            for r in range(8)
        ],
        axis=1,
    )


def product_kernel(offsets, slab_ref, sides_ref, *refs):
    block_refs = refs[: len(offsets)]
    out_ref, grads = refs[len(offsets) :]
    slab = slab_ref[0]
    for offset, ref in zip(offsets, block_refs):
        where = lax.rem(slab + offset, SLABS)
        for x in range(2):
            rows = pl.ds(pl.multiple_of(512 * x + 64 * where, 64), 64)
            for r in range(8):
                grads[rows, 128 * r : 128 * r + 128] = jnp.concatenate(
                    [ref[4 * r + 2 * x, 0], ref[4 * r + 2 * x + 1, 0]], axis=0
                )
    left = assemble(sides_ref.at[:, 0], 0)
    right = assemble(sides_ref.at[:, 1], 0)
    first = jnp.dot(right, grads[...], preferred_element_type=jnp.float32)
    second = lax.dot_general(
        left, grads[...], (((1,), (1,)), ((), ())), preferred_element_type=jnp.float32
    )
    for side, value in enumerate((first, second)):
        value = value.astype(jnp.bfloat16)
        for r in range(8):
            for c in range(4):
                out_ref[4 * r + c, side, 0] = value[
                    32 * c : 32 * c + 32, 128 * r : 128 * r + 128
                ]


def products(slab, sides, blocks):
    groups, pairs, depth, width = sides.shape
    channels = pairs // 2
    sides = sides.reshape(groups, 2, channels, depth, width)
    sides_spec = pl.BlockSpec((groups, 2, 1, depth, width), lambda h: (0, 0, h, 0, 0))
    piece = pl.BlockSpec((groups, 1, depth, width), lambda h: (0, h, 0, 0))
    out = pl.pallas_call(
        functools.partial(product_kernel, [offset for offset, _ in blocks]),
        grid=(channels,),
        in_specs=[pl.BlockSpec(memory_space=pltpu.SMEM), sides_spec] + [piece] * len(blocks),
        out_specs=sides_spec,
        out_shape=jax.ShapeDtypeStruct(sides.shape, jnp.bfloat16),
        scratch_shapes=[pltpu.VMEM((1024, 1024), jnp.bfloat16)],
        compiler_params=pltpu.CompilerParams(vmem_limit_bytes=VMEM_LIMIT),
        cost_estimate=pl.CostEstimate(
            flops=4 * channels * 128 * 1024 * 1024, bytes_accessed=12 << 20, transcendentals=0
        ),
        name="triangle_products",
    )(slab, sides, *[block for _, block in blocks])
    return out.reshape(groups, pairs, depth, width)


def per_device(pair, layernorm_gain, layernorm_bias, proj_weight, product_grad):
    rows, cols, width = pair.shape
    barrier = lax.optimization_barrier
    split = lambda x: jnp.transpose(x, (2, 1, 0)).reshape(GROUPS, -1, cols, rows)
    join = lambda x: jnp.transpose(x.reshape(width, cols, rows), (2, 1, 0))
    gain = layernorm_gain.reshape(1, width)
    bias = layernorm_bias.reshape(1, width)
    slab = lax.axis_index("z").astype(jnp.int32).reshape(1)
    both = lambda pair_of: (shift(pair_of[0], 1), shift(pair_of[1], -1))

    half = width // 2
    a0 = all_to_all(split(product_grad[:, :, :half]), PLANE)
    a1 = both((a0, a0))
    sides_a, sides_b, ordered = pre(pair, gain, bias, proj_weight)
    b0, a0 = barrier((split(product_grad[:, :, half:]), a0))
    b0 = all_to_all(b0, PLANE)
    sides_a, b0, a1 = barrier((split(sides_a), b0, a1))
    a2 = both(a1)
    b1 = both((b0, b0))
    sides_a = all_to_all(sides_a, PLANE)
    sides_b, sides_a, a2, b1 = barrier((split(sides_b), sides_a, a2, b1))
    a3 = both(a2)
    b2 = both(b1)
    sides_b = all_to_all(sides_b, PLANE)
    sides_b, a3, b2 = barrier((sides_b, a3, b2))
    a4 = shift(a3[0], 1)
    b3 = both(b2)
    near = lambda x0, x1, x2, x3: [
        (0, x0), (7, x1[0]), (1, x1[1]), (6, x2[0]), (2, x2[1]), (5, x3[0]), (3, x3[1])
    ]
    back_a = products(slab, sides_a, near(a0, a1, a2, a3) + [(4, a4)])
    b4 = shift(b3[1], -1)
    back_a = all_to_all(back_a, PLANE)
    back_b = products(slab, sides_b, near(b0, b1, b2, b3) + [(4, b4)])
    back_b = all_to_all(back_b, PLANE)

    total_rows = 24 * GROUPS
    pairwise_gradient, total = post(
        pair, join(back_a), join(back_b), gain, bias, ordered, total_rows
    )
    total = jnp.sum(all_to_all(total.reshape(GROUPS, 24, width), PLANE), axis=0)
    total = all_to_all(jnp.broadcast_to(total[None], (SLABS, 24, width)), "z")
    total = jnp.sum(total, axis=0) / (rows * 8)
    total = all_to_all(jnp.broadcast_to(total[None], (GROUPS, 24, width)), PLANE)
    total = total.reshape(total_rows, width)
    proj_grad = jnp.transpose(total[: 4 * width].reshape(4, width, width), (1, 0, 2))
    proj_grad = proj_grad.reshape(width, 4 * width)
    layernorm_gradient = jnp.stack([total[4 * width], total[4 * width + 8]])
    return pairwise_gradient, proj_grad, layernorm_gradient


def solution(mesh):
    fine = Mesh(mesh.devices.reshape(4, 2, 2, 8, 2), ("y", "xh", "xl", "z", "c"))
    tiles = P(("y", "xh"), ("xl", "z", "c"), None)
    return jax.shard_map(
        per_device,
        mesh=fine,
        in_specs=(tiles, P(), P(), P(), tiles),
        out_specs=(tiles, P(), P()),
        check_vma=False,
    )
```

time: 248 us -> 244 us (0.984)
  blocking collectives: 106 us -> 60.7 us
  starting transfers between devices: 23.9 us -> 55.9 us
  waiting for transfers between devices: 66 us -> 79.7 us
  Pallas kernels: 29.6 us -> 23.8 us
    ppermute x8 -> x14, waiting for transfers between devices: 23.2 us -> 62.5 us  [shift(): return lax.ppermute(x, 'z', [(i, (i + by) % SLABS) for i in range(SLABS)])]
    all_to_all x2 -> x5, waiting for transfers between devices: 42.7 us -> 17.2 us  [all_to_all(): return lax.all_to_all(x, axes, split_axis=0, concat_axis=0, tiled=True)]
    all_to_all x2 -> x5, starting transfers between devices: 11.1 us -> 34.5 us  [all_to_all(): return lax.all_to_all(x, axes, split_axis=0, concat_axis=0, tiled=True)]
    all_to_all x4, blocking collectives: 83.8 us -> 60.7 us  [all_to_all(): return lax.all_to_all(x, axes, split_axis=0, concat_axis=0, tiled=True)]
    psum x1 -> x0, blocking collectives: 22.3 us -> none  [per_device(): total = lax.psum(total, 'z') / (rows * 8)]
    ppermute x8 -> x14, starting transfers between devices: 12.8 us -> 21.4 us  [shift(): return lax.ppermute(x, 'z', [(i, (i + by) % SLABS) for i in range(SLABS)])]
    pallas_call x3 -> x2, Pallas kernels: 16.9 us -> 10.3 us  [products(): pl.pallas_call(functools.partial(product_kernel, [offset for offset, _ in...]
    reshape x0 -> x2, local copies, waits for them, and re-layouts: none -> 5.03 us  [per_device(): join = lambda x: jnp.transpose(x.reshape(width, cols, rows), (2, 1, 0))]
  transfers between devices with their start and end apart: 10 -> 19, of which waited for: 4 -> 9; matrix products, arithmetic and copies ran while one was open for 3% -> 4% of each run, Pallas kernels for 7% -> 6%
where the time goes in v2:
time: 244 us; the launch traced here: 243 us
  waiting for transfers between devices  79.7 us (33%)
  blocking collectives  60.7 us (25%)
  starting transfers between devices  55.9 us (23%)
  Pallas kernels  23.8 us (10%)
  local copies, waits for them, and re-layouts  21.1 us (9%)
    ppermute x14, waiting for transfers between devices, shift(): return lax.ppermute(x, 'z', [(i, (i + by) % SLABS) for i in range(SLABS)])  62.5 us
    all_to_all x4, blocking collectives, all_to_all(): return lax.all_to_all(x, axes, split_axis=0, concat_axis=0, tiled=True)  60.7 us
    all_to_all x5, starting transfers between devices, all_to_all(): return lax.all_to_all(x, axes, split_axis=0, concat_axis=0, tiled=True)  34.5 us
    ppermute x14, starting transfers between devices, shift(): return lax.ppermute(x, 'z', [(i, (i + by) % SLABS) for i in range(SLABS)])  21.4 us
    all_to_all x5, waiting for transfers between devices, all_to_all(): return lax.all_to_all(x, axes, split_axis=0, concat_axis=0, tiled=True)  17.2 us
    transpose x5, local copies, waits for them, and re-layouts, per_device(): jnp.transpose(x, (2, 1, 0)).reshape(GROUPS, -1, cols, rows)  10.4 us
    pallas_call x2, Pallas kernels, products(): pl.pallas_call(functools.partial(product_kernel, [offset for offset, _ in...  10.3 us
    pallas_call x1, Pallas kernels, post(): pl.pallas_call(post_kernel, grid=(rows // STEP_ROWS,), in_specs=[tile, ti...  8.42 us
  transfers between devices with their start and end apart: 19, of which 9 were waited for; matrix products, arithmetic and copies ran while one was open for 4% of the time, Pallas kernels for 6%

profile of v2, /device:TPU:1, one launch (start us, length us, event | category | flops | bytes accessed | tf_op | source)
XLA Modules:
  0.0 242.5 jit_solution(3661911163258787774)
XLA Ops:
  0.6 2.0 slice_bitcast_fusion
  4.2 19.9 %all_to_all.45.refs_0_ = bf16[32,2,32,128]{3,2,1,0:T(8,128)(2,1)S(1)} all-to-all(bf16[32,2,32,128]{3,2,1,0:T(8,128)(2,1)S(1)} %bitcast.41), channel_id=1, replica_groups=mesh['y'=4,'xh'=2,'xl'=2,'z'=8,'c'=2] {'y','xh','xl','c'}, dimensions={0} | all-to-all | bytes 1048576 | tf_op jit(solution)/shard_map/all_to_all | solution.py:18
  24.2 5.6 %collective-permute-start.1 = (bf16[32,2,32,128]{3,2,1,0:T(8,128)(2,1)S(1)}, bf16[32,2,32,128]{3,2,1,0:T(8,128)(2,1)}, u32[]{:S(2)}, u32[]{:S(2)}) collective-permute-start(bf16[32,2,32,128]{3,2,1,0:T(8,128)(2,1)S(1)} %all_to_all.45.refs_0_), channel_id=1, source_target_pairs={{0,14},{2,0},{4,2},{6,4},{8,6},{10,8},{12,10},{14,12},{1,15},{3,1}... | collective-permute-start | bytes 1572872 | tf_op jit(solution)/shard_map/ppermute | solution.py:22
  29.7 2.3 copy.24
  32.1 4.4 %all-to-all-start.1 = ((bf16[32,2,32,128]{3,2,1,0:T(8,128)(2,1)}), bf16[32,2,32,128]{3,2,1,0:T(8,128)(2,1)S(1)}, u32[]{:S(2)}, u32[]{:S(2)}) async-start(bf16[32,2,32,128]{3,2,1,0:T(8,128)(2,1)} %bitcast.8), calls=%async_computation.1 | async-start | bytes 1048576 | tf_op jit(solution)/shard_map/all_to_all | solution.py:18
  38.4 5.0 %gated_projections.1 = (bf16[128,32,128]{2,1,0:T(8,128)(2,1)S(1)}, bf16[128,32,128]{2,1,0:T(8,128)(2,1)S(1)}, bf16[128,512]{1,0:T(8,128)(2,1)S(1)}) custom-call(bf16[128,32,128]{2,1,0:T(8,128)(2,1)S(1)} %copy-done.4, f32[1,128]{1,0:T(1,128)S(1)} %bitcast.35, f32[1,128]{1,0:T(1,128)S(1)} %bitcast.37, bf16[128,512]{1,0:T(8,128)(2,1)S(1)} %copy-done.6), custom_call_target="tpu_custom_call" | custom-call | flops 536870912 | bytes 12582912 | tf_op jit(solution)/shard_map/gated_projections/pallas_call | solution.py:69
  43.4 2.3 copy.23
  45.7 2.5 %all-to-all-done.1.refs_0_ = bf16[32,2,32,128]{3,2,1,0:T(8,128)(2,1)S(1)} async-done(((bf16[32,2,32,128]{3,2,1,0:T(8,128)(2,1)}), bf16[32,2,32,128]{3,2,1,0:T(8,128)(2,1)S(1)}, u32[]{:S(2)}, u32[]{:S(2)}) %all-to-all-start.1) | async-done | bytes 524320 | tf_op jit(solution)/shard_map/all_to_all | solution.py:18
  48.1 5.1 %all-to-all-start.2 = ((bf16[32,4,32,128]{3,2,1,0:T(8,128)(2,1)}), bf16[32,4,32,128]{3,2,1,0:T(8,128)(2,1)}, u32[]{:S(2)}, u32[]{:S(2)}) async-start(bf16[32,4,32,128]{3,2,1,0:T(8,128)(2,1)} %bitcast.40), calls=%async_computation.2 | async-start | bytes 2097152 | tf_op jit(solution)/shard_map/all_to_all | solution.py:18
  53.4 3.0 %collective-permute-start.3 = (bf16[32,2,32,128]{3,2,1,0:T(8,128)(2,1)}, bf16[32,2,32,128]{3,2,1,0:T(8,128)(2,1)}, u32[]{:S(2)}, u32[]{:S(2)}) collective-permute-start(bf16[32,2,32,128]{3,2,1,0:T(8,128)(2,1)} %collective-permute-done.1.refs_2_), channel_id=1, source_target_pairs={{0,14},{2,0},{4,2},{6,4},{8,6},{10,8},{12,10},{14,12},{1,15},{3,1}... | collective-permute-start | bytes 1572872 | tf_op jit(solution)/shard_map/ppermute | solution.py:22
  57.8 2.3 copy.22
  60.1 8.5 %collective-permute-done.2.refs_3_ = bf16[32,2,32,128]{3,2,1,0:T(8,128)(2,1)} collective-permute-done((bf16[32,2,32,128]{3,2,1,0:T(8,128)(2,1)}, bf16[32,2,32,128]{3,2,1,0:T(8,128)(2,1)}, u32[]{:S(2)}, u32[]{:S(2)}) %collective-permute-start.2) | collective-permute-done | bytes 524320 | tf_op jit(solution)/shard_map/ppermute | solution.py:22
  68.7 10.2 %collective-permute-done.5.refs_2_ = bf16[32,2,32,128]{3,2,1,0:T(8,128)(2,1)S(1)} collective-permute-done((bf16[32,2,32,128]{3,2,1,0:T(8,128)(2,1)S(1)}, bf16[32,2,32,128]{3,2,1,0:T(8,128)(2,1)S(1)}, u32[]{:S(2)}, u32[]{:S(2)}) %collective-permute-start.5) | collective-permute-done | bytes 524320 | tf_op jit(solution)/shard_map/ppermute | solution.py:22
  79.8 7.9 %all-to-all-start.3 = ((bf16[32,4,32,128]{3,2,1,0:T(8,128)(2,1)}), bf16[32,4,32,128]{3,2,1,0:T(8,128)(2,1)}, u32[]{:S(2)}, u32[]{:S(2)}) async-start(bf16[32,4,32,128]{3,2,1,0:T(8,128)(2,1)} %bitcast.39), calls=%async_computation.3 | async-start | bytes 2097152 | tf_op jit(solution)/shard_map/all_to_all | solution.py:18
  88.0 2.8 %collective-permute-start.7 = (bf16[32,2,32,128]{3,2,1,0:T(8,128)(2,1)}, bf16[32,2,32,128]{3,2,1,0:T(8,128)(2,1)S(1)}, u32[]{:S(2)}, u32[]{:S(2)}) collective-permute-start(bf16[32,2,32,128]{3,2,1,0:T(8,128)(2,1)} %collective-permute-done.3.refs_4_), channel_id=1, source_target_pairs={{0,14},{2,0},{4,2},{6,4},{8,6},{10,8},{12,10},{14,12},{1,15},{3,1}... | collective-permute-start | bytes 1572872 | tf_op jit(solution)/shard_map/ppermute | solution.py:22
  90.8 2.7 %collective-permute-start.9 = (bf16[32,2,32,128]{3,2,1,0:T(8,128)(2,1)S(1)}, bf16[32,2,32,128]{3,2,1,0:T(8,128)(2,1)S(1)}, u32[]{:S(2)}, u32[]{:S(2)}) collective-permute-start(bf16[32,2,32,128]{3,2,1,0:T(8,128)(2,1)S(1)} %collective-permute-done.5.refs_2_), channel_id=1, source_target_pairs={{0,14},{2,0},{4,2},{6,4},{8,6},{10,8},{12,10},{14,12},{1,15},{3,1}... | collective-permute-start | bytes 1572872 | tf_op jit(solution)/shard_map/ppermute | solution.py:22
  93.5 9.3 %collective-permute-done.6.refs_5_ = bf16[32,2,32,128]{3,2,1,0:T(8,128)(2,1)S(1)} collective-permute-done((bf16[32,2,32,128]{3,2,1,0:T(8,128)(2,1)}, bf16[32,2,32,128]{3,2,1,0:T(8,128)(2,1)S(1)}, u32[]{:S(2)}, u32[]{:S(2)}) %collective-permute-start.6) | collective-permute-done | bytes 524320 | tf_op jit(solution)/shard_map/ppermute | solution.py:22
  103.6 10.4 %collective-permute-done.8.refs_3_ = bf16[32,2,32,128]{3,2,1,0:T(8,128)(2,1)S(1)} collective-permute-done((bf16[32,2,32,128]{3,2,1,0:T(8,128)(2,1)S(1)}, bf16[32,2,32,128]{3,2,1,0:T(8,128)(2,1)S(1)}, u32[]{:S(2)}, u32[]{:S(2)}) %collective-permute-start.8) | collective-permute-done | bytes 524320 | tf_op jit(solution)/shard_map/ppermute | solution.py:22
  116.8 11.2 %collective-permute-done.10.refs_7_ = bf16[32,2,32,128]{3,2,1,0:T(8,128)(2,1)} collective-permute-done((bf16[32,2,32,128]{3,2,1,0:T(8,128)(2,1)}, bf16[32,2,32,128]{3,2,1,0:T(8,128)(2,1)}, u32[]{:S(2)}, u32[]{:S(2)}) %collective-permute-start.10) | collective-permute-done | bytes 524320 | tf_op jit(solution)/shard_map/ppermute | solution.py:22
  130.1 5.3 %triangle_products.2 = bf16[32,2,2,32,128]{4,3,2,1,0:T(8,128)(2,1)} custom-call(s32[1]{0:T(128)} %bitcast.slab_ref, bf16[32,2,2,32,128]{4,3,2,1,0:T(8,128)(2,1)} %bitcast.11.sides_ref, bf16[32,2,32,128]{3,2,1,0:T(8,128)(2,1)S(1)} %all_to_all.45.refs_0_, bf16[32,2,32,128]{3,2,1,0:T(8,128)(2,1)} %collective-permute-done.refs_1_, ...), custom_call_target="tpu_custom_call" | custom-call | flops 1073741824 | bytes 12582912 | tf_op jit(solution)/shard_map/triangle_products/pallas_call | solution.py:207
  135.4 9.0 %all-to-all-start.4 = ((bf16[32,4,32,128]{3,2,1,0:T(8,128)(2,1)}), bf16[32,4,32,128]{3,2,1,0:T(8,128)(2,1)}, u32[]{:S(2)}, u32[]{:S(2)}) async-start(bf16[32,4,32,128]{3,2,1,0:T(8,128)(2,1)} %bitcast.12), calls=%async_computation.4 | async-start | bytes 2097152 | tf_op jit(solution)/shard_map/all_to_all | solution.py:18
  144.5 2.7 %collective-permute-start.13 = (bf16[32,2,32,128]{3,2,1,0:T(8,128)(2,1)}, bf16[32,2,32,128]{3,2,1,0:T(8,128)(2,1)S(1)}, u32[]{:S(2)}, u32[]{:S(2)}) collective-permute-start(bf16[32,2,32,128]{3,2,1,0:T(8,128)(2,1)} %collective-permute-done.12.refs_6_), channel_id=1, source_target_pairs={{0,14},{2,0},{4,2},{6,4},{8,6},{10,8},{12,10},{14,12},{1,15},{3,1}... | collective-permute-start | bytes 1572872 | tf_op jit(solution)/shard_map/ppermute | solution.py:22
  147.1 11.8 %collective-permute-done.11.refs_5_ = bf16[32,2,32,128]{3,2,1,0:T(8,128)(2,1)S(1)} collective-permute-done((bf16[32,2,32,128]{3,2,1,0:T(8,128)(2,1)S(1)}, bf16[32,2,32,128]{3,2,1,0:T(8,128)(2,1)S(1)}, u32[]{:S(2)}, u32[]{:S(2)}) %collective-permute-start.11) | collective-permute-done | bytes 524320 | tf_op jit(solution)/shard_map/ppermute | solution.py:22
  159.0 5.0 %triangle_products.3 = bf16[32,2,2,32,128]{4,3,2,1,0:T(8,128)(2,1)} custom-call(s32[1]{0:T(128)} %bitcast.slab_ref, bf16[32,2,2,32,128]{4,3,2,1,0:T(8,128)(2,1)} %bitcast.15.sides_ref, bf16[32,2,32,128]{3,2,1,0:T(8,128)(2,1)S(1)} %all-to-all-done.1.refs_0_, bf16[32,2,32,128]{3,2,1,0:T(8,128)(2,1)S(1)} %collective-permute-done.4.refs_1_, ...), custom_call_target="tpu_custom_call" | custom-call | flops 1073741824 | bytes 12582912 | tf_op jit(solution)/shard_map/triangle_products/pallas_call | solution.py:207
  164.0 8.1 %all-to-all-start.5 = ((bf16[32,4,32,128]{3,2,1,0:T(8,128)(2,1)}), bf16[32,4,32,128]{3,2,1,0:T(8,128)(2,1)}, u32[]{:S(2)}, u32[]{:S(2)}) async-start(bf16[32,4,32,128]{3,2,1,0:T(8,128)(2,1)} %bitcast.16), calls=%async_computation.5 | async-start | bytes 2097152 | tf_op jit(solution)/shard_map/all_to_all | solution.py:18
  172.1 2.5 %copy.26 = bf16[128,32,128]{0,1,2:T(8,128)(2,1)S(1)} copy(bf16[128,32,128]{2,1,0:T(8,128)(2,1)} %bitcast.13) | data formatting | bytes 2097152 | tf_op jit(solution)/shard_map/reshape | solution.py:227
  174.6 14.7 %all-to-all-done.5 = bf16[32,4,32,128]{3,2,1,0:T(8,128)(2,1)} async-done(((bf16[32,4,32,128]{3,2,1,0:T(8,128)(2,1)}), bf16[32,4,32,128]{3,2,1,0:T(8,128)(2,1)}, u32[]{:S(2)}, u32[]{:S(2)}) %all-to-all-start.5) | async-done | bytes 1048608 | tf_op jit(solution)/shard_map/all_to_all | solution.py:18
  189.4 2.6 %copy.27 = bf16[128,32,128]{0,1,2:T(8,128)(2,1)S(1)} copy(bf16[128,32,128]{2,1,0:T(8,128)(2,1)} %bitcast.17) | data formatting | bytes 2097152 | tf_op jit(solution)/shard_map/reshape | solution.py:227
  191.9 8.4 %input_gradients.1 = (bf16[128,32,128]{2,1,0:T(8,128)(2,1)}, f32[768,128]{1,0:T(8,128)S(1)}) custom-call(bf16[128,32,128]{2,1,0:T(8,128)(2,1)S(1)} %copy-done.5, bf16[128,32,128]{2,1,0:T(8,128)(2,1)S(1)} %bitcast.31, bf16[128,32,128]{2,1,0:T(8,128)(2,1)S(1)} %bitcast.32, f32[1,128]{1,0:T(1,128)S(1)} %bitcast.36, f32[1,128]{1,0:T(1,128)S(1)} %bitcast.38, ...), custom_call_target="tpu_custom_call" | custom-call | flops 1610612736 | bytes 20971520 | tf_op jit(solution)/shard_map/input_gradients/pallas_call | solution.py:146
  200.3 13.7 %all_to_all.46 = f32[32,24,128]{2,1,0:T(8,128)S(1)} all-to-all(f32[32,24,128]{2,1,0:T(8,128)S(1)} %bitcast.34), channel_id=1, replica_groups=mesh['y'=4,'xh'=2,'xl'=2,'z'=8,'c'=2] {'y','xh','xl','c'}, dimensions={0} | all-to-all | bytes 786432 | tf_op jit(solution)/shard_map/all_to_all | solution.py:18
  214.1 11.6 %all_to_all.47 = f32[8,24,128]{2,1,0:T(8,128)S(1)} all-to-all(f32[8,24,128]{2,1,0:T(8,128)S(1)} %broadcast_in_dim.4), channel_id=1, replica_groups=mesh['y'=4,'xh'=2,'xl'=2,'z'=8,'c'=2] {'z'}, dimensions={0} | all-to-all | bytes 196608 | tf_op jit(solution)/shard_map/all_to_all | solution.py:18
  225.8 15.4 %all_to_all.48 = f32[32,24,128]{2,1,0:T(8,128)S(1)} all-to-all(f32[32,24,128]{2,1,0:T(8,128)S(1)} %broadcast_in_dim.5), channel_id=1, replica_groups=mesh['y'=4,'xh'=2,'xl'=2,'z'=8,'c'=2] {'y','xh','xl','c'}, dimensions={0} | all-to-all | bytes 786432 | tf_op jit(solution)/shard_map/all_to_all | solution.py:18
  (48 shorter events, 13.4 us)
Async XLA Ops:
  24.2 24.0 %collective-permute-start.1 = (bf16[32,2,32,128]{3,2,1,0:T(8,128)(2,1)S(1)}, bf16[32,2,32,128]{3,2,1,0:T(8,128)(2,1)}, u32[]{:S(2)}, u32[]{:S(2)}) collective-permute-start(bf16[32,2,32,128]{3,2,1,0:T(8,128)(2,1)S(1)} %all_to_all.45.refs_0_), channel_id=1, source_target_pairs={{0,14},{2,0},{4,2},{6,4},{8,6},{10,8},{12,10},{14,12},{1,15},{3,1}... | collective-permute-start | bytes 1572872 | tf_op jit(solution)/shard_map/ppermute | solution.py:22
  29.7 18.4 %collective-permute-start = (bf16[32,2,32,128]{3,2,1,0:T(8,128)(2,1)S(1)}, bf16[32,2,32,128]{3,2,1,0:T(8,128)(2,1)}, u32[]{:S(2)}, u32[]{:S(2)}) collective-permute-start(bf16[32,2,32,128]{3,2,1,0:T(8,128)(2,1)S(1)} %all_to_all.45.refs_0_), channel_id=1, source_target_pairs={{0,2},{2,4},{4,6},{6,8},{8,10},{10,12},{12,14},{14,0},{1,3},{3,5},... | collective-permute-start | bytes 1572872 | tf_op jit(solution)/shard_map/ppermute | solution.py:22
  32.1 4.4 %copy-start.6 = (bf16[128,512]{1,0:T(8,128)(2,1)S(1)}, bf16[128,512]{1,0:T(8,128)(2,1)}, u32[]{:S(2)}) copy-start(bf16[128,512]{1,0:T(8,128)(2,1)} %weight_ref.1) | copy-start | bytes 393220
  32.1 16.1 %all-to-all-start.1 = ((bf16[32,2,32,128]{3,2,1,0:T(8,128)(2,1)}), bf16[32,2,32,128]{3,2,1,0:T(8,128)(2,1)S(1)}, u32[]{:S(2)}, u32[]{:S(2)}) async-start(bf16[32,2,32,128]{3,2,1,0:T(8,128)(2,1)} %bitcast.8), calls=%async_computation.1 | async-start | bytes 1048576 | tf_op jit(solution)/shard_map/all_to_all | solution.py:18
  36.5 0.7 copy-start.7
  36.5 0.7 copy-start.8
  37.1 1.2 copy-start.4
  48.1 31.7 %all-to-all-start.2 = ((bf16[32,4,32,128]{3,2,1,0:T(8,128)(2,1)}), bf16[32,4,32,128]{3,2,1,0:T(8,128)(2,1)}, u32[]{:S(2)}, u32[]{:S(2)}) async-start(bf16[32,4,32,128]{3,2,1,0:T(8,128)(2,1)} %bitcast.40), calls=%async_computation.2 | async-start | bytes 2097152 | tf_op jit(solution)/shard_map/all_to_all | solution.py:18
  53.3 15.4 %collective-permute-start.2 = (bf16[32,2,32,128]{3,2,1,0:T(8,128)(2,1)}, bf16[32,2,32,128]{3,2,1,0:T(8,128)(2,1)}, u32[]{:S(2)}, u32[]{:S(2)}) collective-permute-start(bf16[32,2,32,128]{3,2,1,0:T(8,128)(2,1)} %collective-permute-done.refs_1_), channel_id=1, source_target_pairs={{0,2},{2,4},{4,6},{6,8},{8,10},{10,12},{12,14},{14,0},{1,3},{3,5},... | collective-permute-start | bytes 1572872 | tf_op jit(solution)/shard_map/ppermute | solution.py:22
  53.4 15.3 %collective-permute-start.3 = (bf16[32,2,32,128]{3,2,1,0:T(8,128)(2,1)}, bf16[32,2,32,128]{3,2,1,0:T(8,128)(2,1)}, u32[]{:S(2)}, u32[]{:S(2)}) collective-permute-start(bf16[32,2,32,128]{3,2,1,0:T(8,128)(2,1)} %collective-permute-done.1.refs_2_), channel_id=1, source_target_pairs={{0,14},{2,0},{4,2},{6,4},{8,6},{10,8},{12,10},{14,12},{1,15},{3,1}... | collective-permute-start | bytes 1572872 | tf_op jit(solution)/shard_map/ppermute | solution.py:22
  56.4 22.4 %collective-permute-start.5 = (bf16[32,2,32,128]{3,2,1,0:T(8,128)(2,1)S(1)}, bf16[32,2,32,128]{3,2,1,0:T(8,128)(2,1)S(1)}, u32[]{:S(2)}, u32[]{:S(2)}) collective-permute-start(bf16[32,2,32,128]{3,2,1,0:T(8,128)(2,1)S(1)} %all-to-all-done.1.refs_0_), channel_id=1, source_target_pairs={{0,14},{2,0},{4,2},{6,4},{8,6},{10,8},{12,10},{14,12},{1,15},{3,1}... | collective-permute-start | bytes 1572872 | tf_op jit(solution)/shard_map/ppermute | solution.py:22
  57.8 22.0 %collective-permute-start.4 = (bf16[32,2,32,128]{3,2,1,0:T(8,128)(2,1)S(1)}, bf16[32,2,32,128]{3,2,1,0:T(8,128)(2,1)S(1)}, u32[]{:S(2)}, u32[]{:S(2)}) collective-permute-start(bf16[32,2,32,128]{3,2,1,0:T(8,128)(2,1)S(1)} %all-to-all-done.1.refs_0_), channel_id=1, source_target_pairs={{0,2},{2,4},{4,6},{6,8},{8,10},{10,12},{12,14},{14,0},{1,3},{3,5},... | collective-permute-start | bytes 1572872 | tf_op jit(solution)/shard_map/ppermute | solution.py:22
  79.8 34.2 %all-to-all-start.3 = ((bf16[32,4,32,128]{3,2,1,0:T(8,128)(2,1)}), bf16[32,4,32,128]{3,2,1,0:T(8,128)(2,1)}, u32[]{:S(2)}, u32[]{:S(2)}) async-start(bf16[32,4,32,128]{3,2,1,0:T(8,128)(2,1)} %bitcast.39), calls=%async_computation.3 | async-start | bytes 2097152 | tf_op jit(solution)/shard_map/all_to_all | solution.py:18
  87.7 15.1 %collective-permute-start.6 = (bf16[32,2,32,128]{3,2,1,0:T(8,128)(2,1)}, bf16[32,2,32,128]{3,2,1,0:T(8,128)(2,1)S(1)}, u32[]{:S(2)}, u32[]{:S(2)}) collective-permute-start(bf16[32,2,32,128]{3,2,1,0:T(8,128)(2,1)} %collective-permute-done.2.refs_3_), channel_id=1, source_target_pairs={{0,2},{2,4},{4,6},{6,8},{8,10},{10,12},{12,14},{14,0},{1,3},{3,5},... | collective-permute-start | bytes 1572872 | tf_op jit(solution)/shard_map/ppermute | solution.py:22
  88.0 14.8 %collective-permute-start.7 = (bf16[32,2,32,128]{3,2,1,0:T(8,128)(2,1)}, bf16[32,2,32,128]{3,2,1,0:T(8,128)(2,1)S(1)}, u32[]{:S(2)}, u32[]{:S(2)}) collective-permute-start(bf16[32,2,32,128]{3,2,1,0:T(8,128)(2,1)} %collective-permute-done.3.refs_4_), channel_id=1, source_target_pairs={{0,14},{2,0},{4,2},{6,4},{8,6},{10,8},{12,10},{14,12},{1,15},{3,1}... | collective-permute-start | bytes 1572872 | tf_op jit(solution)/shard_map/ppermute | solution.py:22
  90.8 23.2 %collective-permute-start.8 = (bf16[32,2,32,128]{3,2,1,0:T(8,128)(2,1)S(1)}, bf16[32,2,32,128]{3,2,1,0:T(8,128)(2,1)S(1)}, u32[]{:S(2)}, u32[]{:S(2)}) collective-permute-start(bf16[32,2,32,128]{3,2,1,0:T(8,128)(2,1)S(1)} %collective-permute-done.4.refs_1_), channel_id=1, source_target_pairs={{0,2},{2,4},{4,6},{6,8},{8,10},{10,12},{12,14},{14,0},{1,3},{3,5},... | collective-permute-start | bytes 1572872 | tf_op jit(solution)/shard_map/ppermute | solution.py:22
  90.8 23.2 %collective-permute-start.9 = (bf16[32,2,32,128]{3,2,1,0:T(8,128)(2,1)S(1)}, bf16[32,2,32,128]{3,2,1,0:T(8,128)(2,1)S(1)}, u32[]{:S(2)}, u32[]{:S(2)}) collective-permute-start(bf16[32,2,32,128]{3,2,1,0:T(8,128)(2,1)S(1)} %collective-permute-done.5.refs_2_), channel_id=1, source_target_pairs={{0,14},{2,0},{4,2},{6,4},{8,6},{10,8},{12,10},{14,12},{1,15},{3,1}... | collective-permute-start | bytes 1572872 | tf_op jit(solution)/shard_map/ppermute | solution.py:22
  102.8 11.2 %copy-start = (bf16[32,2,32,128]{3,2,1,0:T(8,128)(2,1)}, bf16[32,2,32,128]{3,2,1,0:T(8,128)(2,1)S(1)}, u32[]{:S(2)}) copy-start(bf16[32,2,32,128]{3,2,1,0:T(8,128)(2,1)S(1)} %collective-permute-done.6.refs_5_) | copy-start | bytes 1572868
  102.8 0.8 copy-start.2
  114.0 14.0 %collective-permute-start.10 = (bf16[32,2,32,128]{3,2,1,0:T(8,128)(2,1)}, bf16[32,2,32,128]{3,2,1,0:T(8,128)(2,1)}, u32[]{:S(2)}, u32[]{:S(2)}) collective-permute-start(bf16[32,2,32,128]{3,2,1,0:T(8,128)(2,1)} %copy-done), channel_id=1, source_target_pairs={{0,2},{2,4},{4,6},{6,8},{8,10},{10,12},{12,14},{14,0},{1,3},{3,5},... | collective-permute-start | bytes 1572872 | tf_op jit(solution)/shard_map/ppermute | solution.py:22
  114.8 29.7 %collective-permute-start.12 = (bf16[32,2,32,128]{3,2,1,0:T(8,128)(2,1)S(1)}, bf16[32,2,32,128]{3,2,1,0:T(8,128)(2,1)}, u32[]{:S(2)}, u32[]{:S(2)}) collective-permute-start(bf16[32,2,32,128]{3,2,1,0:T(8,128)(2,1)S(1)} %collective-permute-done.9.refs_4_), channel_id=1, source_target_pairs={{0,14},{2,0},{4,2},{6,4},{8,6},{10,8},{12,10},{14,12},{1,15},{3,1}... | collective-permute-start | bytes 1572872 | tf_op jit(solution)/shard_map/ppermute | solution.py:22
  128.0 1.0 copy-start.1
  129.1 1.0 copy-start.3
  135.4 28.6 %all-to-all-start.4 = ((bf16[32,4,32,128]{3,2,1,0:T(8,128)(2,1)}), bf16[32,4,32,128]{3,2,1,0:T(8,128)(2,1)}, u32[]{:S(2)}, u32[]{:S(2)}) async-start(bf16[32,4,32,128]{3,2,1,0:T(8,128)(2,1)} %bitcast.12), calls=%async_computation.4 | async-start | bytes 2097152 | tf_op jit(solution)/shard_map/all_to_all | solution.py:18
  144.4 14.6 %collective-permute-start.11 = (bf16[32,2,32,128]{3,2,1,0:T(8,128)(2,1)S(1)}, bf16[32,2,32,128]{3,2,1,0:T(8,128)(2,1)S(1)}, u32[]{:S(2)}, u32[]{:S(2)}) collective-permute-start(bf16[32,2,32,128]{3,2,1,0:T(8,128)(2,1)S(1)} %collective-permute-done.8.refs_3_), channel_id=1, source_target_pairs={{0,2},{2,4},{4,6},{6,8},{8,10},{10,12},{12,14},{14,0},{1,3},{3,5},... | collective-permute-start | bytes 1572872 | tf_op jit(solution)/shard_map/ppermute | solution.py:22
  144.5 14.5 %collective-permute-start.13 = (bf16[32,2,32,128]{3,2,1,0:T(8,128)(2,1)}, bf16[32,2,32,128]{3,2,1,0:T(8,128)(2,1)S(1)}, u32[]{:S(2)}, u32[]{:S(2)}) collective-permute-start(bf16[32,2,32,128]{3,2,1,0:T(8,128)(2,1)} %collective-permute-done.12.refs_6_), channel_id=1, source_target_pairs={{0,14},{2,0},{4,2},{6,4},{8,6},{10,8},{12,10},{14,12},{1,15},{3,1}... | collective-permute-start | bytes 1572872 | tf_op jit(solution)/shard_map/ppermute | solution.py:22
  164.0 25.3 %all-to-all-start.5 = ((bf16[32,4,32,128]{3,2,1,0:T(8,128)(2,1)}), bf16[32,4,32,128]{3,2,1,0:T(8,128)(2,1)}, u32[]{:S(2)}, u32[]{:S(2)}) async-start(bf16[32,4,32,128]{3,2,1,0:T(8,128)(2,1)} %bitcast.16), calls=%async_computation.5 | async-start | bytes 2097152 | tf_op jit(solution)/shard_map/all_to_all | solution.py:18
  189.3 2.6 %copy-start.5 = (bf16[128,32,128]{2,1,0:T(8,128)(2,1)S(1)}, bf16[128,32,128]{2,1,0:T(8,128)(2,1)}, u32[]{:S(2)}) copy-start(bf16[128,32,128]{2,1,0:T(8,128)(2,1)} %pair_ref.3) | copy-start | bytes 3145732

commit v3 on v2

--- a/solution.py
+++ b/solution.py
@@ -10,7 +10,7 @@
 PLANE = ("y", "xh", "xl", "c")
 GROUPS = 32
 SLABS = 8
-STEP_ROWS = 16
+STEP_ROWS = 64
 VMEM_LIMIT = 48 * 1024 * 1024
 
 
@@ -172,17 +172,30 @@
 
 
 def product_kernel(offsets, slab_ref, sides_ref, *refs):
-    block_refs = refs[: len(offsets)]
-    out_ref, grads = refs[len(offsets) :]
-    slab = slab_ref[0]
-    for offset, ref in zip(offsets, block_refs):
-        where = lax.rem(slab + offset, SLABS)
+    block_refs, out_ref, grads = refs[:-2], refs[-2], refs[-1]
+    if offsets is None:
+        blocks = [(z, block_refs[0].at[z]) for z in range(SLABS)]
+    else:
+        blocks = [
+            (lax.rem(slab_ref[0] + offset, SLABS), ref) for offset, ref in zip(offsets, block_refs)
+        ]
+    def place(where, ref):
         for x in range(2):
             rows = pl.ds(pl.multiple_of(512 * x + 64 * where, 64), 64)
             for r in range(8):
                 grads[rows, 128 * r : 128 * r + 128] = jnp.concatenate(
                     [ref[4 * r + 2 * x, 0], ref[4 * r + 2 * x + 1, 0]], axis=0
                 )
+
+    for where, ref in blocks:
+        place(where, ref)
+    if offsets is not None:
+        for channel in range(2):
+            pl.when(pl.program_id(0) == channel)(
+                functools.partial(
+                    place, lax.rem(slab_ref[0] + 4, SLABS), block_refs[len(offsets) + channel]
+                )
+            )
     left = assemble(sides_ref.at[:, 0], 0)
     right = assemble(sides_ref.at[:, 1], 0)
     first = jnp.dot(right, grads[...], preferred_element_type=jnp.float32)
@@ -198,16 +211,21 @@
                 ]
 
 
-def products(slab, sides, blocks):
+def products(slab, sides, offsets, blocks):
     groups, pairs, depth, width = sides.shape
     channels = pairs // 2
     sides = sides.reshape(groups, 2, channels, depth, width)
     sides_spec = pl.BlockSpec((groups, 2, 1, depth, width), lambda h: (0, 0, h, 0, 0))
-    piece = pl.BlockSpec((groups, 1, depth, width), lambda h: (0, h, 0, 0))
+    if offsets is None:
+        piece = pl.BlockSpec((SLABS, groups, 1, depth, width), lambda h: (0, 0, h, 0, 0))
+    else:
+        piece = pl.BlockSpec((groups, 1, depth, width), lambda h: (0, h, 0, 0))
+    alone = pl.BlockSpec((groups, 1, depth, width), lambda h: (0, 0, 0, 0))
+    pieces = [piece if block.shape[-3] == channels else alone for block in blocks]
     out = pl.pallas_call(
-        functools.partial(product_kernel, [offset for offset, _ in blocks]),
+        functools.partial(product_kernel, offsets),
         grid=(channels,),
-        in_specs=[pl.BlockSpec(memory_space=pltpu.SMEM), sides_spec] + [piece] * len(blocks),
+        in_specs=[pl.BlockSpec(memory_space=pltpu.SMEM), sides_spec] + pieces,
         out_specs=sides_spec,
         out_shape=jax.ShapeDtypeStruct(sides.shape, jnp.bfloat16),
         scratch_shapes=[pltpu.VMEM((1024, 1024), jnp.bfloat16)],
@@ -216,7 +234,7 @@
             flops=4 * channels * 128 * 1024 * 1024, bytes_accessed=12 << 20, transcendentals=0
         ),
         name="triangle_products",
-    )(slab, sides, *[block for _, block in blocks])
+    )(slab, sides, *blocks)
     return out.reshape(groups, pairs, depth, width)
 
 
@@ -231,29 +249,27 @@
     both = lambda pair_of: (shift(pair_of[0], 1), shift(pair_of[1], -1))
 
     half = width // 2
-    a0 = all_to_all(split(product_grad[:, :, :half]), PLANE)
-    a1 = both((a0, a0))
+    own_a = all_to_all(split(product_grad[:, :, :half]), PLANE)
+    grads_a = lax.all_gather(own_a, "z", axis=0, tiled=False)
     sides_a, sides_b, ordered = pre(pair, gain, bias, proj_weight)
-    b0, a0 = barrier((split(product_grad[:, :, half:]), a0))
-    b0 = all_to_all(b0, PLANE)
-    sides_a, b0, a1 = barrier((split(sides_a), b0, a1))
-    a2 = both(a1)
-    b1 = both((b0, b0))
+    own_b, own_a = barrier((split(product_grad[:, :, half:]), own_a))
+    own_b = all_to_all(own_b, PLANE)
+    b1 = both((own_b, own_b))
+    sides_a, own_b = barrier((split(sides_a), own_b))
     sides_a = all_to_all(sides_a, PLANE)
-    sides_b, sides_a, a2, b1 = barrier((split(sides_b), sides_a, a2, b1))
-    a3 = both(a2)
+    sides_b, sides_a, b1 = barrier((split(sides_b), sides_a, b1))
     b2 = both(b1)
     sides_b = all_to_all(sides_b, PLANE)
-    sides_b, a3, b2 = barrier((sides_b, a3, b2))
-    a4 = shift(a3[0], 1)
+    sides_b, b2 = barrier((sides_b, b2))
     b3 = both(b2)
-    near = lambda x0, x1, x2, x3: [
-        (0, x0), (7, x1[0]), (1, x1[1]), (6, x2[0]), (2, x2[1]), (5, x3[0]), (3, x3[1])
-    ]
-    back_a = products(slab, sides_a, near(a0, a1, a2, a3) + [(4, a4)])
-    b4 = shift(b3[1], -1)
+    sides_a, b3 = barrier((sides_a, b3))
+    back_a = products(slab, sides_a, None, [grads_a])
+    sides_b, back_a = barrier((sides_b, back_a))
     back_a = all_to_all(back_a, PLANE)
-    back_b = products(slab, sides_b, near(b0, b1, b2, b3) + [(4, b4)])
+    b4 = shift(b3[0][:, :1], 1), shift(b3[1][:, 1:], -1)
+    back_b = products(
+        slab, sides_b, [0, 7, 1, 6, 2, 5, 3], [own_b, *b1, *b2, *b3, *b4]
+    )
     back_b = all_to_all(back_b, PLANE)
 
     total_rows = 24 * GROUPS

time: 244 us -> 236 us (0.967)
  between operations: 0.84 us -> 14.2 us
  starting transfers between devices: 55.9 us -> 44.2 us
  Pallas kernels: 23.8 us -> 19.6 us
  local copies, waits for them, and re-layouts: 21.1 us -> 18.4 us
    ppermute x14 -> x8, starting transfers between devices: 21.4 us -> 13.8 us  [shift(): return lax.ppermute(x, 'z', [(i, (i + by) % SLABS) for i in range(SLABS)])]
    ppermute x14 -> x8, waiting for transfers between devices: 62.5 us -> 56.3 us  [shift(): return lax.ppermute(x, 'z', [(i, (i + by) % SLABS) for i in range(SLABS)])]
    all_to_all x5, waiting for transfers between devices: 17.2 us -> 22.6 us  [all_to_all(): return lax.all_to_all(x, axes, split_axis=0, concat_axis=0, tiled=True)]
    all_to_all x5, starting transfers between devices: 34.5 us -> 30.4 us  [all_to_all(): return lax.all_to_all(x, axes, split_axis=0, concat_axis=0, tiled=True)]
    transpose x5 -> x3, local copies, waits for them, and re-layouts: 10.4 us -> 6.88 us  [per_device(): jnp.transpose(x, (2, 1, 0)).reshape(GROUPS, -1, cols, rows)]
    pallas_call x1, Pallas kernels: 8.42 us -> 5.48 us  [post(): pl.pallas_call(post_kernel, grid=(rows // STEP_ROWS,), in_specs=[tile, ti...]
  transfers between devices with their start and end apart: 19 -> 14, of which waited for: 9 -> 10; matrix products, arithmetic and copies ran while one was open for 4% -> 4% of each run, Pallas kernels for 6% -> 4%
where the time goes in v3:
time: 236 us; the launch traced here: 235 us
  waiting for transfers between devices  78.9 us (33%)
  blocking collectives  59 us (25%)
  starting transfers between devices  44.2 us (19%)
  Pallas kernels  19.6 us (8%)
  local copies, waits for them, and re-layouts  18.4 us (8%)
  between operations  14.2 us (6%)
    all_to_all x4, blocking collectives, all_to_all(): return lax.all_to_all(x, axes, split_axis=0, concat_axis=0, tiled=True)  59 us
    ppermute x8, waiting for transfers between devices, shift(): return lax.ppermute(x, 'z', [(i, (i + by) % SLABS) for i in range(SLABS)])  56.3 us
    all_to_all x5, starting transfers between devices, all_to_all(): return lax.all_to_all(x, axes, split_axis=0, concat_axis=0, tiled=True)  30.4 us
    all_to_all x5, waiting for transfers between devices, all_to_all(): return lax.all_to_all(x, axes, split_axis=0, concat_axis=0, tiled=True)  22.6 us
    ppermute x8, starting transfers between devices, shift(): return lax.ppermute(x, 'z', [(i, (i + by) % SLABS) for i in range(SLABS)])  13.8 us
    pallas_call x2, Pallas kernels, products(): pl.pallas_call(functools.partial(product_kernel, offsets), grid=(channels...  10.8 us
    transpose x3, local copies, waits for them, and re-layouts, per_device(): jnp.transpose(x, (2, 1, 0)).reshape(GROUPS, -1, cols, rows)  6.88 us
    pallas_call x1, Pallas kernels, post(): pl.pallas_call(post_kernel, grid=(rows // STEP_ROWS,), in_specs=[tile, ti...  5.48 us
  transfers between devices with their start and end apart: 14, of which 10 were waited for; matrix products, arithmetic and copies ran while one was open for 4% of the time, Pallas kernels for 4%

profile of v3, /device:TPU:1, one launch (start us, length us, event | category | flops | bytes accessed | tf_op | source)
XLA Modules:
  0.0 235.0 jit_solution(5897610079115366193)
XLA Ops:
  7.2 1.9 fusion
  10.8 20.0 %all_to_all.45 = bf16[32,2,32,128]{3,2,1,0:T(8,128)(2,1)} all-to-all(bf16[32,2,32,128]{3,2,1,0:T(8,128)(2,1)S(1)} %bitcast.45), channel_id=1, replica_groups=mesh['y'=4,'xh'=2,'xl'=2,'z'=8,'c'=2] {'y','xh','xl','c'}, dimensions={0} | all-to-all | bytes 1048576 | tf_op jit(solution)/shard_map/all_to_all | solution.py:18
  30.8 2.3 copy.31
  33.2 4.0 %all-to-all-start.1 = ((bf16[32,2,32,128]{3,2,1,0:T(8,128)(2,1)}), bf16[32,2,32,128]{3,2,1,0:T(8,128)(2,1)S(1)}, u32[]{:S(2)}, u32[]{:S(2)}) async-start(bf16[32,2,32,128]{3,2,1,0:T(8,128)(2,1)} %bitcast.7), calls=%async_computation.1 | async-start | bytes 1048576 | tf_op jit(solution)/shard_map/all_to_all | solution.py:18
  38.4 3.3 %gated_projections.1 = (bf16[128,32,128]{2,1,0:T(8,128)(2,1)S(1)}, bf16[128,32,128]{2,1,0:T(8,128)(2,1)S(1)}, bf16[128,512]{1,0:T(8,128)(2,1)S(1)}) custom-call(bf16[128,32,128]{2,1,0:T(8,128)(2,1)S(1)} %copy-done, f32[1,128]{1,0:T(1,128)S(1)} %bitcast.37, f32[1,128]{1,0:T(1,128)S(1)} %bitcast.39, bf16[128,512]{1,0:T(8,128)(2,1)S(1)} %copy-done.2), custom_call_target="tpu_custom_call" | custom-call | flops 536870912 | bytes 12582912 | tf_op jit(solution)/shard_map/gated_projections/pallas_call | solution.py:69
  41.8 2.3 copy.30
  44.0 4.8 %all-to-all-done.1.refs_0_ = bf16[32,2,32,128]{3,2,1,0:T(8,128)(2,1)S(1)} async-done(((bf16[32,2,32,128]{3,2,1,0:T(8,128)(2,1)}), bf16[32,2,32,128]{3,2,1,0:T(8,128)(2,1)S(1)}, u32[]{:S(2)}, u32[]{:S(2)}) %all-to-all-start.1) | async-done | bytes 524320 | tf_op jit(solution)/shard_map/all_to_all | solution.py:18
  48.8 4.0 %all-to-all-start.2 = ((bf16[32,4,32,128]{3,2,1,0:T(8,128)(2,1)}), bf16[32,4,32,128]{3,2,1,0:T(8,128)(2,1)S(1)}, u32[]{:S(2)}, u32[]{:S(2)}) async-start(bf16[32,4,32,128]{3,2,1,0:T(8,128)(2,1)} %bitcast.43), calls=%async_computation.2 | async-start | bytes 2097152 | tf_op jit(solution)/shard_map/all_to_all | solution.py:18
  52.9 5.7 %collective-permute-start.1 = (bf16[32,2,32,128]{3,2,1,0:T(8,128)(2,1)S(1)}, bf16[32,2,32,128]{3,2,1,0:T(8,128)(2,1)S(1)}, u32[]{:S(2)}, u32[]{:S(2)}) collective-permute-start(bf16[32,2,32,128]{3,2,1,0:T(8,128)(2,1)S(1)} %all-to-all-done.1.refs_0_), channel_id=1, source_target_pairs={{0,14},{2,0},{4,2},{6,4},{8,6},{10,8},{12,10},{14,12},{1,15},{3,1}... | collective-permute-start | bytes 1572872 | tf_op jit(solution)/shard_map/ppermute | solution.py:22
  58.5 2.3 copy.29
  60.8 20.0 %collective-permute-done.1.refs_2_ = bf16[32,2,32,128]{3,2,1,0:T(8,128)(2,1)S(1)} collective-permute-done((bf16[32,2,32,128]{3,2,1,0:T(8,128)(2,1)S(1)}, bf16[32,2,32,128]{3,2,1,0:T(8,128)(2,1)S(1)}, u32[]{:S(2)}, u32[]{:S(2)}) %collective-permute-start.1) | collective-permute-done | bytes 524320 | tf_op jit(solution)/shard_map/ppermute | solution.py:22
  80.8 3.8 %collective-permute-done.refs_1_ = bf16[32,2,32,128]{3,2,1,0:T(8,128)(2,1)} collective-permute-done((bf16[32,2,32,128]{3,2,1,0:T(8,128)(2,1)S(1)}, bf16[32,2,32,128]{3,2,1,0:T(8,128)(2,1)}, u32[]{:S(2)}, u32[]{:S(2)}) %collective-permute-start) | collective-permute-done | bytes 524320 | tf_op jit(solution)/shard_map/ppermute | solution.py:22
  84.6 8.7 %all-to-all-start.3 = ((bf16[32,4,32,128]{3,2,1,0:T(8,128)(2,1)}), bf16[32,4,32,128]{3,2,1,0:T(8,128)(2,1)}, u32[]{:S(2)}, u32[]{:S(2)}) async-start(bf16[32,4,32,128]{3,2,1,0:T(8,128)(2,1)} %bitcast.42), calls=%async_computation.3 | async-start | bytes 2097152 | tf_op jit(solution)/shard_map/all_to_all | solution.py:18
  93.4 2.7 %collective-permute-start.3 = (bf16[32,2,32,128]{3,2,1,0:T(8,128)(2,1)S(1)}, bf16[32,2,32,128]{3,2,1,0:T(8,128)(2,1)}, u32[]{:S(2)}, u32[]{:S(2)}) collective-permute-start(bf16[32,2,32,128]{3,2,1,0:T(8,128)(2,1)S(1)} %collective-permute-done.1.refs_2_), channel_id=1, source_target_pairs={{0,14},{2,0},{4,2},{6,4},{8,6},{10,8},{12,10},{14,12},{1,15},{3,1}... | collective-permute-start | bytes 1572872 | tf_op jit(solution)/shard_map/ppermute | solution.py:22
  96.1 12.1 %collective-permute-done.2.refs_3_ = bf16[32,2,32,128]{3,2,1,0:T(8,128)(2,1)} collective-permute-done((bf16[32,2,32,128]{3,2,1,0:T(8,128)(2,1)}, bf16[32,2,32,128]{3,2,1,0:T(8,128)(2,1)}, u32[]{:S(2)}, u32[]{:S(2)}) %collective-permute-start.2) | collective-permute-done | bytes 524320 | tf_op jit(solution)/shard_map/ppermute | solution.py:22
  108.1 2.4 %all-to-all-done.3 = bf16[32,4,32,128]{3,2,1,0:T(8,128)(2,1)} async-done(((bf16[32,4,32,128]{3,2,1,0:T(8,128)(2,1)}), bf16[32,4,32,128]{3,2,1,0:T(8,128)(2,1)}, u32[]{:S(2)}, u32[]{:S(2)}) %all-to-all-start.3) | async-done | bytes 1048608 | tf_op jit(solution)/shard_map/all_to_all | solution.py:18
  110.6 2.7 %collective-permute-start.5 = (bf16[32,2,32,128]{3,2,1,0:T(8,128)(2,1)}, bf16[32,2,32,128]{3,2,1,0:T(8,128)(2,1)S(1)}, u32[]{:S(2)}, u32[]{:S(2)}) collective-permute-start(bf16[32,2,32,128]{3,2,1,0:T(8,128)(2,1)} %collective-permute-done.3.refs_4_), channel_id=1, source_target_pairs={{0,14},{2,0},{4,2},{6,4},{8,6},{10,8},{12,10},{14,12},{1,15},{3,1}... | collective-permute-start | bytes 1572872 | tf_op jit(solution)/shard_map/ppermute | solution.py:22
  113.2 11.9 %collective-permute-done.4.refs_5_ = bf16[32,2,32,128]{3,2,1,0:T(8,128)(2,1)S(1)} collective-permute-done((bf16[32,2,32,128]{3,2,1,0:T(8,128)(2,1)}, bf16[32,2,32,128]{3,2,1,0:T(8,128)(2,1)S(1)}, u32[]{:S(2)}, u32[]{:S(2)}) %collective-permute-start.4) | collective-permute-done | bytes 524320 | tf_op jit(solution)/shard_map/ppermute | solution.py:22
  125.1 5.6 %triangle_products.2 = bf16[32,2,2,32,128]{4,3,2,1,0:T(8,128)(2,1)} custom-call(s32[1]{0:T(128)} %bitcast.10.slab_ref, bf16[32,2,2,32,128]{4,3,2,1,0:T(8,128)(2,1)S(1)} %bitcast.31, bf16[8,32,2,32,128]{4,3,2,1,0:T(8,128)(2,1)} %bitcast.41), custom_call_target="tpu_custom_call" | custom-call | flops 1073741824 | bytes 12582912 | tf_op jit(solution)/shard_map/triangle_products/pallas_call | solution.py:225
  130.7 5.8 %all-to-all-start.4 = ((bf16[32,4,32,128]{3,2,1,0:T(8,128)(2,1)}), bf16[32,4,32,128]{3,2,1,0:T(8,128)(2,1)}, u32[]{:S(2)}, u32[]{:S(2)}) async-start(bf16[32,4,32,128]{3,2,1,0:T(8,128)(2,1)} %bitcast.13), calls=%async_computation.4 | async-start | bytes 2097152 | tf_op jit(solution)/shard_map/all_to_all | solution.py:18
  136.6 2.7 %collective-permute-start.7 = (bf16[32,1,32,128]{3,2,1,0:T(8,128)(2,1)S(1)}, bf16[32,1,32,128]{3,2,1,0:T(8,128)(2,1)S(1)}, u32[]{:S(2)}, u32[]{:S(2)}) collective-permute-start(bf16[32,1,32,128]{3,2,1,0:T(8,128)(2,1)S(1)} %slice.24), channel_id=1, source_target_pairs={{0,14},{2,0},{4,2},{6,4},{8,6},{10,8},{12,10},{14,12},{1,15},{3,1}... | collective-permute-start | bytes 786440 | tf_op jit(solution)/shard_map/ppermute | solution.py:22
  139.4 5.4 %collective-permute-done.7.refs_8_ = bf16[32,1,32,128]{3,2,1,0:T(8,128)(2,1)S(1)} collective-permute-done((bf16[32,1,32,128]{3,2,1,0:T(8,128)(2,1)S(1)}, bf16[32,1,32,128]{3,2,1,0:T(8,128)(2,1)S(1)}, u32[]{:S(2)}, u32[]{:S(2)}) %collective-permute-start.7) | collective-permute-done | bytes 262176 | tf_op jit(solution)/shard_map/ppermute | solution.py:22
  144.7 3.2 %collective-permute-done.6.refs_7_ = bf16[32,1,32,128]{3,2,1,0:T(8,128)(2,1)S(1)} collective-permute-done((bf16[32,1,32,128]{3,2,1,0:T(8,128)(2,1)S(1)}, bf16[32,1,32,128]{3,2,1,0:T(8,128)(2,1)S(1)}, u32[]{:S(2)}, u32[]{:S(2)}) %collective-permute-start.6) | collective-permute-done | bytes 262176 | tf_op jit(solution)/shard_map/ppermute | solution.py:22
  147.9 5.2 %triangle_products.3 = bf16[32,2,2,32,128]{4,3,2,1,0:T(8,128)(2,1)} custom-call(s32[1]{0:T(128)} %bitcast.10.slab_ref, bf16[32,2,2,32,128]{4,3,2,1,0:T(8,128)(2,1)} %bitcast.16.sides_ref, bf16[32,2,32,128]{3,2,1,0:T(8,128)(2,1)S(1)} %all-to-all-done.1.refs_0_, bf16[32,2,32,128]{3,2,1,0:T(8,128)(2,1)} %collective-permute-done.refs_1_, ...), custom_call_target="tpu_custom_call" | custom-call | flops 1073741824 | bytes 12582912 | tf_op jit(solution)/shard_map/triangle_products/pallas_call | solution.py:225
  153.8 7.8 %all-to-all-start.5 = ((bf16[32,4,32,128]{3,2,1,0:T(8,128)(2,1)}), bf16[32,4,32,128]{3,2,1,0:T(8,128)(2,1)S(1)}, u32[]{:S(2)}, u32[]{:S(2)}) async-start(bf16[32,4,32,128]{3,2,1,0:T(8,128)(2,1)} %bitcast.17), calls=%async_computation.5 | async-start | bytes 2097152 | tf_op jit(solution)/shard_map/all_to_all | solution.py:18
  161.6 2.5 %copy.33 = bf16[128,32,128]{0,1,2:T(8,128)(2,1)S(1)} copy(bf16[128,32,128]{2,1,0:T(8,128)(2,1)} %bitcast.14) | data formatting | bytes 2097152 | tf_op jit(solution)/shard_map/reshape | solution.py:245
  164.2 14.7 %all-to-all-done.5 = bf16[32,4,32,128]{3,2,1,0:T(8,128)(2,1)S(1)} async-done(((bf16[32,4,32,128]{3,2,1,0:T(8,128)(2,1)}), bf16[32,4,32,128]{3,2,1,0:T(8,128)(2,1)S(1)}, u32[]{:S(2)}, u32[]{:S(2)}) %all-to-all-start.5) | async-done | bytes 1048608 | tf_op jit(solution)/shard_map/all_to_all | solution.py:18
  179.8 2.5 %copy.34 = bf16[128,32,128]{0,1,2:T(8,128)(2,1)S(1)} copy(bf16[128,32,128]{2,1,0:T(8,128)(2,1)} %bitcast.44) | data formatting | bytes 2097152 | tf_op jit(solution)/shard_map/reshape | solution.py:245
  182.3 5.5 %input_gradients.1 = (bf16[128,32,128]{2,1,0:T(8,128)(2,1)}, f32[768,128]{1,0:T(8,128)S(1)}) custom-call(bf16[128,32,128]{2,1,0:T(8,128)(2,1)S(1)} %copy-done.1, bf16[128,32,128]{2,1,0:T(8,128)(2,1)S(1)} %bitcast.33, bf16[128,32,128]{2,1,0:T(8,128)(2,1)S(1)} %bitcast.34, f32[1,128]{1,0:T(1,128)S(1)} %bitcast.38, f32[1,128]{1,0:T(1,128)S(1)} %bitcast.40, ...), custom_call_target="tpu_custom_call" | custom-call | flops 1610612736 | bytes 20971520 | tf_op jit(solution)/shard_map/input_gradients/pallas_call | solution.py:146
  187.8 13.7 %all_to_all.46 = f32[32,24,128]{2,1,0:T(8,128)S(1)} all-to-all(f32[32,24,128]{2,1,0:T(8,128)S(1)} %bitcast.36), channel_id=1, replica_groups=mesh['y'=4,'xh'=2,'xl'=2,'z'=8,'c'=2] {'y','xh','xl','c'}, dimensions={0} | all-to-all | bytes 786432 | tf_op jit(solution)/shard_map/all_to_all | solution.py:18
  201.5 9.9 %all_to_all.47 = f32[8,24,128]{2,1,0:T(8,128)S(1)} all-to-all(f32[8,24,128]{2,1,0:T(8,128)S(1)} %broadcast_in_dim.4), channel_id=1, replica_groups=mesh['y'=4,'xh'=2,'xl'=2,'z'=8,'c'=2] {'z'}, dimensions={0} | all-to-all | bytes 196608 | tf_op jit(solution)/shard_map/all_to_all | solution.py:18
  211.4 15.4 %all_to_all.48 = f32[32,24,128]{2,1,0:T(8,128)S(1)} all-to-all(f32[32,24,128]{2,1,0:T(8,128)S(1)} %broadcast_in_dim.5), channel_id=1, replica_groups=mesh['y'=4,'xh'=2,'xl'=2,'z'=8,'c'=2] {'y','xh','xl','c'}, dimensions={0} | all-to-all | bytes 786432 | tf_op jit(solution)/shard_map/all_to_all | solution.py:18
  (35 shorter events, 6.1 us)
Async XLA Ops:
  7.2 30.0 %copy-start.2 = (bf16[128,512]{1,0:T(8,128)(2,1)S(1)}, bf16[128,512]{1,0:T(8,128)(2,1)}, u32[]{:S(2)}) copy-start(bf16[128,512]{1,0:T(8,128)(2,1)} %weight_ref.1) | copy-start | bytes 393220
  7.2 30.0 %copy-start.4 = (f32[128]{0:T(128)S(1)}, f32[128]{0:T(128)}, u32[]{:S(2)}) copy-start(f32[128]{0:T(128)} %param.7) | copy-start | bytes 1540
  7.2 30.0 %copy-start.3 = (f32[128]{0:T(128)S(1)}, f32[128]{0:T(128)}, u32[]{:S(2)}) copy-start(f32[128]{0:T(128)} %param.6) | copy-start | bytes 1540
  7.2 117.9 %all-gather.3.cloned.1.call-start = ((), (), s32[]{:S(2)}) async-start(), calls=%async_computation.9 | async-start | bytes 4718592 | tf_op jit(solution)/shard_map/all_gather | solution.py:253
  33.2 15.7 %all-to-all-start.1 = ((bf16[32,2,32,128]{3,2,1,0:T(8,128)(2,1)}), bf16[32,2,32,128]{3,2,1,0:T(8,128)(2,1)S(1)}, u32[]{:S(2)}, u32[]{:S(2)}) async-start(bf16[32,2,32,128]{3,2,1,0:T(8,128)(2,1)} %bitcast.7), calls=%async_computation.1 | async-start | bytes 1048576 | tf_op jit(solution)/shard_map/all_to_all | solution.py:18
  37.2 1.2 copy-start
  48.8 35.8 %all-to-all-start.2 = ((bf16[32,4,32,128]{3,2,1,0:T(8,128)(2,1)}), bf16[32,4,32,128]{3,2,1,0:T(8,128)(2,1)S(1)}, u32[]{:S(2)}, u32[]{:S(2)}) async-start(bf16[32,4,32,128]{3,2,1,0:T(8,128)(2,1)} %bitcast.43), calls=%async_computation.2 | async-start | bytes 2097152 | tf_op jit(solution)/shard_map/all_to_all | solution.py:18
  52.9 28.0 %collective-permute-start.1 = (bf16[32,2,32,128]{3,2,1,0:T(8,128)(2,1)S(1)}, bf16[32,2,32,128]{3,2,1,0:T(8,128)(2,1)S(1)}, u32[]{:S(2)}, u32[]{:S(2)}) collective-permute-start(bf16[32,2,32,128]{3,2,1,0:T(8,128)(2,1)S(1)} %all-to-all-done.1.refs_0_), channel_id=1, source_target_pairs={{0,14},{2,0},{4,2},{6,4},{8,6},{10,8},{12,10},{14,12},{1,15},{3,1}... | collective-permute-start | bytes 1572872 | tf_op jit(solution)/shard_map/ppermute | solution.py:22
  58.5 26.1 %collective-permute-start = (bf16[32,2,32,128]{3,2,1,0:T(8,128)(2,1)S(1)}, bf16[32,2,32,128]{3,2,1,0:T(8,128)(2,1)}, u32[]{:S(2)}, u32[]{:S(2)}) collective-permute-start(bf16[32,2,32,128]{3,2,1,0:T(8,128)(2,1)S(1)} %all-to-all-done.1.refs_0_), channel_id=1, source_target_pairs={{0,2},{2,4},{4,6},{6,8},{8,10},{10,12},{12,14},{14,0},{1,3},{3,5},... | collective-permute-start | bytes 1572872 | tf_op jit(solution)/shard_map/ppermute | solution.py:22
  84.6 25.9 %all-to-all-start.3 = ((bf16[32,4,32,128]{3,2,1,0:T(8,128)(2,1)}), bf16[32,4,32,128]{3,2,1,0:T(8,128)(2,1)}, u32[]{:S(2)}, u32[]{:S(2)}) async-start(bf16[32,4,32,128]{3,2,1,0:T(8,128)(2,1)} %bitcast.42), calls=%async_computation.3 | async-start | bytes 2097152 | tf_op jit(solution)/shard_map/all_to_all | solution.py:18
  93.3 14.8 %collective-permute-start.2 = (bf16[32,2,32,128]{3,2,1,0:T(8,128)(2,1)}, bf16[32,2,32,128]{3,2,1,0:T(8,128)(2,1)}, u32[]{:S(2)}, u32[]{:S(2)}) collective-permute-start(bf16[32,2,32,128]{3,2,1,0:T(8,128)(2,1)} %collective-permute-done.refs_1_), channel_id=1, source_target_pairs={{0,2},{2,4},{4,6},{6,8},{8,10},{10,12},{12,14},{14,0},{1,3},{3,5},... | collective-permute-start | bytes 1572872 | tf_op jit(solution)/shard_map/ppermute | solution.py:22
  93.4 14.7 %collective-permute-start.3 = (bf16[32,2,32,128]{3,2,1,0:T(8,128)(2,1)S(1)}, bf16[32,2,32,128]{3,2,1,0:T(8,128)(2,1)}, u32[]{:S(2)}, u32[]{:S(2)}) collective-permute-start(bf16[32,2,32,128]{3,2,1,0:T(8,128)(2,1)S(1)} %collective-permute-done.1.refs_2_), channel_id=1, source_target_pairs={{0,14},{2,0},{4,2},{6,4},{8,6},{10,8},{12,10},{14,12},{1,15},{3,1}... | collective-permute-start | bytes 1572872 | tf_op jit(solution)/shard_map/ppermute | solution.py:22
  110.5 14.5 %collective-permute-start.4 = (bf16[32,2,32,128]{3,2,1,0:T(8,128)(2,1)}, bf16[32,2,32,128]{3,2,1,0:T(8,128)(2,1)S(1)}, u32[]{:S(2)}, u32[]{:S(2)}) collective-permute-start(bf16[32,2,32,128]{3,2,1,0:T(8,128)(2,1)} %collective-permute-done.2.refs_3_), channel_id=1, source_target_pairs={{0,2},{2,4},{4,6},{6,8},{8,10},{10,12},{12,14},{14,0},{1,3},{3,5},... | collective-permute-start | bytes 1572872 | tf_op jit(solution)/shard_map/ppermute | solution.py:22
  110.6 14.5 %collective-permute-start.5 = (bf16[32,2,32,128]{3,2,1,0:T(8,128)(2,1)}, bf16[32,2,32,128]{3,2,1,0:T(8,128)(2,1)S(1)}, u32[]{:S(2)}, u32[]{:S(2)}) collective-permute-start(bf16[32,2,32,128]{3,2,1,0:T(8,128)(2,1)} %collective-permute-done.3.refs_4_), channel_id=1, source_target_pairs={{0,14},{2,0},{4,2},{6,4},{8,6},{10,8},{12,10},{14,12},{1,15},{3,1}... | collective-permute-start | bytes 1572872 | tf_op jit(solution)/shard_map/ppermute | solution.py:22
  130.7 23.1 %all-to-all-start.4 = ((bf16[32,4,32,128]{3,2,1,0:T(8,128)(2,1)}), bf16[32,4,32,128]{3,2,1,0:T(8,128)(2,1)}, u32[]{:S(2)}, u32[]{:S(2)}) async-start(bf16[32,4,32,128]{3,2,1,0:T(8,128)(2,1)} %bitcast.13), calls=%async_computation.4 | async-start | bytes 2097152 | tf_op jit(solution)/shard_map/all_to_all | solution.py:18
  136.6 8.1 %collective-permute-start.7 = (bf16[32,1,32,128]{3,2,1,0:T(8,128)(2,1)S(1)}, bf16[32,1,32,128]{3,2,1,0:T(8,128)(2,1)S(1)}, u32[]{:S(2)}, u32[]{:S(2)}) collective-permute-start(bf16[32,1,32,128]{3,2,1,0:T(8,128)(2,1)S(1)} %slice.24), channel_id=1, source_target_pairs={{0,14},{2,0},{4,2},{6,4},{8,6},{10,8},{12,10},{14,12},{1,15},{3,1}... | collective-permute-start | bytes 786440 | tf_op jit(solution)/shard_map/ppermute | solution.py:22
  139.4 8.6 %collective-permute-start.6 = (bf16[32,1,32,128]{3,2,1,0:T(8,128)(2,1)S(1)}, bf16[32,1,32,128]{3,2,1,0:T(8,128)(2,1)S(1)}, u32[]{:S(2)}, u32[]{:S(2)}) collective-permute-start(bf16[32,1,32,128]{3,2,1,0:T(8,128)(2,1)S(1)} %slice.23), channel_id=1, source_target_pairs={{0,2},{2,4},{4,6},{6,8},{8,10},{10,12},{12,14},{14,0},{1,3},{3,5},... | collective-permute-start | bytes 786440 | tf_op jit(solution)/shard_map/ppermute | solution.py:22
  153.1 29.2 %copy-start.1 = (bf16[128,32,128]{2,1,0:T(8,128)(2,1)S(1)}, bf16[128,32,128]{2,1,0:T(8,128)(2,1)}, u32[]{:S(2)}) copy-start(bf16[128,32,128]{2,1,0:T(8,128)(2,1)} %pair_ref.3) | copy-start | bytes 3145732
  153.8 25.0 %all-to-all-start.5 = ((bf16[32,4,32,128]{3,2,1,0:T(8,128)(2,1)}), bf16[32,4,32,128]{3,2,1,0:T(8,128)(2,1)S(1)}, u32[]{:S(2)}, u32[]{:S(2)}) async-start(bf16[32,4,32,128]{3,2,1,0:T(8,128)(2,1)} %bitcast.17), calls=%async_computation.5 | async-start | bytes 2097152 | tf_op jit(solution)/shard_map/all_to_all | solution.py:18
  178.8 1.0 copy-start.5
Sparse Core Ops, SparseCore 0:
  31.0 65.1 all-gather.2

commit v4 on v2

v4 whole, which is shorter than its diff:
```python
import functools

import jax
import jax.numpy as jnp
from jax import lax
from jax.experimental import pallas as pl
from jax.experimental.pallas import tpu as pltpu
from jax.sharding import Mesh, PartitionSpec as P

PLANE = ("y", "xh", "xl", "c")
CHIPS = ("y", "xh", "xl")
GROUPS = 32
SLABS = 8
STEP_ROWS = 64
VMEM_LIMIT = 32 * 1024 * 1024


def all_to_all(x, axes):
    return lax.all_to_all(x, axes, split_axis=0, concat_axis=0, tiled=True)


def shift(x, by):
    return lax.ppermute(x, "z", [(i, (i + by) % SLABS) for i in range(SLABS)])


def normalize(pair_ref, gain_ref, bias_ref):
    x = pair_ref[...].astype(jnp.float32)
    x = x.reshape(x.shape[0] * x.shape[1], x.shape[2])
    centred = x - jnp.mean(x, axis=1, keepdims=True)
    inverse = lax.rsqrt(jnp.mean(centred * centred, axis=1, keepdims=True) + 1e-05)
    xhat = centred * inverse
    normed = (xhat * gain_ref[...] + bias_ref[...]).astype(jnp.bfloat16)
    return xhat, inverse, normed


def lane_order(transposed):
    source = lax.broadcasted_iota(jnp.int32, (256, 256), 1 if transposed else 0)
    lane = lax.broadcasted_iota(jnp.int32, (256, 256), 0 if transposed else 1)
    side, half = (lane >> 1) & 1, (lane >> 2) & 1
    wanted = side * 128 + (lane >> 3) * 4 + half * 2 + (lane & 1)
    return jnp.where(source == wanted, 1.0, 0.0).astype(jnp.float32)


def pre_kernel(pair_ref, gain_ref, bias_ref, weight_ref, sides_ref, ordered_ref):
    @pl.when(pl.program_id(0) == 0)
    def _():
        order = lane_order(False).astype(jnp.bfloat16)
        for kind in range(2):
            plain = jnp.concatenate(
                [weight_ref[:, at : at + 128] for at in (128 * kind, 256 + 128 * kind)], axis=1
            )
            ordered_ref[:, 256 * kind : 256 * kind + 256] = jnp.dot(
                plain, order, preferred_element_type=jnp.float32
            ).astype(jnp.bfloat16)

    _, _, normed = normalize(pair_ref, gain_ref, bias_ref)
    proj = jnp.dot(normed, ordered_ref[...], preferred_element_type=jnp.float32)
    sides = jax.nn.sigmoid(proj[:, 256:]) * proj[:, :256]
    sides_ref[...] = sides.astype(jnp.bfloat16).reshape(sides_ref.shape)


def pre(pair, gain, bias, weight):
    rows, cols, width = pair.shape
    tile = pl.BlockSpec((STEP_ROWS, cols, width), lambda i: (i, 0, 0))
    whole = lambda *shape: pl.BlockSpec(shape, lambda i: (0,) * len(shape))
    return pl.pallas_call(
        pre_kernel,
        grid=(rows // STEP_ROWS,),
        in_specs=[tile, whole(1, width), whole(1, width), whole(*weight.shape)],
        out_specs=[
            pl.BlockSpec((STEP_ROWS, cols, 2 * width), lambda i: (i, 0, 0)),
            whole(*weight.shape),
        ],
        out_shape=[
            jax.ShapeDtypeStruct((rows, cols, 2 * width), jnp.bfloat16),
            jax.ShapeDtypeStruct(weight.shape, jnp.bfloat16),
        ],
        compiler_params=pltpu.CompilerParams(vmem_limit_bytes=VMEM_LIMIT),
        cost_estimate=pl.CostEstimate(
            flops=2 * rows * cols * width * 512, bytes_accessed=12 << 20, transcendentals=1 << 20
        ),
        name="gated_projections",
    )(pair, gain, bias, weight)


def post_kernel(
    pair_ref, back_ref, gain_ref, bias_ref, ordered_ref, grad_ref, total_ref, wgrad_ref
):
    step = pl.program_id(0)

    @pl.when(step == 0)
    def _():
        total_ref[...] = jnp.zeros_like(total_ref)
        wgrad_ref[...] = jnp.zeros_like(wgrad_ref)

    xhat, inverse, normed = normalize(pair_ref, gain_ref, bias_ref)
    proj = jnp.dot(normed, ordered_ref[...], preferred_element_type=jnp.float32)
    width = xhat.shape[1]
    value, gate = proj[:, :256], jax.nn.sigmoid(proj[:, 256:])
    gated = back_ref[...].astype(jnp.float32).reshape(gate.shape) * gate
    dproj = jnp.concatenate(
        [gated.astype(jnp.bfloat16), (gated * value * (1.0 - gate)).astype(jnp.bfloat16)], axis=1
    )
    dnormed = lax.dot_general(
        dproj, ordered_ref[...], (((1,), (1,)), ((), ())), preferred_element_type=jnp.float32
    )
    wgrad_ref[...] += lax.dot_general(
        normed, dproj, (((0,), (0,)), ((), ())), preferred_element_type=jnp.float32
    )
    total_ref[4 * width : 4 * width + 1, :] += jnp.sum(dnormed * xhat, axis=0, keepdims=True)
    total_ref[4 * width + 8 : 4 * width + 9, :] += jnp.sum(dnormed, axis=0, keepdims=True)
    g = dnormed * gain_ref[...]
    grad = (
        g
        - jnp.mean(g, axis=1, keepdims=True)
        - xhat * jnp.mean(g * xhat, axis=1, keepdims=True)
    ) * inverse
    grad_ref[...] = grad.astype(jnp.bfloat16).reshape(grad_ref.shape)

    @pl.when(step == pl.num_programs(0) - 1)
    def _():
        order = lane_order(True)
        for kind in range(2):
            plain = jnp.dot(
                wgrad_ref[:, 256 * kind : 256 * kind + 256],
                order,
                precision=lax.Precision.HIGHEST,
                preferred_element_type=jnp.float32,
            )
            for side in range(2):
                at = (2 * side + kind) * width
                total_ref[at : at + width, :] = plain[:, 128 * side : 128 * side + 128]


def post(pair, back, gain, bias, ordered, total_rows):
    rows, cols, width = pair.shape
    tile = pl.BlockSpec((STEP_ROWS, cols, width), lambda i: (i, 0, 0))
    whole = lambda *shape: pl.BlockSpec(shape, lambda i: (0,) * len(shape))
    return pl.pallas_call(
        post_kernel,
        grid=(rows // STEP_ROWS,),
        in_specs=[
            tile,
            pl.BlockSpec((STEP_ROWS, cols, 2 * width), lambda i: (i, 0, 0)),
            whole(1, width),
            whole(1, width),
            whole(*ordered.shape),
        ],
        out_specs=[tile, whole(total_rows, width)],
        out_shape=[
            jax.ShapeDtypeStruct(pair.shape, jnp.bfloat16),
            jax.ShapeDtypeStruct((total_rows, width), jnp.float32),
        ],
        scratch_shapes=[pltpu.VMEM(ordered.shape, jnp.float32)],
        compiler_params=pltpu.CompilerParams(vmem_limit_bytes=VMEM_LIMIT),
        cost_estimate=pl.CostEstimate(
            flops=6 * rows * cols * width * 512, bytes_accessed=20 << 20, transcendentals=1 << 20
        ),
        name="input_gradients",
    )(pair, back, gain, bias, ordered)


def assemble(ref, at):
    return jnp.concatenate(
        [
            jnp.concatenate([ref[4 * r + c, at] for c in range(4)], axis=0)
            for r in range(8)
        ],
        axis=1,
    )


def product_kernel(second_half, slab_ref, sides_ref, *refs):
    *block_refs, up_ref, down_ref = refs[: 9]
    out_ref, grads = refs[9 + second_half :]

    def place(offset, ref):
        where = lax.rem(slab_ref[0] + offset, SLABS)
        for x in range(2):
            rows = pl.ds(pl.multiple_of(512 * x + 64 * where, 64), 64)
            for r in range(8):
                grads[rows, 128 * r : 128 * r + 128] = jnp.concatenate(
                    [ref[4 * r + 2 * x, 0], ref[4 * r + 2 * x + 1, 0]], axis=0
                )

    for offset, ref in zip((0, 7, 1, 6, 2, 5, 3), block_refs):
        place(offset, ref)
    for channel, ref in enumerate((up_ref, down_ref)):
        pl.when(pl.program_id(0) == channel)(functools.partial(place, 4, ref))
    left = assemble(sides_ref.at[:, 0], 0)
    right = assemble(sides_ref.at[:, 1], 0)
    first = jnp.dot(right, grads[...], preferred_element_type=jnp.float32)
    second = lax.dot_general(
        left, grads[...], (((1,), (1,)), ((), ())), preferred_element_type=jnp.float32
    )
    for side, value in enumerate((first, second)):
        value = value.astype(jnp.bfloat16)
        for r in range(8):
            for c in range(4):
                out_ref[4 * r + c, side, 0] = value[
                    32 * c : 32 * c + 32, 128 * r : 128 * r + 128
                ]


def products(slab, sides, half, blocks, earlier=None):
    groups, pairs, depth, width = sides.shape
    channels = pairs // 4
    sides = sides.reshape(groups, 4, channels, depth, width)
    sides_spec = pl.BlockSpec((groups, 2, 1, depth, width), lambda h: (0, half, h, 0, 0))
    piece = pl.BlockSpec((groups, 1, depth, width), lambda h: (0, h, 0, 0))
    alone = pl.BlockSpec((groups, 1, depth, width), lambda h: (0, 0, 0, 0))
    operands = [slab, sides, *blocks]
    specs = [pl.BlockSpec(memory_space=pltpu.SMEM), sides_spec] + [piece] * 7 + [alone] * 2
    if earlier is not None:
        operands.append(earlier)
        specs.append(pl.BlockSpec(memory_space=pl.ANY))
    return pl.pallas_call(
        functools.partial(product_kernel, earlier is not None),
        grid=(channels,),
        in_specs=specs,
        out_specs=sides_spec,
        out_shape=jax.ShapeDtypeStruct(sides.shape, jnp.bfloat16),
        scratch_shapes=[pltpu.VMEM((1024, 1024), jnp.bfloat16)],
        input_output_aliases={} if earlier is None else {len(operands) - 1: 0},
        compiler_params=pltpu.CompilerParams(vmem_limit_bytes=VMEM_LIMIT),
        cost_estimate=pl.CostEstimate(
            flops=4 * channels * 128 * 1024 * 1024, bytes_accessed=12 << 20, transcendentals=0
        ),
        name="triangle_products",
    )(*operands)


def sum_of_all(x):
    me = lax.axis_index("c")
    swap = lambda x: lax.ppermute(x, "c", [(0, 1), (1, 0)])
    mine = lax.dynamic_index_in_dim(x, me, 0, keepdims=False)
    others = lax.dynamic_index_in_dim(x, 1 - me, 0, keepdims=False)
    part = jnp.sum(all_to_all(mine + swap(others), CHIPS), axis=0)
    part = jnp.sum(all_to_all(jnp.broadcast_to(part, (SLABS,) + part.shape), "z"), axis=0)
    mine = all_to_all(jnp.broadcast_to(part, x.shape[1:]), CHIPS)
    others = swap(mine)
    first = me == 0
    return jnp.stack([jnp.where(first, mine, others), jnp.where(first, others, mine)])


def per_device(pair, layernorm_gain, layernorm_bias, proj_weight, product_grad):
    rows, cols, width = pair.shape
    barrier = lax.optimization_barrier
    split = lambda x: jnp.transpose(x, (2, 1, 0)).reshape(GROUPS, -1, cols, rows)
    join = lambda x: jnp.transpose(x.reshape(-1, cols, rows), (2, 1, 0))
    gain = layernorm_gain.reshape(1, width)
    bias = layernorm_bias.reshape(1, width)
    slab = lax.axis_index("z").astype(jnp.int32).reshape(1)
    both = lambda pair_of: (shift(pair_of[0], 1), shift(pair_of[1], -1))

    after = lambda wanted, done: barrier((wanted, done))[0]
    own = all_to_all(split(product_grad), PLANE)
    sides, ordered = pre(pair, gain, bias, proj_weight)
    own, sides = barrier((own, split(sides)))
    sides = all_to_all(sides, PLANE)
    a0, b0 = barrier((own[:, :2], own[:, 2:]))
    a1 = both((a0, a0))
    b1 = both((b0, b0))
    a1 = barrier(a1)
    a2 = both(a1)
    b1 = after(b1, a1)
    b2 = both(b1)
    a2 = after(a2, b1)
    a3 = both(a2)
    b2 = after(b2, a2)
    b3 = both(b2)
    a3 = after(a3, b2)
    a4 = shift(a3[0][:, :1], 1), shift(a3[1][:, 1:], -1)
    b3 = after(b3, a3)
    b4 = shift(b3[0][:, :1], 1), shift(b3[1][:, 1:], -1)
    back = products(slab, sides, 0, [a0, *a1, *a2, *a3, *a4])
    back = products(slab, sides, 1, [b0, *b1, *b2, *b3, *b4], back)
    back = all_to_all(back.reshape(sides.shape), PLANE)

    total_rows = 24 * GROUPS
    pairwise_gradient, total = post(
        pair, join(back), gain, bias, ordered, total_rows
    )
    total = sum_of_all(total.reshape(2, 16, 24, width)) / (rows * 8)
    total = total.reshape(total_rows, width)
    proj_grad = jnp.transpose(total[: 4 * width].reshape(4, width, width), (1, 0, 2))
    proj_grad = proj_grad.reshape(width, 4 * width)
    layernorm_gradient = jnp.stack([total[4 * width], total[4 * width + 8]])
    return pairwise_gradient, proj_grad, layernorm_gradient


def solution(mesh):
    fine = Mesh(mesh.devices.reshape(4, 2, 2, 8, 2), ("y", "xh", "xl", "z", "c"))
    tiles = P(("y", "xh"), ("xl", "z", "c"), None)
    return jax.shard_map(
        per_device,
        mesh=fine,
        in_specs=(tiles, P(), P(), P(), tiles),
        out_specs=(tiles, P(), P()),
        check_vma=False,
    )
```

time: 244 us -> 224 us (0.918)
  blocking collectives: 60.7 us -> 33 us
  local copies, waits for them, and re-layouts: 21.1 us -> 34.2 us
  Pallas kernels: 23.8 us -> 18 us
  waiting for transfers between devices: 79.7 us -> 83.8 us
  starting transfers between devices: 55.9 us -> 52.3 us
    all_to_all x4 -> x3, blocking collectives: 60.7 us -> 33 us  [all_to_all(): return lax.all_to_all(x, axes, split_axis=0, concat_axis=0, tiled=True)]
    all_to_all x5 -> x3, waiting for transfers between devices: 17.2 us -> 37.7 us  [all_to_all(): return lax.all_to_all(x, axes, split_axis=0, concat_axis=0, tiled=True)]
    ppermute x14 -> x16, waiting for transfers between devices: 62.5 us -> 44 us  [shift(): return lax.ppermute(x, 'z', [(i, (i + by) % SLABS) for i in range(SLABS)])]
    all_to_all x5 -> x3, starting transfers between devices: 34.5 us -> 21.2 us  [all_to_all(): return lax.all_to_all(x, axes, split_axis=0, concat_axis=0, tiled=True)]
    unnamed x18 -> x66, local copies, waits for them, and re-layouts: 4.8 us -> 17.9 us
    ppermute x0 -> x2, starting transfers between devices: none -> 6.64 us  [sum_of_all(): swap = lambda x: lax.ppermute(x, 'c', [(0, 1), (1, 0)])]
    slice x0 -> x5, local copies, waits for them, and re-layouts: none -> 4.24 us  [the longest x2 1.48 us: per_device(): a4 = (shift(a3[0][:, :1], 1), shift(a3[1][:, 1:], -1))]
    pallas_call x3, Pallas kernels: 18.7 us -> 14.7 us  [the longest x2 8.71 us: products(): pl.pallas_call(functools.partial(product_kernel, earlier is not None), gr...]
  transfers between devices with their start and end apart: 19 -> 21, of which waited for: 9 -> 11; matrix products, arithmetic and copies ran while one was open for 4% -> 4% of each run, Pallas kernels for 6% -> 3%
where the time goes in v4:
time: 224 us; the launch traced here: 223 us
  waiting for transfers between devices  83.8 us (37%)
  starting transfers between devices  52.3 us (23%)
  local copies, waits for them, and re-layouts  34.2 us (15%)
  blocking collectives  33 us (15%)
  Pallas kernels  18 us (8%)
    ppermute x16, waiting for transfers between devices, shift(): return lax.ppermute(x, 'z', [(i, (i + by) % SLABS) for i in range(SLABS)])  44 us
    all_to_all x3, waiting for transfers between devices, all_to_all(): return lax.all_to_all(x, axes, split_axis=0, concat_axis=0, tiled=True)  37.7 us
    all_to_all x3, blocking collectives, all_to_all(): return lax.all_to_all(x, axes, split_axis=0, concat_axis=0, tiled=True)  33 us
    ppermute x16, starting transfers between devices, shift(): return lax.ppermute(x, 'z', [(i, (i + by) % SLABS) for i in range(SLABS)])  24.5 us
    all_to_all x3, starting transfers between devices, all_to_all(): return lax.all_to_all(x, axes, split_axis=0, concat_axis=0, tiled=True)  21.2 us
    unnamed x66, local copies, waits for them, and re-layouts  17.9 us
    pallas_call x2, Pallas kernels, products(): pl.pallas_call(functools.partial(product_kernel, earlier is not None), gr...  8.71 us
    transpose x2, local copies, waits for them, and re-layouts, per_device(): jnp.transpose(x, (2, 1, 0)).reshape(GROUPS, -1, cols, rows)  7.27 us
  transfers between devices with their start and end apart: 21, of which 11 were waited for; matrix products, arithmetic and copies ran while one was open for 4% of the time, Pallas kernels for 3%

profile of v4, /device:TPU:1, one launch (start us, length us, event | category | flops | bytes accessed | tf_op | source)
XLA Modules:
  0.0 223.0 jit_solution(15243360356254252081)
XLA Ops:
  0.7 3.3 %copy.17 = bf16[128,32,128]{2,1,0:T(8,128)(2,1)} copy(bf16[128,32,128]{0,1,2:T(8,128)(2,1)} %bitcast.43) | data formatting | bytes 2097152 | tf_op jit(solution)/shard_map/transpose | solution.py:249
  3.9 8.6 %all-to-all-start = ((bf16[32,4,32,128]{3,2,1,0:T(8,128)(2,1)}), bf16[32,4,32,128]{3,2,1,0:T(8,128)(2,1)}, u32[]{:S(2)}, u32[]{:S(2)}) async-start(bf16[32,4,32,128]{3,2,1,0:T(8,128)(2,1)} %bitcast.2), calls=%async_computation | async-start | bytes 2097152 | tf_op jit(solution)/shard_map/all_to_all | solution.py:19
  12.6 3.3 %gated_projections.1 = (bf16[128,32,256]{2,1,0:T(8,128)(2,1)S(1)}, bf16[128,512]{1,0:T(8,128)(2,1)S(1)}) custom-call(bf16[128,32,128]{2,1,0:T(8,128)(2,1)S(1)} %copy-done.25, f32[1,128]{1,0:T(1,128)S(1)} %bitcast.35, f32[1,128]{1,0:T(1,128)S(1)} %bitcast.37, bf16[128,512]{1,0:T(8,128)(2,1)S(1)} %copy-done.27), custom_call_target="tpu_custom_call" | custom-call | flops 536870912 | bytes 12582912 | tf_op jit(solution)/shard_map/gated_projections/pallas_call | solution.py:66
  16.0 4.0 %copy.18 = bf16[256,32,128]{2,1,0:T(8,128)(2,1)} copy(bf16[256,32,128]{0,1,2:T(8,128)(2,1)S(1)} %bitcast.32) | data formatting | bytes 4194304 | tf_op jit(solution)/shard_map/transpose | solution.py:249
  20.0 9.9 %all-to-all-done = bf16[32,4,32,128]{3,2,1,0:T(8,128)(2,1)} async-done(((bf16[32,4,32,128]{3,2,1,0:T(8,128)(2,1)}), bf16[32,4,32,128]{3,2,1,0:T(8,128)(2,1)}, u32[]{:S(2)}, u32[]{:S(2)}) %all-to-all-start) | async-done | bytes 1048608 | tf_op jit(solution)/shard_map/all_to_all | solution.py:19
  29.8 4.1 %all-to-all-start.1 = ((bf16[32,8,32,128]{3,2,1,0:T(8,128)(2,1)}), bf16[32,8,32,128]{3,2,1,0:T(8,128)(2,1)S(1)}, u32[]{:S(2)}, u32[]{:S(2)}) async-start(bf16[32,8,32,128]{3,2,1,0:T(8,128)(2,1)} %bitcast.39), calls=%async_computation.1 | async-start | bytes 4194304 | tf_op jit(solution)/shard_map/all_to_all | solution.py:19
  35.2 1.7 collective-permute-start.2
  36.9 4.0 %collective-permute-start.3 = (bf16[32,2,32,128]{3,2,1,0:T(8,128)(2,1)S(1)}, bf16[32,2,32,128]{3,2,1,0:T(8,128)(2,1)S(1)}, u32[]{:S(2)}, u32[]{:S(2)}) collective-permute-start(bf16[32,2,32,128]{3,2,1,0:T(8,128)(2,1)S(1)} %get-tuple-element.27.refs_0_), channel_id=1, source_target_pairs={{0,14},{2,0},{4,2},{6,4},{8,6},{10,8},{12,10},{14,12},{1,15},{3,1}... | collective-permute-start | bytes 1572872 | tf_op jit(solution)/shard_map/ppermute | solution.py:23
  40.9 2.7 %collective-permute-start.1 = (bf16[32,2,32,128]{3,2,1,0:T(8,128)(2,1)S(1)}, bf16[32,2,32,128]{3,2,1,0:T(8,128)(2,1)S(1)}, u32[]{:S(2)}, u32[]{:S(2)}) collective-permute-start(bf16[32,2,32,128]{3,2,1,0:T(8,128)(2,1)S(1)} %get-tuple-element.26.refs_0_), channel_id=1, source_target_pairs={{0,14},{2,0},{4,2},{6,4},{8,6},{10,8},{12,10},{14,12},{1,15},{3,1}... | collective-permute-start | bytes 1572872 | tf_op jit(solution)/shard_map/ppermute | solution.py:23
  43.6 9.2 %collective-permute-done.2.refs_1_ = bf16[32,2,32,128]{3,2,1,0:T(8,128)(2,1)S(1)} collective-permute-done((bf16[32,2,32,128]{3,2,1,0:T(8,128)(2,1)S(1)}, bf16[32,2,32,128]{3,2,1,0:T(8,128)(2,1)S(1)}, u32[]{:S(2)}, u32[]{:S(2)}) %collective-permute-start.2) | collective-permute-done | bytes 524320 | tf_op jit(solution)/shard_map/ppermute | solution.py:23
  53.6 2.7 %collective-permute-start.7 = (bf16[32,2,32,128]{3,2,1,0:T(8,128)(2,1)S(1)}, bf16[32,2,32,128]{3,2,1,0:T(8,128)(2,1)S(1)}, u32[]{:S(2)}, u32[]{:S(2)}) collective-permute-start(bf16[32,2,32,128]{3,2,1,0:T(8,128)(2,1)S(1)} %collective-permute-done.3.refs_2_), channel_id=1, source_target_pairs={{0,14},{2,0},{4,2},{6,4},{8,6},{10,8},{12,10},{14,12},{1,15},{3,1}... | collective-permute-start | bytes 1572872 | tf_op jit(solution)/shard_map/ppermute | solution.py:23
  57.1 6.9 %collective-permute-done.refs_1_ = bf16[32,2,32,128]{3,2,1,0:T(8,128)(2,1)S(1)} collective-permute-done((bf16[32,2,32,128]{3,2,1,0:T(8,128)(2,1)S(1)}, bf16[32,2,32,128]{3,2,1,0:T(8,128)(2,1)S(1)}, u32[]{:S(2)}, u32[]{:S(2)}) %collective-permute-start) | collective-permute-done | bytes 524320 | tf_op jit(solution)/shard_map/ppermute | solution.py:23
  64.9 2.7 %collective-permute-start.5 = (bf16[32,2,32,128]{3,2,1,0:T(8,128)(2,1)S(1)}, bf16[32,2,32,128]{3,2,1,0:T(8,128)(2,1)S(1)}, u32[]{:S(2)}, u32[]{:S(2)}) collective-permute-start(bf16[32,2,32,128]{3,2,1,0:T(8,128)(2,1)S(1)} %collective-permute-done.1.refs_2_), channel_id=1, source_target_pairs={{0,14},{2,0},{4,2},{6,4},{8,6},{10,8},{12,10},{14,12},{1,15},{3,1}... | collective-permute-start | bytes 1572872 | tf_op jit(solution)/shard_map/ppermute | solution.py:23
  68.3 7.0 %collective-permute-done.6.refs_3_ = bf16[32,2,32,128]{3,2,1,0:T(8,128)(2,1)S(1)} collective-permute-done((bf16[32,2,32,128]{3,2,1,0:T(8,128)(2,1)S(1)}, bf16[32,2,32,128]{3,2,1,0:T(8,128)(2,1)S(1)}, u32[]{:S(2)}, u32[]{:S(2)}) %collective-permute-start.6) | collective-permute-done | bytes 524320 | tf_op jit(solution)/shard_map/ppermute | solution.py:23
  76.1 2.7 %collective-permute-start.11 = (bf16[32,2,32,128]{3,2,1,0:T(8,128)(2,1)S(1)}, bf16[32,2,32,128]{3,2,1,0:T(8,128)(2,1)S(1)}, u32[]{:S(2)}, u32[]{:S(2)}) collective-permute-start(bf16[32,2,32,128]{3,2,1,0:T(8,128)(2,1)S(1)} %collective-permute-done.7.refs_4_), channel_id=1, source_target_pairs={{0,14},{2,0},{4,2},{6,4},{8,6},{10,8},{12,10},{14,12},{1,15},{3,1}... | collective-permute-start | bytes 1572872 | tf_op jit(solution)/shard_map/ppermute | solution.py:23
  79.6 6.9 %collective-permute-done.4.refs_3_ = bf16[32,2,32,128]{3,2,1,0:T(8,128)(2,1)S(1)} collective-permute-done((bf16[32,2,32,128]{3,2,1,0:T(8,128)(2,1)S(1)}, bf16[32,2,32,128]{3,2,1,0:T(8,128)(2,1)S(1)}, u32[]{:S(2)}, u32[]{:S(2)}) %collective-permute-start.4) | collective-permute-done | bytes 524320 | tf_op jit(solution)/shard_map/ppermute | solution.py:23
  87.4 2.7 %collective-permute-start.9 = (bf16[32,2,32,128]{3,2,1,0:T(8,128)(2,1)S(1)}, bf16[32,2,32,128]{3,2,1,0:T(8,128)(2,1)S(1)}, u32[]{:S(2)}, u32[]{:S(2)}) collective-permute-start(bf16[32,2,32,128]{3,2,1,0:T(8,128)(2,1)S(1)} %collective-permute-done.5.refs_4_), channel_id=1, source_target_pairs={{0,14},{2,0},{4,2},{6,4},{8,6},{10,8},{12,10},{14,12},{1,15},{3,1}... | collective-permute-start | bytes 1572872 | tf_op jit(solution)/shard_map/ppermute | solution.py:23
  90.8 7.0 %collective-permute-done.10.refs_5_ = bf16[32,2,32,128]{3,2,1,0:T(8,128)(2,1)S(1)} collective-permute-done((bf16[32,2,32,128]{3,2,1,0:T(8,128)(2,1)S(1)}, bf16[32,2,32,128]{3,2,1,0:T(8,128)(2,1)S(1)}, u32[]{:S(2)}, u32[]{:S(2)}) %collective-permute-start.10) | collective-permute-done | bytes 524320 | tf_op jit(solution)/shard_map/ppermute | solution.py:23
  100.1 2.7 %collective-permute-start.15 = (bf16[32,1,32,128]{3,2,1,0:T(8,128)(2,1)}, bf16[32,1,32,128]{3,2,1,0:T(8,128)(2,1)}, u32[]{:S(2)}, u32[]{:S(2)}) collective-permute-start(bf16[32,1,32,128]{3,2,1,0:T(8,128)(2,1)} %slice.32), channel_id=1, source_target_pairs={{0,14},{2,0},{4,2},{6,4},{8,6},{10,8},{12,10},{14,12},{1,15},{3,1}... | collective-permute-start | bytes 786440 | tf_op jit(solution)/shard_map/ppermute | solution.py:23
  102.8 6.2 %collective-permute-done.8.refs_5_ = bf16[32,2,32,128]{3,2,1,0:T(8,128)(2,1)S(1)} collective-permute-done((bf16[32,2,32,128]{3,2,1,0:T(8,128)(2,1)S(1)}, bf16[32,2,32,128]{3,2,1,0:T(8,128)(2,1)S(1)}, u32[]{:S(2)}, u32[]{:S(2)}) %collective-permute-start.8) | collective-permute-done | bytes 524320 | tf_op jit(solution)/shard_map/ppermute | solution.py:23
  111.3 2.7 %collective-permute-start.13 = (bf16[32,1,32,128]{3,2,1,0:T(8,128)(2,1)}, bf16[32,1,32,128]{3,2,1,0:T(8,128)(2,1)}, u32[]{:S(2)}, u32[]{:S(2)}) collective-permute-start(bf16[32,1,32,128]{3,2,1,0:T(8,128)(2,1)} %slice.30), channel_id=1, source_target_pairs={{0,14},{2,0},{4,2},{6,4},{8,6},{10,8},{12,10},{14,12},{1,15},{3,1}... | collective-permute-start | bytes 786440 | tf_op jit(solution)/shard_map/ppermute | solution.py:23
  120.9 4.4 %triangle_products.2.refs_9_ = bf16[32,4,2,32,128]{4,3,2,1,0:T(8,128)(2,1)S(1)} custom-call(s32[1]{0:T(128)} %bitcast.slab_ref, bf16[32,4,2,32,128]{4,3,2,1,0:T(8,128)(2,1)S(1)} %bitcast.28, bf16[32,2,32,128]{3,2,1,0:T(8,128)(2,1)S(1)} %get-tuple-element.27.refs_0_, bf16[32,2,32,128]{3,2,1,0:T(8,128)(2,1)S(1)} %copy-done.10, ...), custom_call_target="tpu_custom_call" | custom-call | flops 1073741824 | bytes 12582912 | tf_op jit(solution)/shard_map/triangle_products/pallas_call | solution.py:217
  125.4 4.3 %triangle_products.3 = bf16[32,4,2,32,128]{4,3,2,1,0:T(8,128)(2,1)S(1)} custom-call(s32[1]{0:T(128)} %bitcast.slab_ref, bf16[32,4,2,32,128]{4,3,2,1,0:T(8,128)(2,1)S(1)} %bitcast.29, bf16[32,2,32,128]{3,2,1,0:T(8,128)(2,1)S(1)} %get-tuple-element.26.refs_0_, bf16[32,2,32,128]{3,2,1,0:T(8,128)(2,1)S(1)} %copy-done.18, ...), custom_call_target="tpu_custom_call", output_to_operand_aliasing={{}: (11, {})} | custom-call | flops 1073741824 | bytes 12582912 | tf_op jit(solution)/shard_map/triangle_products/pallas_call | solution.py:217
  131.1 8.5 %all-to-all-start.2 = ((bf16[32,8,32,128]{3,2,1,0:T(8,128)(2,1)}), bf16[32,8,32,128]{3,2,1,0:T(8,128)(2,1)S(1)}, u32[]{:S(2)}, u32[]{:S(2)}) async-start(bf16[32,8,32,128]{3,2,1,0:T(8,128)(2,1)} %bitcast.30), calls=%async_computation.2 | async-start | bytes 4194304 | tf_op jit(solution)/shard_map/all_to_all | solution.py:19
  139.6 27.8 %all-to-all-done.2 = bf16[32,8,32,128]{3,2,1,0:T(8,128)(2,1)S(1)} async-done(((bf16[32,8,32,128]{3,2,1,0:T(8,128)(2,1)}), bf16[32,8,32,128]{3,2,1,0:T(8,128)(2,1)S(1)}, u32[]{:S(2)}, u32[]{:S(2)}) %all-to-all-start.2) | async-done | bytes 2097184 | tf_op jit(solution)/shard_map/all_to_all | solution.py:19
  168.8 4.0 %copy.19 = bf16[256,32,128]{0,1,2:T(8,128)(2,1)S(1)} copy(bf16[256,32,128]{2,1,0:T(8,128)(2,1)} %bitcast.40) | data formatting | bytes 4194304 | tf_op jit(solution)/shard_map/reshape | solution.py:250
  173.7 6.0 %input_gradients.1 = (bf16[128,32,128]{2,1,0:T(8,128)(2,1)}, f32[768,128]{1,0:T(8,128)S(1)}) custom-call(bf16[128,32,128]{2,1,0:T(8,128)(2,1)S(1)} %copy-done.26, bf16[128,32,256]{2,1,0:T(8,128)(2,1)S(1)} %bitcast.31, f32[1,128]{1,0:T(1,128)S(1)} %bitcast.36, f32[1,128]{1,0:T(1,128)S(1)} %bitcast.38, bf16[128,512]{1,0:T(8,128)(2,1)S(1)} %copy-done.31), custom_call_target="tpu_custom_call" | custom-call | flops 1610612736 | bytes 20971520 | tf_op jit(solution)/shard_map/input_gradients/pallas_call | solution.py:139
  179.7 2.5 %collective-permute-start.16 = (f32[16,24,128]{2,1,0:T(8,128)S(1)}, f32[16,24,128]{2,1,0:T(8,128)S(1)}, u32[]{:S(2)}, u32[]{:S(2)}) collective-permute-start(f32[16,24,128]{2,1,0:T(8,128)S(1)} %dynamic-slice_bitcast_fusion), channel_id=1, source_target_pairs={{0,1},{1,0},{2,3},{3,2},{4,5},{5,4},{6,7},{7,6},{8,9},{9,8},{10,11... | collective-permute-start | bytes 589832 | tf_op jit(solution)/shard_map/ppermute | solution.py:235
  183.2 10.3 %all_to_all.30 = f32[16,24,128]{2,1,0:T(8,128)S(1)} all-to-all(f32[16,24,128]{2,1,0:T(8,128)S(1)} %bitcast_add_fusion), channel_id=1, replica_groups=mesh['y'=4,'xh'=2,'xl'=2,'z'=8,'c'=2] {'y','xh','xl'}, dimensions={0} | all-to-all | bytes 393216 | tf_op jit(solution)/shard_map/all_to_all | solution.py:19
  193.6 12.9 %all_to_all.31 = f32[8,24,128]{2,1,0:T(8,128)S(1)} all-to-all(f32[8,24,128]{2,1,0:T(8,128)S(1)} %broadcast_in_dim.6), channel_id=1, replica_groups=mesh['y'=4,'xh'=2,'xl'=2,'z'=8,'c'=2] {'z'}, dimensions={0} | all-to-all | bytes 196608 | tf_op jit(solution)/shard_map/all_to_all | solution.py:19
  206.5 9.8 %all_to_all.32 = f32[16,24,128]{2,1,0:T(8,128)S(1)} all-to-all(f32[16,24,128]{2,1,0:T(8,128)S(1)} %broadcast_in_dim.7), channel_id=1, replica_groups=mesh['y'=4,'xh'=2,'xl'=2,'z'=8,'c'=2] {'y','xh','xl'}, dimensions={0} | all-to-all | bytes 393216 | tf_op jit(solution)/shard_map/all_to_all | solution.py:19
  216.3 4.2 %collective-permute-start.17 = (f32[16,24,128]{2,1,0:T(8,128)S(1)}, f32[16,24,128]{2,1,0:T(8,128)S(1)}, u32[]{:S(2)}, u32[]{:S(2)}) collective-permute-start(f32[16,24,128]{2,1,0:T(8,128)S(1)} %all_to_all.32), channel_id=1, source_target_pairs={{0,1},{1,0},{2,3},{3,2},{4,5},{5,4},{6,7},{7,6},{8,9},{9,8},{10,11... | collective-permute-start | bytes 589832 | tf_op jit(solution)/shard_map/ppermute | solution.py:235
  (103 shorter events, 26.5 us)
Async XLA Ops:
  0.6 12.0 %copy-start.25 = (bf16[128,32,128]{2,1,0:T(8,128)(2,1)S(1)}, bf16[128,32,128]{2,1,0:T(8,128)(2,1)}, u32[]{:S(2)}) copy-start(bf16[128,32,128]{2,1,0:T(8,128)(2,1)} %pair_ref.3) | copy-start | bytes 3145732
  0.6 12.0 %copy-start.27 = (bf16[128,512]{1,0:T(8,128)(2,1)S(1)}, bf16[128,512]{1,0:T(8,128)(2,1)}, u32[]{:S(2)}) copy-start(bf16[128,512]{1,0:T(8,128)(2,1)} %weight_ref.1) | copy-start | bytes 393220
  0.7 12.0 %copy-start.28 = (f32[128]{0:T(128)S(1)}, f32[128]{0:T(128)}, u32[]{:S(2)}) copy-start(f32[128]{0:T(128)} %param.6) | copy-start | bytes 1540
  0.7 12.0 %copy-start.29 = (f32[128]{0:T(128)S(1)}, f32[128]{0:T(128)}, u32[]{:S(2)}) copy-start(f32[128]{0:T(128)} %param.7) | copy-start | bytes 1540
  3.9 25.9 %all-to-all-start = ((bf16[32,4,32,128]{3,2,1,0:T(8,128)(2,1)}), bf16[32,4,32,128]{3,2,1,0:T(8,128)(2,1)}, u32[]{:S(2)}, u32[]{:S(2)}) async-start(bf16[32,4,32,128]{3,2,1,0:T(8,128)(2,1)} %bitcast.2), calls=%async_computation | async-start | bytes 2097152 | tf_op jit(solution)/shard_map/all_to_all | solution.py:19
  15.9 4.0 %copy-start.30 = (bf16[128,512]{1,0:T(8,128)(2,1)}, bf16[128,512]{1,0:T(8,128)(2,1)S(1)}, u32[]{:S(2)}) copy-start(bf16[128,512]{1,0:T(8,128)(2,1)S(1)} %get-tuple-element.40.ordered_ref) | copy-start | bytes 393220
  29.8 84.8 %all-to-all-start.1 = ((bf16[32,8,32,128]{3,2,1,0:T(8,128)(2,1)}), bf16[32,8,32,128]{3,2,1,0:T(8,128)(2,1)S(1)}, u32[]{:S(2)}, u32[]{:S(2)}) async-start(bf16[32,8,32,128]{3,2,1,0:T(8,128)(2,1)} %bitcast.39), calls=%async_computation.1 | async-start | bytes 4194304 | tf_op jit(solution)/shard_map/all_to_all | solution.py:19
  35.2 17.7 %collective-permute-start.2 = (bf16[32,2,32,128]{3,2,1,0:T(8,128)(2,1)S(1)}, bf16[32,2,32,128]{3,2,1,0:T(8,128)(2,1)S(1)}, u32[]{:S(2)}, u32[]{:S(2)}) collective-permute-start(bf16[32,2,32,128]{3,2,1,0:T(8,128)(2,1)S(1)} %get-tuple-element.27.refs_0_), channel_id=1, source_target_pairs={{0,2},{2,4},{4,6},{6,8},{8,10},{10,12},{12,14},{14,0},{1,3},{3,5},... | collective-permute-start | bytes 1572872 | tf_op jit(solution)/shard_map/ppermute | solution.py:23
  36.9 16.0 %collective-permute-start.3 = (bf16[32,2,32,128]{3,2,1,0:T(8,128)(2,1)S(1)}, bf16[32,2,32,128]{3,2,1,0:T(8,128)(2,1)S(1)}, u32[]{:S(2)}, u32[]{:S(2)}) collective-permute-start(bf16[32,2,32,128]{3,2,1,0:T(8,128)(2,1)S(1)} %get-tuple-element.27.refs_0_), channel_id=1, source_target_pairs={{0,14},{2,0},{4,2},{6,4},{8,6},{10,8},{12,10},{14,12},{1,15},{3,1}... | collective-permute-start | bytes 1572872 | tf_op jit(solution)/shard_map/ppermute | solution.py:23
  40.9 23.2 %collective-permute-start = (bf16[32,2,32,128]{3,2,1,0:T(8,128)(2,1)S(1)}, bf16[32,2,32,128]{3,2,1,0:T(8,128)(2,1)S(1)}, u32[]{:S(2)}, u32[]{:S(2)}) collective-permute-start(bf16[32,2,32,128]{3,2,1,0:T(8,128)(2,1)S(1)} %get-tuple-element.26.refs_0_), channel_id=1, source_target_pairs={{0,2},{2,4},{4,6},{6,8},{8,10},{10,12},{12,14},{14,0},{1,3},{3,5},... | collective-permute-start | bytes 1572872 | tf_op jit(solution)/shard_map/ppermute | solution.py:23
  40.9 23.2 %collective-permute-start.1 = (bf16[32,2,32,128]{3,2,1,0:T(8,128)(2,1)S(1)}, bf16[32,2,32,128]{3,2,1,0:T(8,128)(2,1)S(1)}, u32[]{:S(2)}, u32[]{:S(2)}) collective-permute-start(bf16[32,2,32,128]{3,2,1,0:T(8,128)(2,1)S(1)} %get-tuple-element.26.refs_0_), channel_id=1, source_target_pairs={{0,14},{2,0},{4,2},{6,4},{8,6},{10,8},{12,10},{14,12},{1,15},{3,1}... | collective-permute-start | bytes 1572872 | tf_op jit(solution)/shard_map/ppermute | solution.py:23
  52.8 22.5 %collective-permute-start.6 = (bf16[32,2,32,128]{3,2,1,0:T(8,128)(2,1)S(1)}, bf16[32,2,32,128]{3,2,1,0:T(8,128)(2,1)S(1)}, u32[]{:S(2)}, u32[]{:S(2)}) collective-permute-start(bf16[32,2,32,128]{3,2,1,0:T(8,128)(2,1)S(1)} %collective-permute-done.2.refs_1_), channel_id=1, source_target_pairs={{0,2},{2,4},{4,6},{6,8},{8,10},{10,12},{12,14},{14,0},{1,3},{3,5},... | collective-permute-start | bytes 1572872 | tf_op jit(solution)/shard_map/ppermute | solution.py:23
  53.6 21.7 %collective-permute-start.7 = (bf16[32,2,32,128]{3,2,1,0:T(8,128)(2,1)S(1)}, bf16[32,2,32,128]{3,2,1,0:T(8,128)(2,1)S(1)}, u32[]{:S(2)}, u32[]{:S(2)}) collective-permute-start(bf16[32,2,32,128]{3,2,1,0:T(8,128)(2,1)S(1)} %collective-permute-done.3.refs_2_), channel_id=1, source_target_pairs={{0,14},{2,0},{4,2},{6,4},{8,6},{10,8},{12,10},{14,12},{1,15},{3,1}... | collective-permute-start | bytes 1572872 | tf_op jit(solution)/shard_map/ppermute | solution.py:23
  64.1 22.5 %collective-permute-start.4 = (bf16[32,2,32,128]{3,2,1,0:T(8,128)(2,1)S(1)}, bf16[32,2,32,128]{3,2,1,0:T(8,128)(2,1)S(1)}, u32[]{:S(2)}, u32[]{:S(2)}) collective-permute-start(bf16[32,2,32,128]{3,2,1,0:T(8,128)(2,1)S(1)} %collective-permute-done.refs_1_), channel_id=1, source_target_pairs={{0,2},{2,4},{4,6},{6,8},{8,10},{10,12},{12,14},{14,0},{1,3},{3,5},... | collective-permute-start | bytes 1572872 | tf_op jit(solution)/shard_map/ppermute | solution.py:23
  64.9 21.7 %collective-permute-start.5 = (bf16[32,2,32,128]{3,2,1,0:T(8,128)(2,1)S(1)}, bf16[32,2,32,128]{3,2,1,0:T(8,128)(2,1)S(1)}, u32[]{:S(2)}, u32[]{:S(2)}) collective-permute-start(bf16[32,2,32,128]{3,2,1,0:T(8,128)(2,1)S(1)} %collective-permute-done.1.refs_2_), channel_id=1, source_target_pairs={{0,14},{2,0},{4,2},{6,4},{8,6},{10,8},{12,10},{14,12},{1,15},{3,1}... | collective-permute-start | bytes 1572872 | tf_op jit(solution)/shard_map/ppermute | solution.py:23
  75.3 22.5 %collective-permute-start.10 = (bf16[32,2,32,128]{3,2,1,0:T(8,128)(2,1)S(1)}, bf16[32,2,32,128]{3,2,1,0:T(8,128)(2,1)S(1)}, u32[]{:S(2)}, u32[]{:S(2)}) collective-permute-start(bf16[32,2,32,128]{3,2,1,0:T(8,128)(2,1)S(1)} %collective-permute-done.6.refs_3_), channel_id=1, source_target_pairs={{0,2},{2,4},{4,6},{6,8},{8,10},{10,12},{12,14},{14,0},{1,3},{3,5},... | collective-permute-start | bytes 1572872 | tf_op jit(solution)/shard_map/ppermute | solution.py:23
  76.1 21.7 %collective-permute-start.11 = (bf16[32,2,32,128]{3,2,1,0:T(8,128)(2,1)S(1)}, bf16[32,2,32,128]{3,2,1,0:T(8,128)(2,1)S(1)}, u32[]{:S(2)}, u32[]{:S(2)}) collective-permute-start(bf16[32,2,32,128]{3,2,1,0:T(8,128)(2,1)S(1)} %collective-permute-done.7.refs_4_), channel_id=1, source_target_pairs={{0,14},{2,0},{4,2},{6,4},{8,6},{10,8},{12,10},{14,12},{1,15},{3,1}... | collective-permute-start | bytes 1572872 | tf_op jit(solution)/shard_map/ppermute | solution.py:23
  86.5 22.5 %collective-permute-start.8 = (bf16[32,2,32,128]{3,2,1,0:T(8,128)(2,1)S(1)}, bf16[32,2,32,128]{3,2,1,0:T(8,128)(2,1)S(1)}, u32[]{:S(2)}, u32[]{:S(2)}) collective-permute-start(bf16[32,2,32,128]{3,2,1,0:T(8,128)(2,1)S(1)} %collective-permute-done.4.refs_3_), channel_id=1, source_target_pairs={{0,2},{2,4},{4,6},{6,8},{8,10},{10,12},{12,14},{14,0},{1,3},{3,5},... | collective-permute-start | bytes 1572872 | tf_op jit(solution)/shard_map/ppermute | solution.py:23
  87.4 21.7 %collective-permute-start.9 = (bf16[32,2,32,128]{3,2,1,0:T(8,128)(2,1)S(1)}, bf16[32,2,32,128]{3,2,1,0:T(8,128)(2,1)S(1)}, u32[]{:S(2)}, u32[]{:S(2)}) collective-permute-start(bf16[32,2,32,128]{3,2,1,0:T(8,128)(2,1)S(1)} %collective-permute-done.5.refs_4_), channel_id=1, source_target_pairs={{0,14},{2,0},{4,2},{6,4},{8,6},{10,8},{12,10},{14,12},{1,15},{3,1}... | collective-permute-start | bytes 1572872 | tf_op jit(solution)/shard_map/ppermute | solution.py:23
  99.4 15.2 %collective-permute-start.14 = (bf16[32,1,32,128]{3,2,1,0:T(8,128)(2,1)}, bf16[32,1,32,128]{3,2,1,0:T(8,128)(2,1)S(1)}, u32[]{:S(2)}, u32[]{:S(2)}) collective-permute-start(bf16[32,1,32,128]{3,2,1,0:T(8,128)(2,1)} %slice.31), channel_id=1, source_target_pairs={{0,2},{2,4},{4,6},{6,8},{8,10},{10,12},{12,14},{14,0},{1,3},{3,5},... | collective-permute-start | bytes 786440 | tf_op jit(solution)/shard_map/ppermute | solution.py:23
  100.1 14.5 %collective-permute-start.15 = (bf16[32,1,32,128]{3,2,1,0:T(8,128)(2,1)}, bf16[32,1,32,128]{3,2,1,0:T(8,128)(2,1)}, u32[]{:S(2)}, u32[]{:S(2)}) collective-permute-start(bf16[32,1,32,128]{3,2,1,0:T(8,128)(2,1)} %slice.32), channel_id=1, source_target_pairs={{0,14},{2,0},{4,2},{6,4},{8,6},{10,8},{12,10},{14,12},{1,15},{3,1}... | collective-permute-start | bytes 786440 | tf_op jit(solution)/shard_map/ppermute | solution.py:23
  110.6 14.7 %collective-permute-start.12 = (bf16[32,1,32,128]{3,2,1,0:T(8,128)(2,1)}, bf16[32,1,32,128]{3,2,1,0:T(8,128)(2,1)}, u32[]{:S(2)}, u32[]{:S(2)}) collective-permute-start(bf16[32,1,32,128]{3,2,1,0:T(8,128)(2,1)} %slice.29), channel_id=1, source_target_pairs={{0,2},{2,4},{4,6},{6,8},{8,10},{10,12},{12,14},{14,0},{1,3},{3,5},... | collective-permute-start | bytes 786440 | tf_op jit(solution)/shard_map/ppermute | solution.py:23
  111.3 14.0 %collective-permute-start.13 = (bf16[32,1,32,128]{3,2,1,0:T(8,128)(2,1)}, bf16[32,1,32,128]{3,2,1,0:T(8,128)(2,1)}, u32[]{:S(2)}, u32[]{:S(2)}) collective-permute-start(bf16[32,1,32,128]{3,2,1,0:T(8,128)(2,1)} %slice.30), channel_id=1, source_target_pairs={{0,14},{2,0},{4,2},{6,4},{8,6},{10,8},{12,10},{14,12},{1,15},{3,1}... | collective-permute-start | bytes 786440 | tf_op jit(solution)/shard_map/ppermute | solution.py:23
  120.9 4.4 %copy-start.6 = (bf16[32,2,32,128]{3,2,1,0:T(8,128)(2,1)S(1)}, bf16[32,2,32,128]{3,2,1,0:T(8,128)(2,1)}, u32[]{:S(2)}) copy-start(bf16[32,2,32,128]{3,2,1,0:T(8,128)(2,1)} %copy-done.5) | copy-start | bytes 1572868
  120.9 4.5 %copy-start.8 = (bf16[32,2,32,128]{3,2,1,0:T(8,128)(2,1)S(1)}, bf16[32,2,32,128]{3,2,1,0:T(8,128)(2,1)}, u32[]{:S(2)}) copy-start(bf16[32,2,32,128]{3,2,1,0:T(8,128)(2,1)} %copy-done.7) | copy-start | bytes 1572868
  120.9 4.5 %copy-start.18 = (bf16[32,2,32,128]{3,2,1,0:T(8,128)(2,1)S(1)}, bf16[32,2,32,128]{3,2,1,0:T(8,128)(2,1)}, u32[]{:S(2)}) copy-start(bf16[32,2,32,128]{3,2,1,0:T(8,128)(2,1)} %copy-done.17) | copy-start | bytes 1572868
  120.9 4.5 %copy-start.20 = (bf16[32,2,32,128]{3,2,1,0:T(8,128)(2,1)S(1)}, bf16[32,2,32,128]{3,2,1,0:T(8,128)(2,1)}, u32[]{:S(2)}) copy-start(bf16[32,2,32,128]{3,2,1,0:T(8,128)(2,1)} %copy-done.19) | copy-start | bytes 1572868
  120.9 4.5 %copy-start.22 = (bf16[32,2,32,128]{3,2,1,0:T(8,128)(2,1)S(1)}, bf16[32,2,32,128]{3,2,1,0:T(8,128)(2,1)}, u32[]{:S(2)}) copy-start(bf16[32,2,32,128]{3,2,1,0:T(8,128)(2,1)} %copy-done.21) | copy-start | bytes 1572868
  120.9 4.5 %copy-start.24 = (bf16[32,2,32,128]{3,2,1,0:T(8,128)(2,1)S(1)}, bf16[32,2,32,128]{3,2,1,0:T(8,128)(2,1)}, u32[]{:S(2)}) copy-start(bf16[32,2,32,128]{3,2,1,0:T(8,128)(2,1)} %copy-done.23) | copy-start | bytes 1572868
  131.1 36.3 %all-to-all-start.2 = ((bf16[32,8,32,128]{3,2,1,0:T(8,128)(2,1)}), bf16[32,8,32,128]{3,2,1,0:T(8,128)(2,1)S(1)}, u32[]{:S(2)}, u32[]{:S(2)}) async-start(bf16[32,8,32,128]{3,2,1,0:T(8,128)(2,1)} %bitcast.30), calls=%async_computation.2 | async-start | bytes 4194304 | tf_op jit(solution)/shard_map/all_to_all | solution.py:19
  179.7 3.5 %collective-permute-start.16 = (f32[16,24,128]{2,1,0:T(8,128)S(1)}, f32[16,24,128]{2,1,0:T(8,128)S(1)}, u32[]{:S(2)}, u32[]{:S(2)}) collective-permute-start(f32[16,24,128]{2,1,0:T(8,128)S(1)} %dynamic-slice_bitcast_fusion), channel_id=1, source_target_pairs={{0,1},{1,0},{2,3},{3,2},{4,5},{5,4},{6,7},{7,6},{8,9},{9,8},{10,11... | collective-permute-start | bytes 589832 | tf_op jit(solution)/shard_map/ppermute | solution.py:235
  216.3 5.3 %collective-permute-start.17 = (f32[16,24,128]{2,1,0:T(8,128)S(1)}, f32[16,24,128]{2,1,0:T(8,128)S(1)}, u32[]{:S(2)}, u32[]{:S(2)}) collective-permute-start(f32[16,24,128]{2,1,0:T(8,128)S(1)} %all_to_all.32), channel_id=1, source_target_pairs={{0,1},{1,0},{2,3},{3,2},{4,5},{5,4},{6,7},{7,6},{8,9},{9,8},{10,11... | collective-permute-start | bytes 589832 | tf_op jit(solution)/shard_map/ppermute | solution.py:235
  (22 other events, 25.1 us)

commit v5 on v4

--- a/solution.py
+++ b/solution.py
@@ -13,6 +13,7 @@
 SLABS = 8
 STEP_ROWS = 64
 VMEM_LIMIT = 32 * 1024 * 1024
+PRODUCT_LIMIT = 58 * 1024 * 1024
 
 
 def all_to_all(x, axes):
@@ -160,69 +161,88 @@
     )(pair, back, gain, bias, ordered)
 
 
-def assemble(ref, at):
-    return jnp.concatenate(
-        [
-            jnp.concatenate([ref[4 * r + c, at] for c in range(4)], axis=0)
-            for r in range(8)
-        ],
-        axis=1,
-    )
-
-
-def product_kernel(second_half, slab_ref, sides_ref, *refs):
-    *block_refs, up_ref, down_ref = refs[: 9]
-    out_ref, grads = refs[9 + second_half :]
-
-    def place(offset, ref):
+def product_kernel(half, slab_ref, sides_hbm, *refs):
+    block_hbm = refs[:SLABS]
+    out_hbm, sides, blocks, out, grads, sems, out_sems = refs[SLABS + half :]
+    here = pl.ds(2 * half, 2)
+    loads = [
+        pltpu.make_async_copy(ref, blocks.at[n], sems.at[n]) for n, ref in enumerate(block_hbm)
+    ]
+    loads.append(pltpu.make_async_copy(sides_hbm.at[:, here], sides, sems.at[SLABS]))
+    for load in loads:
+        load.start()
+
+    def place(channel, offset, piece):
         where = lax.rem(slab_ref[0] + offset, SLABS)
         for x in range(2):
             rows = pl.ds(pl.multiple_of(512 * x + 64 * where, 64), 64)
             for r in range(8):
-                grads[rows, 128 * r : 128 * r + 128] = jnp.concatenate(
-                    [ref[4 * r + 2 * x, 0], ref[4 * r + 2 * x + 1, 0]], axis=0
+                grads[channel, rows, 128 * r : 128 * r + 128] = jnp.concatenate(
+                    [piece(4 * r + 2 * x), piece(4 * r + 2 * x + 1)], axis=0
                 )
 
-    for offset, ref in zip((0, 7, 1, 6, 2, 5, 3), block_refs):
-        place(offset, ref)
-    for channel, ref in enumerate((up_ref, down_ref)):
-        pl.when(pl.program_id(0) == channel)(functools.partial(place, 4, ref))
-    left = assemble(sides_ref.at[:, 0], 0)
-    right = assemble(sides_ref.at[:, 1], 0)
-    first = jnp.dot(right, grads[...], preferred_element_type=jnp.float32)
-    second = lax.dot_general(
-        left, grads[...], (((1,), (1,)), ((), ())), preferred_element_type=jnp.float32
-    )
-    for side, value in enumerate((first, second)):
-        value = value.astype(jnp.bfloat16)
-        for r in range(8):
-            for c in range(4):
-                out_ref[4 * r + c, side, 0] = value[
-                    32 * c : 32 * c + 32, 128 * r : 128 * r + 128
-                ]
+    def whole(channel, side):
+        return jnp.concatenate(
+            [
+                jnp.concatenate([sides[4 * r + c, side, channel] for c in range(4)], axis=0)
+                for r in range(8)
+            ],
+            axis=1,
+        )
+
+    for n, offset in enumerate((0, 7, 1, 6, 2, 5, 3, 4)):
+        loads[n].wait()
+        for channel in range(2):
+            place(channel, offset, lambda d: blocks[n, d, channel])
+    loads[SLABS].wait()
+    stores = []
+    for channel in range(2):
+        first = jnp.dot(whole(channel, 1), grads[channel], preferred_element_type=jnp.float32)
+        second = lax.dot_general(
+            whole(channel, 0),
+            grads[channel],
+            (((1,), (1,)), ((), ())),
+            preferred_element_type=jnp.float32,
+        )
+        for side, value in enumerate((first, second)):
+            value = value.astype(jnp.bfloat16)
+            for r in range(8):
+                for c in range(4):
+                    out[channel, 4 * r + c, side] = value[
+                        32 * c : 32 * c + 32, 128 * r : 128 * r + 128
+                    ]
+        stores.append(
+            pltpu.make_async_copy(
+                out.at[channel], out_hbm.at[:, here, channel], out_sems.at[channel]
+            )
+        )
+        stores[-1].start()
+    for store in stores:
+        store.wait()
 
 
 def products(slab, sides, half, blocks, earlier=None):
     groups, pairs, depth, width = sides.shape
     channels = pairs // 4
     sides = sides.reshape(groups, 4, channels, depth, width)
-    sides_spec = pl.BlockSpec((groups, 2, 1, depth, width), lambda h: (0, half, h, 0, 0))
-    piece = pl.BlockSpec((groups, 1, depth, width), lambda h: (0, h, 0, 0))
-    alone = pl.BlockSpec((groups, 1, depth, width), lambda h: (0, 0, 0, 0))
-    operands = [slab, sides, *blocks]
-    specs = [pl.BlockSpec(memory_space=pltpu.SMEM), sides_spec] + [piece] * 7 + [alone] * 2
-    if earlier is not None:
-        operands.append(earlier)
-        specs.append(pl.BlockSpec(memory_space=pl.ANY))
+    operands = [slab, sides, *blocks] + ([] if earlier is None else [earlier])
+    bf16 = lambda *shape: pltpu.VMEM(shape, jnp.bfloat16)
     return pl.pallas_call(
-        functools.partial(product_kernel, earlier is not None),
-        grid=(channels,),
-        in_specs=specs,
-        out_specs=sides_spec,
+        functools.partial(product_kernel, half),
+        in_specs=[pl.BlockSpec(memory_space=pltpu.SMEM)]
+        + [pl.BlockSpec(memory_space=pltpu.HBM)] * (len(operands) - 1),
+        out_specs=pl.BlockSpec(memory_space=pltpu.HBM),
         out_shape=jax.ShapeDtypeStruct(sides.shape, jnp.bfloat16),
-        scratch_shapes=[pltpu.VMEM((1024, 1024), jnp.bfloat16)],
+        scratch_shapes=[
+            bf16(groups, 2, channels, depth, width),
+            bf16(SLABS, groups, channels, depth, width),
+            bf16(channels, groups, 2, depth, width),
+            bf16(channels, 1024, 1024),
+            pltpu.SemaphoreType.DMA((SLABS + 1,)),
+            pltpu.SemaphoreType.DMA((2,)),
+        ],
         input_output_aliases={} if earlier is None else {len(operands) - 1: 0},
-        compiler_params=pltpu.CompilerParams(vmem_limit_bytes=VMEM_LIMIT),
+        compiler_params=pltpu.CompilerParams(vmem_limit_bytes=PRODUCT_LIMIT),
         cost_estimate=pl.CostEstimate(
             flops=4 * channels * 128 * 1024 * 1024, bytes_accessed=12 << 20, transcendentals=0
         ),
@@ -256,9 +276,8 @@
     after = lambda wanted, done: barrier((wanted, done))[0]
     own = all_to_all(split(product_grad), PLANE)
     sides, ordered = pre(pair, gain, bias, proj_weight)
-    own, sides = barrier((own, split(sides)))
+    a0, b0, sides = barrier((own[:, :2], own[:, 2:], split(sides)))
     sides = all_to_all(sides, PLANE)
-    a0, b0 = barrier((own[:, :2], own[:, 2:]))
     a1 = both((a0, a0))
     b1 = both((b0, b0))
     a1 = barrier(a1)
@@ -270,11 +289,11 @@
     b2 = after(b2, a2)
     b3 = both(b2)
     a3 = after(a3, b2)
-    a4 = shift(a3[0][:, :1], 1), shift(a3[1][:, 1:], -1)
+    a4 = shift(a3[0], 1)
     b3 = after(b3, a3)
-    b4 = shift(b3[0][:, :1], 1), shift(b3[1][:, 1:], -1)
-    back = products(slab, sides, 0, [a0, *a1, *a2, *a3, *a4])
-    back = products(slab, sides, 1, [b0, *b1, *b2, *b3, *b4], back)
+    b4 = shift(b3[1], -1)
+    back = products(slab, sides, 0, [a0, *a1, *a2, *a3, a4])
+    back = products(slab, sides, 1, [b0, *b1, *b2, *b3, b4], back)
     back = all_to_all(back.reshape(sides.shape), PLANE)
 
     total_rows = 24 * GROUPS

time: 224 us -> 217 us (0.969)
  local copies, waits for them, and re-layouts: 34.2 us -> 18 us
  waiting for transfers between devices: 83.8 us -> 97.4 us
  starting transfers between devices: 52.3 us -> 46 us
  Pallas kernels: 18 us -> 20.5 us
    unnamed x66 -> x32, local copies, waits for them, and re-layouts: 17.9 us -> 3.85 us
    ppermute x16 -> x14, waiting for transfers between devices: 44 us -> 57.5 us  [shift(): return lax.ppermute(x, 'z', [(i, (i + by) % SLABS) for i in range(SLABS)])]
    all_to_all x3, starting transfers between devices: 21.2 us -> 17.6 us  [all_to_all(): return lax.all_to_all(x, axes, split_axis=0, concat_axis=0, tiled=True)]
    ppermute x16 -> x14, starting transfers between devices: 24.5 us -> 21.8 us  [shift(): return lax.ppermute(x, 'z', [(i, (i + by) % SLABS) for i in range(SLABS)])]
    pallas_call x2, Pallas kernels: 8.71 us -> 11.3 us  [products(): pl.pallas_call(functools.partial(product_kernel, half), in_specs=[pl.Bloc...]
  transfers between devices with their start and end apart: 21 -> 19, of which waited for: 11 -> 11; matrix products, arithmetic and copies ran while one was open for 4% -> 2% of each run, Pallas kernels for 3% -> 4%
where the time goes in v5:
time: 217 us; the launch traced here: 216 us
  waiting for transfers between devices  97.4 us (45%)
  starting transfers between devices  46 us (21%)
  blocking collectives  32.8 us (15%)
  Pallas kernels  20.5 us (9%)
  local copies, waits for them, and re-layouts  18 us (8%)
    ppermute x14, waiting for transfers between devices, shift(): return lax.ppermute(x, 'z', [(i, (i + by) % SLABS) for i in range(SLABS)])  57.5 us
    all_to_all x3, waiting for transfers between devices, all_to_all(): return lax.all_to_all(x, axes, split_axis=0, concat_axis=0, tiled=True)  37.8 us
    all_to_all x3, blocking collectives, all_to_all(): return lax.all_to_all(x, axes, split_axis=0, concat_axis=0, tiled=True)  32.8 us
    ppermute x14, starting transfers between devices, shift(): return lax.ppermute(x, 'z', [(i, (i + by) % SLABS) for i in range(SLABS)])  21.8 us
    all_to_all x3, starting transfers between devices, all_to_all(): return lax.all_to_all(x, axes, split_axis=0, concat_axis=0, tiled=True)  17.6 us
    pallas_call x2, Pallas kernels, products(): pl.pallas_call(functools.partial(product_kernel, half), in_specs=[pl.Bloc...  11.3 us
    transpose x2, local copies, waits for them, and re-layouts, per_device(): jnp.transpose(x, (2, 1, 0)).reshape(GROUPS, -1, cols, rows)  7.27 us
    ppermute x2, starting transfers between devices, sum_of_all(): swap = lambda x: lax.ppermute(x, 'c', [(0, 1), (1, 0)])  6.62 us
  transfers between devices with their start and end apart: 19, of which 11 were waited for; matrix products, arithmetic and copies ran while one was open for 2% of the time, Pallas kernels for 4%

profile of v5, /device:TPU:1, one launch (start us, length us, event | category | flops | bytes accessed | tf_op | source)
XLA Modules:
  0.0 216.4 jit_solution(12728391631665779931)
XLA Ops:
  0.7 3.3 %copy.17 = bf16[128,32,128]{2,1,0:T(8,128)(2,1)} copy(bf16[128,32,128]{0,1,2:T(8,128)(2,1)} %bitcast.43) | data formatting | bytes 2097152 | tf_op jit(solution)/shard_map/transpose | solution.py:269
  3.9 8.6 %all-to-all-start = ((bf16[32,4,32,128]{3,2,1,0:T(8,128)(2,1)}), bf16[32,4,32,128]{3,2,1,0:T(8,128)(2,1)}, u32[]{:S(2)}, u32[]{:S(2)}) async-start(bf16[32,4,32,128]{3,2,1,0:T(8,128)(2,1)} %bitcast.2), calls=%async_computation | async-start | bytes 2097152 | tf_op jit(solution)/shard_map/all_to_all | solution.py:20
  12.6 3.3 %gated_projections.1 = (bf16[128,32,256]{2,1,0:T(8,128)(2,1)S(1)}, bf16[128,512]{1,0:T(8,128)(2,1)S(1)}) custom-call(bf16[128,32,128]{2,1,0:T(8,128)(2,1)S(1)} %copy-done, f32[1,128]{1,0:T(1,128)S(1)} %bitcast.32, f32[1,128]{1,0:T(1,128)S(1)} %bitcast.34, bf16[128,512]{1,0:T(8,128)(2,1)S(1)} %copy-done.1), custom_call_target="tpu_custom_call" | custom-call | flops 536870912 | bytes 12582912 | tf_op jit(solution)/shard_map/gated_projections/pallas_call | solution.py:67
  15.9 4.0 %copy.18 = bf16[256,32,128]{2,1,0:T(8,128)(2,1)} copy(bf16[256,32,128]{0,1,2:T(8,128)(2,1)S(1)} %bitcast.29) | data formatting | bytes 4194304 | tf_op jit(solution)/shard_map/transpose | solution.py:269
  19.9 9.9 %all-to-all-done = bf16[32,4,32,128]{3,2,1,0:T(8,128)(2,1)} async-done(((bf16[32,4,32,128]{3,2,1,0:T(8,128)(2,1)}), bf16[32,4,32,128]{3,2,1,0:T(8,128)(2,1)}, u32[]{:S(2)}, u32[]{:S(2)}) %all-to-all-start) | async-done | bytes 1048608 | tf_op jit(solution)/shard_map/all_to_all | solution.py:20
  29.8 2.2 %fusion = (bf16[32,2,32,128]{3,2,1,0:T(8,128)(2,1)}, bf16[32,2,32,128]{3,2,1,0:T(8,128)(2,1)}) fusion(bf16[32,4,32,128]{3,2,1,0:T(8,128)(2,1)} %all-to-all-done), kind=kLoop, calls=%fused_computation.7 | loop fusion | bytes 2097152 | tf_op jit(solution)/shard_map/slice | solution.py:279
  33.7 3.9 %collective-permute-start.3 = (bf16[32,2,32,128]{3,2,1,0:T(8,128)(2,1)}, bf16[32,2,32,128]{3,2,1,0:T(8,128)(2,1)}, u32[]{:S(2)}, u32[]{:S(2)}) collective-permute-start(bf16[32,2,32,128]{3,2,1,0:T(8,128)(2,1)} %get-tuple-element.25.refs_0_), channel_id=1, source_target_pairs={{0,14},{2,0},{4,2},{6,4},{8,6},{10,8},{12,10},{14,12},{1,15},{3,1}... | collective-permute-start | bytes 1572872 | tf_op jit(solution)/shard_map/ppermute | solution.py:24
  37.6 4.3 %all-to-all-start.1 = ((bf16[32,8,32,128]{3,2,1,0:T(8,128)(2,1)}), bf16[32,8,32,128]{3,2,1,0:T(8,128)(2,1)S(1)}, u32[]{:S(2)}, u32[]{:S(2)}) async-start(bf16[32,8,32,128]{3,2,1,0:T(8,128)(2,1)} %bitcast.39), calls=%async_computation.1 | async-start | bytes 4194304 | tf_op jit(solution)/shard_map/all_to_all | solution.py:20
  42.1 2.7 %collective-permute-start.1 = (bf16[32,2,32,128]{3,2,1,0:T(8,128)(2,1)}, bf16[32,2,32,128]{3,2,1,0:T(8,128)(2,1)S(1)}, u32[]{:S(2)}, u32[]{:S(2)}) collective-permute-start(bf16[32,2,32,128]{3,2,1,0:T(8,128)(2,1)} %get-tuple-element.24.refs_0_), channel_id=1, source_target_pairs={{0,14},{2,0},{4,2},{6,4},{8,6},{10,8},{12,10},{14,12},{1,15},{3,1}... | collective-permute-start | bytes 1572872 | tf_op jit(solution)/shard_map/ppermute | solution.py:24
  44.7 5.2 %collective-permute-done.2.refs_1_ = bf16[32,2,32,128]{3,2,1,0:T(8,128)(2,1)} collective-permute-done((bf16[32,2,32,128]{3,2,1,0:T(8,128)(2,1)}, bf16[32,2,32,128]{3,2,1,0:T(8,128)(2,1)}, u32[]{:S(2)}, u32[]{:S(2)}) %collective-permute-start.2) | collective-permute-done | bytes 524320 | tf_op jit(solution)/shard_map/ppermute | solution.py:24
  49.9 2.7 %collective-permute-start.7 = (bf16[32,2,32,128]{3,2,1,0:T(8,128)(2,1)}, bf16[32,2,32,128]{3,2,1,0:T(8,128)(2,1)S(1)}, u32[]{:S(2)}, u32[]{:S(2)}) collective-permute-start(bf16[32,2,32,128]{3,2,1,0:T(8,128)(2,1)} %collective-permute-done.3.refs_2_), channel_id=1, source_target_pairs={{0,14},{2,0},{4,2},{6,4},{8,6},{10,8},{12,10},{14,12},{1,15},{3,1}... | collective-permute-start | bytes 1572872 | tf_op jit(solution)/shard_map/ppermute | solution.py:24
  52.6 8.4 %collective-permute-done.refs_1_ = bf16[32,2,32,128]{3,2,1,0:T(8,128)(2,1)S(1)} collective-permute-done((bf16[32,2,32,128]{3,2,1,0:T(8,128)(2,1)}, bf16[32,2,32,128]{3,2,1,0:T(8,128)(2,1)S(1)}, u32[]{:S(2)}, u32[]{:S(2)}) %collective-permute-start) | collective-permute-done | bytes 524320 | tf_op jit(solution)/shard_map/ppermute | solution.py:24
  61.1 2.7 %collective-permute-start.5 = (bf16[32,2,32,128]{3,2,1,0:T(8,128)(2,1)S(1)}, bf16[32,2,32,128]{3,2,1,0:T(8,128)(2,1)S(1)}, u32[]{:S(2)}, u32[]{:S(2)}) collective-permute-start(bf16[32,2,32,128]{3,2,1,0:T(8,128)(2,1)S(1)} %collective-permute-done.1.refs_2_), channel_id=1, source_target_pairs={{0,14},{2,0},{4,2},{6,4},{8,6},{10,8},{12,10},{14,12},{1,15},{3,1}... | collective-permute-start | bytes 1572872 | tf_op jit(solution)/shard_map/ppermute | solution.py:24
  63.8 8.5 %collective-permute-done.6.refs_3_ = bf16[32,2,32,128]{3,2,1,0:T(8,128)(2,1)S(1)} collective-permute-done((bf16[32,2,32,128]{3,2,1,0:T(8,128)(2,1)}, bf16[32,2,32,128]{3,2,1,0:T(8,128)(2,1)S(1)}, u32[]{:S(2)}, u32[]{:S(2)}) %collective-permute-start.6) | collective-permute-done | bytes 524320 | tf_op jit(solution)/shard_map/ppermute | solution.py:24
  73.0 2.7 %collective-permute-start.11 = (bf16[32,2,32,128]{3,2,1,0:T(8,128)(2,1)S(1)}, bf16[32,2,32,128]{3,2,1,0:T(8,128)(2,1)S(1)}, u32[]{:S(2)}, u32[]{:S(2)}) collective-permute-start(bf16[32,2,32,128]{3,2,1,0:T(8,128)(2,1)S(1)} %collective-permute-done.7.refs_4_), channel_id=1, source_target_pairs={{0,14},{2,0},{4,2},{6,4},{8,6},{10,8},{12,10},{14,12},{1,15},{3,1}... | collective-permute-start | bytes 1572872 | tf_op jit(solution)/shard_map/ppermute | solution.py:24
  75.7 7.8 %collective-permute-done.4.refs_3_ = bf16[32,2,32,128]{3,2,1,0:T(8,128)(2,1)S(1)} collective-permute-done((bf16[32,2,32,128]{3,2,1,0:T(8,128)(2,1)S(1)}, bf16[32,2,32,128]{3,2,1,0:T(8,128)(2,1)S(1)}, u32[]{:S(2)}, u32[]{:S(2)}) %collective-permute-start.4) | collective-permute-done | bytes 524320 | tf_op jit(solution)/shard_map/ppermute | solution.py:24
  83.8 2.7 %collective-permute-start.9 = (bf16[32,2,32,128]{3,2,1,0:T(8,128)(2,1)S(1)}, bf16[32,2,32,128]{3,2,1,0:T(8,128)(2,1)}, u32[]{:S(2)}, u32[]{:S(2)}) collective-permute-start(bf16[32,2,32,128]{3,2,1,0:T(8,128)(2,1)S(1)} %collective-permute-done.5.refs_4_), channel_id=1, source_target_pairs={{0,14},{2,0},{4,2},{6,4},{8,6},{10,8},{12,10},{14,12},{1,15},{3,1}... | collective-permute-start | bytes 1572872 | tf_op jit(solution)/shard_map/ppermute | solution.py:24
  86.4 8.4 %collective-permute-done.10.refs_5_ = bf16[32,2,32,128]{3,2,1,0:T(8,128)(2,1)} collective-permute-done((bf16[32,2,32,128]{3,2,1,0:T(8,128)(2,1)S(1)}, bf16[32,2,32,128]{3,2,1,0:T(8,128)(2,1)}, u32[]{:S(2)}, u32[]{:S(2)}) %collective-permute-start.10) | collective-permute-done | bytes 524320 | tf_op jit(solution)/shard_map/ppermute | solution.py:24
  95.6 10.3 %collective-permute-done.8.refs_5_ = bf16[32,2,32,128]{3,2,1,0:T(8,128)(2,1)S(1)} collective-permute-done((bf16[32,2,32,128]{3,2,1,0:T(8,128)(2,1)S(1)}, bf16[32,2,32,128]{3,2,1,0:T(8,128)(2,1)S(1)}, u32[]{:S(2)}, u32[]{:S(2)}) %collective-permute-start.8) | collective-permute-done | bytes 524320 | tf_op jit(solution)/shard_map/ppermute | solution.py:24
  106.0 2.4 %collective-permute-start.12 = (bf16[32,2,32,128]{3,2,1,0:T(8,128)(2,1)}, bf16[32,2,32,128]{3,2,1,0:T(8,128)(2,1)}, u32[]{:S(2)}, u32[]{:S(2)}) collective-permute-start(bf16[32,2,32,128]{3,2,1,0:T(8,128)(2,1)} %collective-permute-done.9.refs_6_), channel_id=1, source_target_pairs={{0,14},{2,0},{4,2},{6,4},{8,6},{10,8},{12,10},{14,12},{1,15},{3,1}... | collective-permute-start | bytes 1572872 | tf_op jit(solution)/shard_map/ppermute | solution.py:24
  108.5 8.9 %collective-permute-done.13.refs_7_ = bf16[32,2,32,128]{3,2,1,0:T(8,128)(2,1)} collective-permute-done((bf16[32,2,32,128]{3,2,1,0:T(8,128)(2,1)}, bf16[32,2,32,128]{3,2,1,0:T(8,128)(2,1)}, u32[]{:S(2)}, u32[]{:S(2)}) %collective-permute-start.13) | collective-permute-done | bytes 524320 | tf_op jit(solution)/shard_map/ppermute | solution.py:24
  117.3 5.6 %triangle_products.2.refs_8_ = bf16[32,4,2,32,128]{4,3,2,1,0:T(8,128)(2,1)} custom-call(s32[1]{0:T(128)} %bitcast.slab_ref, bf16[32,4,2,32,128]{4,3,2,1,0:T(8,128)(2,1)} %bitcast.36, bf16[32,2,32,128]{3,2,1,0:T(8,128)(2,1)} %get-tuple-element.25.refs_0_, bf16[32,2,32,128]{3,2,1,0:T(8,128)(2,1)} %collective-permute-done.2.refs_1_, ...), custom_call_target="tpu_custom_call" | custom-call | flops 1073741824 | bytes 12582912 | tf_op jit(solution)/shard_map/triangle_products/pallas_call | solution.py:230
  123.0 5.6 %triangle_products.3 = bf16[32,4,2,32,128]{4,3,2,1,0:T(8,128)(2,1)} custom-call(s32[1]{0:T(128)} %bitcast.slab_ref, bf16[32,4,2,32,128]{4,3,2,1,0:T(8,128)(2,1)} %bitcast.37, bf16[32,2,32,128]{3,2,1,0:T(8,128)(2,1)} %get-tuple-element.24.refs_0_, bf16[32,2,32,128]{3,2,1,0:T(8,128)(2,1)} %copy-done.11, ...), custom_call_target="tpu_custom_call", output_to_operand_aliasing={{}: (10, {})} | custom-call | flops 1073741824 | bytes 12582912 | tf_op jit(solution)/shard_map/triangle_products/pallas_call | solution.py:230
  128.6 4.6 %all-to-all-start.2 = ((bf16[32,8,32,128]{3,2,1,0:T(8,128)(2,1)}), bf16[32,8,32,128]{3,2,1,0:T(8,128)(2,1)S(1)}, u32[]{:S(2)}, u32[]{:S(2)}) async-start(bf16[32,8,32,128]{3,2,1,0:T(8,128)(2,1)} %bitcast.38), calls=%async_computation.2 | async-start | bytes 4194304 | tf_op jit(solution)/shard_map/all_to_all | solution.py:20
  133.2 28.0 %all-to-all-done.2 = bf16[32,8,32,128]{3,2,1,0:T(8,128)(2,1)S(1)} async-done(((bf16[32,8,32,128]{3,2,1,0:T(8,128)(2,1)}), bf16[32,8,32,128]{3,2,1,0:T(8,128)(2,1)S(1)}, u32[]{:S(2)}, u32[]{:S(2)}) %all-to-all-start.2) | async-done | bytes 2097184 | tf_op jit(solution)/shard_map/all_to_all | solution.py:20
  162.5 3.9 %copy.19 = bf16[256,32,128]{0,1,2:T(8,128)(2,1)S(1)} copy(bf16[256,32,128]{2,1,0:T(8,128)(2,1)} %bitcast.40) | data formatting | bytes 4194304 | tf_op jit(solution)/shard_map/reshape | solution.py:270
  167.3 6.0 %input_gradients.1 = (bf16[128,32,128]{2,1,0:T(8,128)(2,1)}, f32[768,128]{1,0:T(8,128)S(1)}) custom-call(bf16[128,32,128]{2,1,0:T(8,128)(2,1)S(1)} %copy-done, bf16[128,32,256]{2,1,0:T(8,128)(2,1)S(1)} %bitcast.28, f32[1,128]{1,0:T(1,128)S(1)} %bitcast.33, f32[1,128]{1,0:T(1,128)S(1)} %bitcast.35, bf16[128,512]{1,0:T(8,128)(2,1)S(1)} %copy-done.5), custom_call_target="tpu_custom_call" | custom-call | flops 1610612736 | bytes 20971520 | tf_op jit(solution)/shard_map/input_gradients/pallas_call | solution.py:140
  173.3 2.5 %collective-permute-start.14 = (f32[16,24,128]{2,1,0:T(8,128)S(1)}, f32[16,24,128]{2,1,0:T(8,128)S(1)}, u32[]{:S(2)}, u32[]{:S(2)}) collective-permute-start(f32[16,24,128]{2,1,0:T(8,128)S(1)} %dynamic-slice_bitcast_fusion), channel_id=1, source_target_pairs={{0,1},{1,0},{2,3},{3,2},{4,5},{5,4},{6,7},{7,6},{8,9},{9,8},{10,11... | collective-permute-start | bytes 589832 | tf_op jit(solution)/shard_map/ppermute | solution.py:255
  176.9 10.3 %all_to_all.30 = f32[16,24,128]{2,1,0:T(8,128)S(1)} all-to-all(f32[16,24,128]{2,1,0:T(8,128)S(1)} %bitcast_add_fusion), channel_id=1, replica_groups=mesh['y'=4,'xh'=2,'xl'=2,'z'=8,'c'=2] {'y','xh','xl'}, dimensions={0} | all-to-all | bytes 393216 | tf_op jit(solution)/shard_map/all_to_all | solution.py:20
  187.2 12.7 %all_to_all.31 = f32[8,24,128]{2,1,0:T(8,128)S(1)} all-to-all(f32[8,24,128]{2,1,0:T(8,128)S(1)} %broadcast_in_dim.6), channel_id=1, replica_groups=mesh['y'=4,'xh'=2,'xl'=2,'z'=8,'c'=2] {'z'}, dimensions={0} | all-to-all | bytes 196608 | tf_op jit(solution)/shard_map/all_to_all | solution.py:20
  199.9 9.8 %all_to_all.32 = f32[16,24,128]{2,1,0:T(8,128)S(1)} all-to-all(f32[16,24,128]{2,1,0:T(8,128)S(1)} %broadcast_in_dim.7), channel_id=1, replica_groups=mesh['y'=4,'xh'=2,'xl'=2,'z'=8,'c'=2] {'y','xh','xl'}, dimensions={0} | all-to-all | bytes 393216 | tf_op jit(solution)/shard_map/all_to_all | solution.py:20
  209.7 4.2 %collective-permute-start.15 = (f32[16,24,128]{2,1,0:T(8,128)S(1)}, f32[16,24,128]{2,1,0:T(8,128)S(1)}, u32[]{:S(2)}, u32[]{:S(2)}) collective-permute-start(f32[16,24,128]{2,1,0:T(8,128)S(1)} %all_to_all.32), channel_id=1, source_target_pairs={{0,1},{1,0},{2,3},{3,2},{4,5},{5,4},{6,7},{7,6},{8,9},{9,8},{10,11... | collective-permute-start | bytes 589832 | tf_op jit(solution)/shard_map/ppermute | solution.py:255
  (61 shorter events, 9.6 us)
Async XLA Ops:
  0.6 12.0 %copy-start = (bf16[128,32,128]{2,1,0:T(8,128)(2,1)S(1)}, bf16[128,32,128]{2,1,0:T(8,128)(2,1)}, u32[]{:S(2)}) copy-start(bf16[128,32,128]{2,1,0:T(8,128)(2,1)} %pair_ref.3) | copy-start | bytes 3145732
  0.6 12.0 %copy-start.1 = (bf16[128,512]{1,0:T(8,128)(2,1)S(1)}, bf16[128,512]{1,0:T(8,128)(2,1)}, u32[]{:S(2)}) copy-start(bf16[128,512]{1,0:T(8,128)(2,1)} %weight_ref.1) | copy-start | bytes 393220
  0.7 12.0 %copy-start.2 = (f32[128]{0:T(128)S(1)}, f32[128]{0:T(128)}, u32[]{:S(2)}) copy-start(f32[128]{0:T(128)} %param.6) | copy-start | bytes 1540
  0.7 12.0 %copy-start.3 = (f32[128]{0:T(128)S(1)}, f32[128]{0:T(128)}, u32[]{:S(2)}) copy-start(f32[128]{0:T(128)} %param.7) | copy-start | bytes 1540
  3.9 25.9 %all-to-all-start = ((bf16[32,4,32,128]{3,2,1,0:T(8,128)(2,1)}), bf16[32,4,32,128]{3,2,1,0:T(8,128)(2,1)}, u32[]{:S(2)}, u32[]{:S(2)}) async-start(bf16[32,4,32,128]{3,2,1,0:T(8,128)(2,1)} %bitcast.2), calls=%async_computation | async-start | bytes 2097152 | tf_op jit(solution)/shard_map/all_to_all | solution.py:20
  15.9 4.0 %copy-start.4 = (bf16[128,512]{1,0:T(8,128)(2,1)}, bf16[128,512]{1,0:T(8,128)(2,1)S(1)}, u32[]{:S(2)}) copy-start(bf16[128,512]{1,0:T(8,128)(2,1)S(1)} %get-tuple-element.38.ordered_ref) | copy-start | bytes 393220
  32.0 17.9 %collective-permute-start.2 = (bf16[32,2,32,128]{3,2,1,0:T(8,128)(2,1)}, bf16[32,2,32,128]{3,2,1,0:T(8,128)(2,1)}, u32[]{:S(2)}, u32[]{:S(2)}) collective-permute-start(bf16[32,2,32,128]{3,2,1,0:T(8,128)(2,1)} %get-tuple-element.25.refs_0_), channel_id=1, source_target_pairs={{0,2},{2,4},{4,6},{6,8},{8,10},{10,12},{12,14},{14,0},{1,3},{3,5},... | collective-permute-start | bytes 1572872 | tf_op jit(solution)/shard_map/ppermute | solution.py:24
  33.7 16.2 %collective-permute-start.3 = (bf16[32,2,32,128]{3,2,1,0:T(8,128)(2,1)}, bf16[32,2,32,128]{3,2,1,0:T(8,128)(2,1)}, u32[]{:S(2)}, u32[]{:S(2)}) collective-permute-start(bf16[32,2,32,128]{3,2,1,0:T(8,128)(2,1)} %get-tuple-element.25.refs_0_), channel_id=1, source_target_pairs={{0,14},{2,0},{4,2},{6,4},{8,6},{10,8},{12,10},{14,12},{1,15},{3,1}... | collective-permute-start | bytes 1572872 | tf_op jit(solution)/shard_map/ppermute | solution.py:24
  37.6 70.8 %all-to-all-start.1 = ((bf16[32,8,32,128]{3,2,1,0:T(8,128)(2,1)}), bf16[32,8,32,128]{3,2,1,0:T(8,128)(2,1)S(1)}, u32[]{:S(2)}, u32[]{:S(2)}) async-start(bf16[32,8,32,128]{3,2,1,0:T(8,128)(2,1)} %bitcast.39), calls=%async_computation.1 | async-start | bytes 4194304 | tf_op jit(solution)/shard_map/all_to_all | solution.py:20
  42.0 19.1 %collective-permute-start = (bf16[32,2,32,128]{3,2,1,0:T(8,128)(2,1)}, bf16[32,2,32,128]{3,2,1,0:T(8,128)(2,1)S(1)}, u32[]{:S(2)}, u32[]{:S(2)}) collective-permute-start(bf16[32,2,32,128]{3,2,1,0:T(8,128)(2,1)} %get-tuple-element.24.refs_0_), channel_id=1, source_target_pairs={{0,2},{2,4},{4,6},{6,8},{8,10},{10,12},{12,14},{14,0},{1,3},{3,5},... | collective-permute-start | bytes 1572872 | tf_op jit(solution)/shard_map/ppermute | solution.py:24
  42.1 19.0 %collective-permute-start.1 = (bf16[32,2,32,128]{3,2,1,0:T(8,128)(2,1)}, bf16[32,2,32,128]{3,2,1,0:T(8,128)(2,1)S(1)}, u32[]{:S(2)}, u32[]{:S(2)}) collective-permute-start(bf16[32,2,32,128]{3,2,1,0:T(8,128)(2,1)} %get-tuple-element.24.refs_0_), channel_id=1, source_target_pairs={{0,14},{2,0},{4,2},{6,4},{8,6},{10,8},{12,10},{14,12},{1,15},{3,1}... | collective-permute-start | bytes 1572872 | tf_op jit(solution)/shard_map/ppermute | solution.py:24
  49.9 22.4 %collective-permute-start.6 = (bf16[32,2,32,128]{3,2,1,0:T(8,128)(2,1)}, bf16[32,2,32,128]{3,2,1,0:T(8,128)(2,1)S(1)}, u32[]{:S(2)}, u32[]{:S(2)}) collective-permute-start(bf16[32,2,32,128]{3,2,1,0:T(8,128)(2,1)} %collective-permute-done.2.refs_1_), channel_id=1, source_target_pairs={{0,2},{2,4},{4,6},{6,8},{8,10},{10,12},{12,14},{14,0},{1,3},{3,5},... | collective-permute-start | bytes 1572872 | tf_op jit(solution)/shard_map/ppermute | solution.py:24
  49.9 22.4 %collective-permute-start.7 = (bf16[32,2,32,128]{3,2,1,0:T(8,128)(2,1)}, bf16[32,2,32,128]{3,2,1,0:T(8,128)(2,1)S(1)}, u32[]{:S(2)}, u32[]{:S(2)}) collective-permute-start(bf16[32,2,32,128]{3,2,1,0:T(8,128)(2,1)} %collective-permute-done.3.refs_2_), channel_id=1, source_target_pairs={{0,14},{2,0},{4,2},{6,4},{8,6},{10,8},{12,10},{14,12},{1,15},{3,1}... | collective-permute-start | bytes 1572872 | tf_op jit(solution)/shard_map/ppermute | solution.py:24
  61.0 34.6 %copy-start.11 = (bf16[32,2,32,128]{3,2,1,0:T(8,128)(2,1)}, bf16[32,2,32,128]{3,2,1,0:T(8,128)(2,1)S(1)}, u32[]{:S(2)}) copy-start(bf16[32,2,32,128]{3,2,1,0:T(8,128)(2,1)S(1)} %collective-permute-done.refs_1_) | copy-start | bytes 1572868
  61.0 44.9 %copy-start.12 = (bf16[32,2,32,128]{3,2,1,0:T(8,128)(2,1)}, bf16[32,2,32,128]{3,2,1,0:T(8,128)(2,1)S(1)}, u32[]{:S(2)}) copy-start(bf16[32,2,32,128]{3,2,1,0:T(8,128)(2,1)S(1)} %collective-permute-done.1.refs_2_) | copy-start | bytes 1572868
  61.0 22.5 %collective-permute-start.4 = (bf16[32,2,32,128]{3,2,1,0:T(8,128)(2,1)S(1)}, bf16[32,2,32,128]{3,2,1,0:T(8,128)(2,1)S(1)}, u32[]{:S(2)}, u32[]{:S(2)}) collective-permute-start(bf16[32,2,32,128]{3,2,1,0:T(8,128)(2,1)S(1)} %collective-permute-done.refs_1_), channel_id=1, source_target_pairs={{0,2},{2,4},{4,6},{6,8},{8,10},{10,12},{12,14},{14,0},{1,3},{3,5},... | collective-permute-start | bytes 1572872 | tf_op jit(solution)/shard_map/ppermute | solution.py:24
  61.1 22.4 %collective-permute-start.5 = (bf16[32,2,32,128]{3,2,1,0:T(8,128)(2,1)S(1)}, bf16[32,2,32,128]{3,2,1,0:T(8,128)(2,1)S(1)}, u32[]{:S(2)}, u32[]{:S(2)}) collective-permute-start(bf16[32,2,32,128]{3,2,1,0:T(8,128)(2,1)S(1)} %collective-permute-done.1.refs_2_), channel_id=1, source_target_pairs={{0,14},{2,0},{4,2},{6,4},{8,6},{10,8},{12,10},{14,12},{1,15},{3,1}... | collective-permute-start | bytes 1572872 | tf_op jit(solution)/shard_map/ppermute | solution.py:24
  73.0 21.8 %copy-start.9 = (bf16[32,2,32,128]{3,2,1,0:T(8,128)(2,1)}, bf16[32,2,32,128]{3,2,1,0:T(8,128)(2,1)S(1)}, u32[]{:S(2)}) copy-start(bf16[32,2,32,128]{3,2,1,0:T(8,128)(2,1)S(1)} %collective-permute-done.7.refs_4_) | copy-start | bytes 1572868
  73.0 21.8 %collective-permute-start.10 = (bf16[32,2,32,128]{3,2,1,0:T(8,128)(2,1)S(1)}, bf16[32,2,32,128]{3,2,1,0:T(8,128)(2,1)}, u32[]{:S(2)}, u32[]{:S(2)}) collective-permute-start(bf16[32,2,32,128]{3,2,1,0:T(8,128)(2,1)S(1)} %collective-permute-done.6.refs_3_), channel_id=1, source_target_pairs={{0,2},{2,4},{4,6},{6,8},{8,10},{10,12},{12,14},{14,0},{1,3},{3,5},... | collective-permute-start | bytes 1572872 | tf_op jit(solution)/shard_map/ppermute | solution.py:24
  73.0 21.8 %collective-permute-start.11 = (bf16[32,2,32,128]{3,2,1,0:T(8,128)(2,1)S(1)}, bf16[32,2,32,128]{3,2,1,0:T(8,128)(2,1)S(1)}, u32[]{:S(2)}, u32[]{:S(2)}) collective-permute-start(bf16[32,2,32,128]{3,2,1,0:T(8,128)(2,1)S(1)} %collective-permute-done.7.refs_4_), channel_id=1, source_target_pairs={{0,14},{2,0},{4,2},{6,4},{8,6},{10,8},{12,10},{14,12},{1,15},{3,1}... | collective-permute-start | bytes 1572872 | tf_op jit(solution)/shard_map/ppermute | solution.py:24
  83.5 22.5 %copy-start.13 = (bf16[32,2,32,128]{3,2,1,0:T(8,128)(2,1)}, bf16[32,2,32,128]{3,2,1,0:T(8,128)(2,1)S(1)}, u32[]{:S(2)}) copy-start(bf16[32,2,32,128]{3,2,1,0:T(8,128)(2,1)S(1)} %collective-permute-done.4.refs_3_) | copy-start | bytes 1572868
  83.5 24.9 %copy-start.14 = (bf16[32,2,32,128]{3,2,1,0:T(8,128)(2,1)}, bf16[32,2,32,128]{3,2,1,0:T(8,128)(2,1)S(1)}, u32[]{:S(2)}) copy-start(bf16[32,2,32,128]{3,2,1,0:T(8,128)(2,1)S(1)} %collective-permute-done.5.refs_4_) | copy-start | bytes 1572868
  83.5 22.5 %collective-permute-start.8 = (bf16[32,2,32,128]{3,2,1,0:T(8,128)(2,1)S(1)}, bf16[32,2,32,128]{3,2,1,0:T(8,128)(2,1)S(1)}, u32[]{:S(2)}, u32[]{:S(2)}) collective-permute-start(bf16[32,2,32,128]{3,2,1,0:T(8,128)(2,1)S(1)} %collective-permute-done.4.refs_3_), channel_id=1, source_target_pairs={{0,2},{2,4},{4,6},{6,8},{8,10},{10,12},{12,14},{14,0},{1,3},{3,5},... | collective-permute-start | bytes 1572872 | tf_op jit(solution)/shard_map/ppermute | solution.py:24
  83.8 22.2 %collective-permute-start.9 = (bf16[32,2,32,128]{3,2,1,0:T(8,128)(2,1)S(1)}, bf16[32,2,32,128]{3,2,1,0:T(8,128)(2,1)}, u32[]{:S(2)}, u32[]{:S(2)}) collective-permute-start(bf16[32,2,32,128]{3,2,1,0:T(8,128)(2,1)S(1)} %collective-permute-done.5.refs_4_), channel_id=1, source_target_pairs={{0,14},{2,0},{4,2},{6,4},{8,6},{10,8},{12,10},{14,12},{1,15},{3,1}... | collective-permute-start | bytes 1572872 | tf_op jit(solution)/shard_map/ppermute | solution.py:24
  95.6 21.7 %collective-permute-start.13 = (bf16[32,2,32,128]{3,2,1,0:T(8,128)(2,1)}, bf16[32,2,32,128]{3,2,1,0:T(8,128)(2,1)}, u32[]{:S(2)}, u32[]{:S(2)}) collective-permute-start(bf16[32,2,32,128]{3,2,1,0:T(8,128)(2,1)} %collective-permute-done.10.refs_5_), channel_id=1, source_target_pairs={{0,2},{2,4},{4,6},{6,8},{8,10},{10,12},{12,14},{14,0},{1,3},{3,5},... | collective-permute-start | bytes 1572872 | tf_op jit(solution)/shard_map/ppermute | solution.py:24
  106.0 2.5 %copy-start.15 = (bf16[32,2,32,128]{3,2,1,0:T(8,128)(2,1)}, bf16[32,2,32,128]{3,2,1,0:T(8,128)(2,1)S(1)}, u32[]{:S(2)}) copy-start(bf16[32,2,32,128]{3,2,1,0:T(8,128)(2,1)S(1)} %collective-permute-done.8.refs_5_) | copy-start | bytes 1572868
  106.0 17.0 %collective-permute-start.12 = (bf16[32,2,32,128]{3,2,1,0:T(8,128)(2,1)}, bf16[32,2,32,128]{3,2,1,0:T(8,128)(2,1)}, u32[]{:S(2)}, u32[]{:S(2)}) collective-permute-start(bf16[32,2,32,128]{3,2,1,0:T(8,128)(2,1)} %collective-permute-done.9.refs_6_), channel_id=1, source_target_pairs={{0,14},{2,0},{4,2},{6,4},{8,6},{10,8},{12,10},{14,12},{1,15},{3,1}... | collective-permute-start | bytes 1572872 | tf_op jit(solution)/shard_map/ppermute | solution.py:24
  108.4 8.9 %copy-start.6 = (bf16[32,8,32,128]{3,2,1,0:T(8,128)(2,1)}, bf16[32,8,32,128]{3,2,1,0:T(8,128)(2,1)S(1)}, u32[]{:S(2)}) copy-start(bf16[32,8,32,128]{3,2,1,0:T(8,128)(2,1)S(1)} %all-to-all-done.1) | copy-start | bytes 6291460
  128.6 32.5 %all-to-all-start.2 = ((bf16[32,8,32,128]{3,2,1,0:T(8,128)(2,1)}), bf16[32,8,32,128]{3,2,1,0:T(8,128)(2,1)S(1)}, u32[]{:S(2)}, u32[]{:S(2)}) async-start(bf16[32,8,32,128]{3,2,1,0:T(8,128)(2,1)} %bitcast.38), calls=%async_computation.2 | async-start | bytes 4194304 | tf_op jit(solution)/shard_map/all_to_all | solution.py:20
  161.1 1.4 copy-start.7
  173.3 3.5 %collective-permute-start.14 = (f32[16,24,128]{2,1,0:T(8,128)S(1)}, f32[16,24,128]{2,1,0:T(8,128)S(1)}, u32[]{:S(2)}, u32[]{:S(2)}) collective-permute-start(f32[16,24,128]{2,1,0:T(8,128)S(1)} %dynamic-slice_bitcast_fusion), channel_id=1, source_target_pairs={{0,1},{1,0},{2,3},{3,2},{4,5},{5,4},{6,7},{7,6},{8,9},{9,8},{10,11... | collective-permute-start | bytes 589832 | tf_op jit(solution)/shard_map/ppermute | solution.py:255
  209.7 5.2 %collective-permute-start.15 = (f32[16,24,128]{2,1,0:T(8,128)S(1)}, f32[16,24,128]{2,1,0:T(8,128)S(1)}, u32[]{:S(2)}, u32[]{:S(2)}) collective-permute-start(f32[16,24,128]{2,1,0:T(8,128)S(1)} %all_to_all.32), channel_id=1, source_target_pairs={{0,1},{1,0},{2,3},{3,2},{4,5},{5,4},{6,7},{7,6},{8,9},{9,8},{10,11... | collective-permute-start | bytes 589832 | tf_op jit(solution)/shard_map/ppermute | solution.py:255
  (3 other events, 2.5 us)

commit v6 on v5

--- a/solution.py
+++ b/solution.py
@@ -8,7 +8,6 @@
 from jax.sharding import Mesh, PartitionSpec as P
 
 PLANE = ("y", "xh", "xl", "c")
-CHIPS = ("y", "xh", "xl")
 GROUPS = 32
 SLABS = 8
 STEP_ROWS = 64
@@ -251,16 +250,9 @@
 
 
 def sum_of_all(x):
-    me = lax.axis_index("c")
-    swap = lambda x: lax.ppermute(x, "c", [(0, 1), (1, 0)])
-    mine = lax.dynamic_index_in_dim(x, me, 0, keepdims=False)
-    others = lax.dynamic_index_in_dim(x, 1 - me, 0, keepdims=False)
-    part = jnp.sum(all_to_all(mine + swap(others), CHIPS), axis=0)
+    part = jnp.sum(all_to_all(x, PLANE), axis=0)
     part = jnp.sum(all_to_all(jnp.broadcast_to(part, (SLABS,) + part.shape), "z"), axis=0)
-    mine = all_to_all(jnp.broadcast_to(part, x.shape[1:]), CHIPS)
-    others = swap(mine)
-    first = me == 0
-    return jnp.stack([jnp.where(first, mine, others), jnp.where(first, others, mine)])
+    return all_to_all(jnp.broadcast_to(part, x.shape), PLANE)
 
 
 def per_device(pair, layernorm_gain, layernorm_bias, proj_weight, product_grad):
@@ -300,7 +292,7 @@
     pairwise_gradient, total = post(
         pair, join(back), gain, bias, ordered, total_rows
     )
-    total = sum_of_all(total.reshape(2, 16, 24, width)) / (rows * 8)
+    total = sum_of_all(total.reshape(GROUPS, 24, width)) / (rows * 8)
     total = total.reshape(total_rows, width)
     proj_grad = jnp.transpose(total[: 4 * width].reshape(4, width, width), (1, 0, 2))
     proj_grad = proj_grad.reshape(width, 4 * width)

time: 217 us -> 216 us (level)
  blocking collectives: 32.8 us -> 75.4 us
  waiting for transfers between devices: 97.4 us -> 67.4 us
  starting transfers between devices: 46 us -> 34.8 us
  local copies, waits for them, and re-layouts: 18 us -> 15.8 us
    all_to_all x3 -> x4, blocking collectives: 32.8 us -> 75.4 us  [all_to_all(): return lax.all_to_all(x, axes, split_axis=0, concat_axis=0, tiled=True)]
    all_to_all x3 -> x2, waiting for transfers between devices: 37.8 us -> 9.89 us  [all_to_all(): return lax.all_to_all(x, axes, split_axis=0, concat_axis=0, tiled=True)]
    ppermute x2 -> x0, starting transfers between devices: 6.62 us -> none  [sum_of_all(): swap = lambda x: lax.ppermute(x, 'c', [(0, 1), (1, 0)])]
    all_to_all x3 -> x2, starting transfers between devices: 17.6 us -> 13 us  [all_to_all(): return lax.all_to_all(x, axes, split_axis=0, concat_axis=0, tiled=True)]
    unnamed x32 -> x26, local copies, waits for them, and re-layouts: 3.85 us -> 1.61 us
  transfers between devices with their start and end apart: 19 -> 16, of which waited for: 11 -> 8; matrix products, arithmetic and copies ran while one was open for 2% -> 2% of each run, Pallas kernels for 4% -> 4%
where the time goes in v6:
time: 216 us; the launch traced here: 215 us
  blocking collectives  75.4 us (35%)
  waiting for transfers between devices  67.4 us (31%)
  starting transfers between devices  34.8 us (16%)
  Pallas kernels  20.5 us (9%)
  local copies, waits for them, and re-layouts  15.8 us (7%)
    all_to_all x4, blocking collectives, all_to_all(): return lax.all_to_all(x, axes, split_axis=0, concat_axis=0, tiled=True)  75.4 us
    ppermute x14, waiting for transfers between devices, shift(): return lax.ppermute(x, 'z', [(i, (i + by) % SLABS) for i in range(SLABS)])  57.5 us
    ppermute x14, starting transfers between devices, shift(): return lax.ppermute(x, 'z', [(i, (i + by) % SLABS) for i in range(SLABS)])  21.8 us
    all_to_all x2, starting transfers between devices, all_to_all(): return lax.all_to_all(x, axes, split_axis=0, concat_axis=0, tiled=True)  13 us
    pallas_call x2, Pallas kernels, products(): pl.pallas_call(functools.partial(product_kernel, half), in_specs=[pl.Bloc...  11.3 us
    all_to_all x2, waiting for transfers between devices, all_to_all(): return lax.all_to_all(x, axes, split_axis=0, concat_axis=0, tiled=True)  9.89 us
    transpose x2, local copies, waits for them, and re-layouts, per_device(): jnp.transpose(x, (2, 1, 0)).reshape(GROUPS, -1, cols, rows)  7.26 us
    pallas_call x1, Pallas kernels, post(): pl.pallas_call(post_kernel, grid=(rows // STEP_ROWS,), in_specs=[tile, pl...  5.98 us
  transfers between devices with their start and end apart: 16, of which 8 were waited for; matrix products, arithmetic and copies ran while one was open for 2% of the time, Pallas kernels for 4%

profile of v6, /device:TPU:1, one launch (start us, length us, event | category | flops | bytes accessed | tf_op | source)
XLA Modules:
  0.0 215.4 jit_solution(17445824775195341749)
XLA Ops:
  0.7 3.3 %copy.17 = bf16[128,32,128]{2,1,0:T(8,128)(2,1)} copy(bf16[128,32,128]{0,1,2:T(8,128)(2,1)} %bitcast.34) | data formatting | bytes 2097152 | tf_op jit(solution)/shard_map/transpose | solution.py:261
  3.9 8.6 %all-to-all-start = ((bf16[32,4,32,128]{3,2,1,0:T(8,128)(2,1)}), bf16[32,4,32,128]{3,2,1,0:T(8,128)(2,1)}, u32[]{:S(2)}, u32[]{:S(2)}) async-start(bf16[32,4,32,128]{3,2,1,0:T(8,128)(2,1)} %bitcast.2), calls=%async_computation | async-start | bytes 2097152 | tf_op jit(solution)/shard_map/all_to_all | solution.py:19
  12.6 3.3 %gated_projections.1 = (bf16[128,32,256]{2,1,0:T(8,128)(2,1)S(1)}, bf16[128,512]{1,0:T(8,128)(2,1)S(1)}) custom-call(bf16[128,32,128]{2,1,0:T(8,128)(2,1)S(1)} %copy-done, f32[1,128]{1,0:T(1,128)S(1)} %bitcast.23, f32[1,128]{1,0:T(1,128)S(1)} %bitcast.25, bf16[128,512]{1,0:T(8,128)(2,1)S(1)} %copy-done.1), custom_call_target="tpu_custom_call" | custom-call | flops 536870912 | bytes 12582912 | tf_op jit(solution)/shard_map/gated_projections/pallas_call | solution.py:66
  15.9 4.0 %copy.18 = bf16[256,32,128]{2,1,0:T(8,128)(2,1)} copy(bf16[256,32,128]{0,1,2:T(8,128)(2,1)S(1)} %bitcast.21) | data formatting | bytes 4194304 | tf_op jit(solution)/shard_map/transpose | solution.py:261
  19.9 9.9 %all-to-all-done = bf16[32,4,32,128]{3,2,1,0:T(8,128)(2,1)} async-done(((bf16[32,4,32,128]{3,2,1,0:T(8,128)(2,1)}), bf16[32,4,32,128]{3,2,1,0:T(8,128)(2,1)}, u32[]{:S(2)}, u32[]{:S(2)}) %all-to-all-start) | async-done | bytes 1048608 | tf_op jit(solution)/shard_map/all_to_all | solution.py:19
  29.8 2.2 %fusion = (bf16[32,2,32,128]{3,2,1,0:T(8,128)(2,1)}, bf16[32,2,32,128]{3,2,1,0:T(8,128)(2,1)}) fusion(bf16[32,4,32,128]{3,2,1,0:T(8,128)(2,1)} %all-to-all-done), kind=kLoop, calls=%fused_computation.3 | loop fusion | bytes 2097152 | tf_op jit(solution)/shard_map/slice | solution.py:271
  32.1 1.6 collective-permute-start.2
  33.7 3.9 %collective-permute-start.3 = (bf16[32,2,32,128]{3,2,1,0:T(8,128)(2,1)}, bf16[32,2,32,128]{3,2,1,0:T(8,128)(2,1)}, u32[]{:S(2)}, u32[]{:S(2)}) collective-permute-start(bf16[32,2,32,128]{3,2,1,0:T(8,128)(2,1)} %get-tuple-element.25.refs_0_), channel_id=1, source_target_pairs={{0,14},{2,0},{4,2},{6,4},{8,6},{10,8},{12,10},{14,12},{1,15},{3,1}... | collective-permute-start | bytes 1572872 | tf_op jit(solution)/shard_map/ppermute | solution.py:23
  37.6 4.3 %all-to-all-start.1 = ((bf16[32,8,32,128]{3,2,1,0:T(8,128)(2,1)}), bf16[32,8,32,128]{3,2,1,0:T(8,128)(2,1)S(1)}, u32[]{:S(2)}, u32[]{:S(2)}) async-start(bf16[32,8,32,128]{3,2,1,0:T(8,128)(2,1)} %bitcast.30), calls=%async_computation.1 | async-start | bytes 4194304 | tf_op jit(solution)/shard_map/all_to_all | solution.py:19
  42.1 2.7 %collective-permute-start.1 = (bf16[32,2,32,128]{3,2,1,0:T(8,128)(2,1)}, bf16[32,2,32,128]{3,2,1,0:T(8,128)(2,1)S(1)}, u32[]{:S(2)}, u32[]{:S(2)}) collective-permute-start(bf16[32,2,32,128]{3,2,1,0:T(8,128)(2,1)} %get-tuple-element.24.refs_0_), channel_id=1, source_target_pairs={{0,14},{2,0},{4,2},{6,4},{8,6},{10,8},{12,10},{14,12},{1,15},{3,1}... | collective-permute-start | bytes 1572872 | tf_op jit(solution)/shard_map/ppermute | solution.py:23
  44.7 5.2 %collective-permute-done.2.refs_1_ = bf16[32,2,32,128]{3,2,1,0:T(8,128)(2,1)} collective-permute-done((bf16[32,2,32,128]{3,2,1,0:T(8,128)(2,1)}, bf16[32,2,32,128]{3,2,1,0:T(8,128)(2,1)}, u32[]{:S(2)}, u32[]{:S(2)}) %collective-permute-start.2) | collective-permute-done | bytes 524320 | tf_op jit(solution)/shard_map/ppermute | solution.py:23
  49.9 2.7 %collective-permute-start.7 = (bf16[32,2,32,128]{3,2,1,0:T(8,128)(2,1)}, bf16[32,2,32,128]{3,2,1,0:T(8,128)(2,1)S(1)}, u32[]{:S(2)}, u32[]{:S(2)}) collective-permute-start(bf16[32,2,32,128]{3,2,1,0:T(8,128)(2,1)} %collective-permute-done.3.refs_2_), channel_id=1, source_target_pairs={{0,14},{2,0},{4,2},{6,4},{8,6},{10,8},{12,10},{14,12},{1,15},{3,1}... | collective-permute-start | bytes 1572872 | tf_op jit(solution)/shard_map/ppermute | solution.py:23
  52.6 8.4 %collective-permute-done.refs_1_ = bf16[32,2,32,128]{3,2,1,0:T(8,128)(2,1)S(1)} collective-permute-done((bf16[32,2,32,128]{3,2,1,0:T(8,128)(2,1)}, bf16[32,2,32,128]{3,2,1,0:T(8,128)(2,1)S(1)}, u32[]{:S(2)}, u32[]{:S(2)}) %collective-permute-start) | collective-permute-done | bytes 524320 | tf_op jit(solution)/shard_map/ppermute | solution.py:23
  61.1 2.7 %collective-permute-start.5 = (bf16[32,2,32,128]{3,2,1,0:T(8,128)(2,1)S(1)}, bf16[32,2,32,128]{3,2,1,0:T(8,128)(2,1)S(1)}, u32[]{:S(2)}, u32[]{:S(2)}) collective-permute-start(bf16[32,2,32,128]{3,2,1,0:T(8,128)(2,1)S(1)} %collective-permute-done.1.refs_2_), channel_id=1, source_target_pairs={{0,14},{2,0},{4,2},{6,4},{8,6},{10,8},{12,10},{14,12},{1,15},{3,1}... | collective-permute-start | bytes 1572872 | tf_op jit(solution)/shard_map/ppermute | solution.py:23
  63.8 8.5 %collective-permute-done.6.refs_3_ = bf16[32,2,32,128]{3,2,1,0:T(8,128)(2,1)S(1)} collective-permute-done((bf16[32,2,32,128]{3,2,1,0:T(8,128)(2,1)}, bf16[32,2,32,128]{3,2,1,0:T(8,128)(2,1)S(1)}, u32[]{:S(2)}, u32[]{:S(2)}) %collective-permute-start.6) | collective-permute-done | bytes 524320 | tf_op jit(solution)/shard_map/ppermute | solution.py:23
  72.3 0.8 copy-done.5
  73.1 2.7 %collective-permute-start.11 = (bf16[32,2,32,128]{3,2,1,0:T(8,128)(2,1)S(1)}, bf16[32,2,32,128]{3,2,1,0:T(8,128)(2,1)S(1)}, u32[]{:S(2)}, u32[]{:S(2)}) collective-permute-start(bf16[32,2,32,128]{3,2,1,0:T(8,128)(2,1)S(1)} %collective-permute-done.7.refs_4_), channel_id=1, source_target_pairs={{0,14},{2,0},{4,2},{6,4},{8,6},{10,8},{12,10},{14,12},{1,15},{3,1}... | collective-permute-start | bytes 1572872 | tf_op jit(solution)/shard_map/ppermute | solution.py:23
  75.8 7.8 %collective-permute-done.4.refs_3_ = bf16[32,2,32,128]{3,2,1,0:T(8,128)(2,1)S(1)} collective-permute-done((bf16[32,2,32,128]{3,2,1,0:T(8,128)(2,1)S(1)}, bf16[32,2,32,128]{3,2,1,0:T(8,128)(2,1)S(1)}, u32[]{:S(2)}, u32[]{:S(2)}) %collective-permute-start.4) | collective-permute-done | bytes 524320 | tf_op jit(solution)/shard_map/ppermute | solution.py:23
  83.8 2.7 %collective-permute-start.9 = (bf16[32,2,32,128]{3,2,1,0:T(8,128)(2,1)S(1)}, bf16[32,2,32,128]{3,2,1,0:T(8,128)(2,1)}, u32[]{:S(2)}, u32[]{:S(2)}) collective-permute-start(bf16[32,2,32,128]{3,2,1,0:T(8,128)(2,1)S(1)} %collective-permute-done.5.refs_4_), channel_id=1, source_target_pairs={{0,14},{2,0},{4,2},{6,4},{8,6},{10,8},{12,10},{14,12},{1,15},{3,1}... | collective-permute-start | bytes 1572872 | tf_op jit(solution)/shard_map/ppermute | solution.py:23
  86.5 8.4 %collective-permute-done.10.refs_5_ = bf16[32,2,32,128]{3,2,1,0:T(8,128)(2,1)} collective-permute-done((bf16[32,2,32,128]{3,2,1,0:T(8,128)(2,1)S(1)}, bf16[32,2,32,128]{3,2,1,0:T(8,128)(2,1)}, u32[]{:S(2)}, u32[]{:S(2)}) %collective-permute-start.10) | collective-permute-done | bytes 524320 | tf_op jit(solution)/shard_map/ppermute | solution.py:23
  94.9 0.8 copy-done.7
  95.7 10.3 %collective-permute-done.8.refs_5_ = bf16[32,2,32,128]{3,2,1,0:T(8,128)(2,1)S(1)} collective-permute-done((bf16[32,2,32,128]{3,2,1,0:T(8,128)(2,1)S(1)}, bf16[32,2,32,128]{3,2,1,0:T(8,128)(2,1)S(1)}, u32[]{:S(2)}, u32[]{:S(2)}) %collective-permute-start.8) | collective-permute-done | bytes 524320 | tf_op jit(solution)/shard_map/ppermute | solution.py:23
  106.0 2.4 %collective-permute-start.12 = (bf16[32,2,32,128]{3,2,1,0:T(8,128)(2,1)}, bf16[32,2,32,128]{3,2,1,0:T(8,128)(2,1)}, u32[]{:S(2)}, u32[]{:S(2)}) collective-permute-start(bf16[32,2,32,128]{3,2,1,0:T(8,128)(2,1)} %collective-permute-done.9.refs_6_), channel_id=1, source_target_pairs={{0,14},{2,0},{4,2},{6,4},{8,6},{10,8},{12,10},{14,12},{1,15},{3,1}... | collective-permute-start | bytes 1572872 | tf_op jit(solution)/shard_map/ppermute | solution.py:23
  108.5 8.9 %collective-permute-done.13.refs_7_ = bf16[32,2,32,128]{3,2,1,0:T(8,128)(2,1)} collective-permute-done((bf16[32,2,32,128]{3,2,1,0:T(8,128)(2,1)}, bf16[32,2,32,128]{3,2,1,0:T(8,128)(2,1)}, u32[]{:S(2)}, u32[]{:S(2)}) %collective-permute-start.13) | collective-permute-done | bytes 524320 | tf_op jit(solution)/shard_map/ppermute | solution.py:23
  117.3 5.6 %triangle_products.2.refs_8_ = bf16[32,4,2,32,128]{4,3,2,1,0:T(8,128)(2,1)} custom-call(s32[1]{0:T(128)} %bitcast.slab_ref, bf16[32,4,2,32,128]{4,3,2,1,0:T(8,128)(2,1)} %bitcast.27, bf16[32,2,32,128]{3,2,1,0:T(8,128)(2,1)} %get-tuple-element.25.refs_0_, bf16[32,2,32,128]{3,2,1,0:T(8,128)(2,1)} %collective-permute-done.2.refs_1_, ...), custom_call_target="tpu_custom_call" | custom-call | flops 1073741824 | bytes 12582912 | tf_op jit(solution)/shard_map/triangle_products/pallas_call | solution.py:229
  123.0 5.6 %triangle_products.3 = bf16[32,4,2,32,128]{4,3,2,1,0:T(8,128)(2,1)} custom-call(s32[1]{0:T(128)} %bitcast.slab_ref, bf16[32,4,2,32,128]{4,3,2,1,0:T(8,128)(2,1)} %bitcast.28, bf16[32,2,32,128]{3,2,1,0:T(8,128)(2,1)} %get-tuple-element.24.refs_0_, bf16[32,2,32,128]{3,2,1,0:T(8,128)(2,1)} %copy-done.8, ...), custom_call_target="tpu_custom_call", output_to_operand_aliasing={{}: (10, {})} | custom-call | flops 1073741824 | bytes 12582912 | tf_op jit(solution)/shard_map/triangle_products/pallas_call | solution.py:229
  128.6 33.8 %all_to_all.30 = bf16[32,8,32,128]{3,2,1,0:T(8,128)(2,1)} all-to-all(bf16[32,8,32,128]{3,2,1,0:T(8,128)(2,1)} %bitcast.29), channel_id=1, replica_groups=mesh['y'=4,'xh'=2,'xl'=2,'z'=8,'c'=2] {'y','xh','xl','c'}, dimensions={0} | all-to-all | bytes 4194304 | tf_op jit(solution)/shard_map/all_to_all | solution.py:19
  162.4 3.9 %copy.19 = bf16[256,32,128]{0,1,2:T(8,128)(2,1)S(1)} copy(bf16[256,32,128]{2,1,0:T(8,128)(2,1)} %bitcast.31) | data formatting | bytes 4194304 | tf_op jit(solution)/shard_map/reshape | solution.py:262
  166.4 6.0 %input_gradients.1 = (bf16[128,32,128]{2,1,0:T(8,128)(2,1)}, f32[768,128]{1,0:T(8,128)S(1)}) custom-call(bf16[128,32,128]{2,1,0:T(8,128)(2,1)S(1)} %copy-done, bf16[128,32,256]{2,1,0:T(8,128)(2,1)S(1)} %bitcast.20, f32[1,128]{1,0:T(1,128)S(1)} %bitcast.24, f32[1,128]{1,0:T(1,128)S(1)} %bitcast.26, bf16[128,512]{1,0:T(8,128)(2,1)S(1)} %get-tuple-element.38.ordered_ref), custom_call_target="tpu_custom_call" | custom-call | flops 1610612736 | bytes 20971520 | tf_op jit(solution)/shard_map/input_gradients/pallas_call | solution.py:139
  172.3 13.6 %all_to_all.31 = f32[32,24,128]{2,1,0:T(8,128)S(1)} all-to-all(f32[32,24,128]{2,1,0:T(8,128)S(1)} %bitcast.22), channel_id=1, replica_groups=mesh['y'=4,'xh'=2,'xl'=2,'z'=8,'c'=2] {'y','xh','xl','c'}, dimensions={0} | all-to-all | bytes 786432 | tf_op jit(solution)/shard_map/all_to_all | solution.py:19
  186.0 12.5 %all_to_all.32 = f32[8,24,128]{2,1,0:T(8,128)S(1)} all-to-all(f32[8,24,128]{2,1,0:T(8,128)S(1)} %broadcast_in_dim.6), channel_id=1, replica_groups=mesh['y'=4,'xh'=2,'xl'=2,'z'=8,'c'=2] {'z'}, dimensions={0} | all-to-all | bytes 196608 | tf_op jit(solution)/shard_map/all_to_all | solution.py:19
  198.6 15.4 %all_to_all.33 = f32[32,24,128]{2,1,0:T(8,128)S(1)} all-to-all(f32[32,24,128]{2,1,0:T(8,128)S(1)} %broadcast_in_dim.7), channel_id=1, replica_groups=mesh['y'=4,'xh'=2,'xl'=2,'z'=8,'c'=2] {'y','xh','xl','c'}, dimensions={0} | all-to-all | bytes 786432 | tf_op jit(solution)/shard_map/all_to_all | solution.py:19
  (47 shorter events, 1.9 us)
Async XLA Ops:
  0.6 12.0 %copy-start = (bf16[128,32,128]{2,1,0:T(8,128)(2,1)S(1)}, bf16[128,32,128]{2,1,0:T(8,128)(2,1)}, u32[]{:S(2)}) copy-start(bf16[128,32,128]{2,1,0:T(8,128)(2,1)} %pair_ref.3) | copy-start | bytes 3145732
  0.6 12.0 %copy-start.1 = (bf16[128,512]{1,0:T(8,128)(2,1)S(1)}, bf16[128,512]{1,0:T(8,128)(2,1)}, u32[]{:S(2)}) copy-start(bf16[128,512]{1,0:T(8,128)(2,1)} %weight_ref.1) | copy-start | bytes 393220
  0.7 12.0 %copy-start.2 = (f32[128]{0:T(128)S(1)}, f32[128]{0:T(128)}, u32[]{:S(2)}) copy-start(f32[128]{0:T(128)} %param.6) | copy-start | bytes 1540
  0.7 12.0 %copy-start.3 = (f32[128]{0:T(128)S(1)}, f32[128]{0:T(128)}, u32[]{:S(2)}) copy-start(f32[128]{0:T(128)} %param.7) | copy-start | bytes 1540
  3.9 25.9 %all-to-all-start = ((bf16[32,4,32,128]{3,2,1,0:T(8,128)(2,1)}), bf16[32,4,32,128]{3,2,1,0:T(8,128)(2,1)}, u32[]{:S(2)}, u32[]{:S(2)}) async-start(bf16[32,4,32,128]{3,2,1,0:T(8,128)(2,1)} %bitcast.2), calls=%async_computation | async-start | bytes 2097152 | tf_op jit(solution)/shard_map/all_to_all | solution.py:19
  32.1 17.9 %collective-permute-start.2 = (bf16[32,2,32,128]{3,2,1,0:T(8,128)(2,1)}, bf16[32,2,32,128]{3,2,1,0:T(8,128)(2,1)}, u32[]{:S(2)}, u32[]{:S(2)}) collective-permute-start(bf16[32,2,32,128]{3,2,1,0:T(8,128)(2,1)} %get-tuple-element.25.refs_0_), channel_id=1, source_target_pairs={{0,2},{2,4},{4,6},{6,8},{8,10},{10,12},{12,14},{14,0},{1,3},{3,5},... | collective-permute-start | bytes 1572872 | tf_op jit(solution)/shard_map/ppermute | solution.py:23
  33.7 16.2 %collective-permute-start.3 = (bf16[32,2,32,128]{3,2,1,0:T(8,128)(2,1)}, bf16[32,2,32,128]{3,2,1,0:T(8,128)(2,1)}, u32[]{:S(2)}, u32[]{:S(2)}) collective-permute-start(bf16[32,2,32,128]{3,2,1,0:T(8,128)(2,1)} %get-tuple-element.25.refs_0_), channel_id=1, source_target_pairs={{0,14},{2,0},{4,2},{6,4},{8,6},{10,8},{12,10},{14,12},{1,15},{3,1}... | collective-permute-start | bytes 1572872 | tf_op jit(solution)/shard_map/ppermute | solution.py:23
  37.6 70.8 %all-to-all-start.1 = ((bf16[32,8,32,128]{3,2,1,0:T(8,128)(2,1)}), bf16[32,8,32,128]{3,2,1,0:T(8,128)(2,1)S(1)}, u32[]{:S(2)}, u32[]{:S(2)}) async-start(bf16[32,8,32,128]{3,2,1,0:T(8,128)(2,1)} %bitcast.30), calls=%async_computation.1 | async-start | bytes 4194304 | tf_op jit(solution)/shard_map/all_to_all | solution.py:19
  42.0 19.1 %collective-permute-start = (bf16[32,2,32,128]{3,2,1,0:T(8,128)(2,1)}, bf16[32,2,32,128]{3,2,1,0:T(8,128)(2,1)S(1)}, u32[]{:S(2)}, u32[]{:S(2)}) collective-permute-start(bf16[32,2,32,128]{3,2,1,0:T(8,128)(2,1)} %get-tuple-element.24.refs_0_), channel_id=1, source_target_pairs={{0,2},{2,4},{4,6},{6,8},{8,10},{10,12},{12,14},{14,0},{1,3},{3,5},... | collective-permute-start | bytes 1572872 | tf_op jit(solution)/shard_map/ppermute | solution.py:23
  42.1 19.0 %collective-permute-start.1 = (bf16[32,2,32,128]{3,2,1,0:T(8,128)(2,1)}, bf16[32,2,32,128]{3,2,1,0:T(8,128)(2,1)S(1)}, u32[]{:S(2)}, u32[]{:S(2)}) collective-permute-start(bf16[32,2,32,128]{3,2,1,0:T(8,128)(2,1)} %get-tuple-element.24.refs_0_), channel_id=1, source_target_pairs={{0,14},{2,0},{4,2},{6,4},{8,6},{10,8},{12,10},{14,12},{1,15},{3,1}... | collective-permute-start | bytes 1572872 | tf_op jit(solution)/shard_map/ppermute | solution.py:23
  49.9 22.4 %collective-permute-start.6 = (bf16[32,2,32,128]{3,2,1,0:T(8,128)(2,1)}, bf16[32,2,32,128]{3,2,1,0:T(8,128)(2,1)S(1)}, u32[]{:S(2)}, u32[]{:S(2)}) collective-permute-start(bf16[32,2,32,128]{3,2,1,0:T(8,128)(2,1)} %collective-permute-done.2.refs_1_), channel_id=1, source_target_pairs={{0,2},{2,4},{4,6},{6,8},{8,10},{10,12},{12,14},{14,0},{1,3},{3,5},... | collective-permute-start | bytes 1572872 | tf_op jit(solution)/shard_map/ppermute | solution.py:23
  49.9 22.4 %collective-permute-start.7 = (bf16[32,2,32,128]{3,2,1,0:T(8,128)(2,1)}, bf16[32,2,32,128]{3,2,1,0:T(8,128)(2,1)S(1)}, u32[]{:S(2)}, u32[]{:S(2)}) collective-permute-start(bf16[32,2,32,128]{3,2,1,0:T(8,128)(2,1)} %collective-permute-done.3.refs_2_), channel_id=1, source_target_pairs={{0,14},{2,0},{4,2},{6,4},{8,6},{10,8},{12,10},{14,12},{1,15},{3,1}... | collective-permute-start | bytes 1572872 | tf_op jit(solution)/shard_map/ppermute | solution.py:23
  61.0 34.6 %copy-start.8 = (bf16[32,2,32,128]{3,2,1,0:T(8,128)(2,1)}, bf16[32,2,32,128]{3,2,1,0:T(8,128)(2,1)S(1)}, u32[]{:S(2)}) copy-start(bf16[32,2,32,128]{3,2,1,0:T(8,128)(2,1)S(1)} %collective-permute-done.refs_1_) | copy-start | bytes 1572868
  61.1 44.9 %copy-start.9 = (bf16[32,2,32,128]{3,2,1,0:T(8,128)(2,1)}, bf16[32,2,32,128]{3,2,1,0:T(8,128)(2,1)S(1)}, u32[]{:S(2)}) copy-start(bf16[32,2,32,128]{3,2,1,0:T(8,128)(2,1)S(1)} %collective-permute-done.1.refs_2_) | copy-start | bytes 1572868
  61.1 22.5 %collective-permute-start.4 = (bf16[32,2,32,128]{3,2,1,0:T(8,128)(2,1)S(1)}, bf16[32,2,32,128]{3,2,1,0:T(8,128)(2,1)S(1)}, u32[]{:S(2)}, u32[]{:S(2)}) collective-permute-start(bf16[32,2,32,128]{3,2,1,0:T(8,128)(2,1)S(1)} %collective-permute-done.refs_1_), channel_id=1, source_target_pairs={{0,2},{2,4},{4,6},{6,8},{8,10},{10,12},{12,14},{14,0},{1,3},{3,5},... | collective-permute-start | bytes 1572872 | tf_op jit(solution)/shard_map/ppermute | solution.py:23
  61.1 22.4 %collective-permute-start.5 = (bf16[32,2,32,128]{3,2,1,0:T(8,128)(2,1)S(1)}, bf16[32,2,32,128]{3,2,1,0:T(8,128)(2,1)S(1)}, u32[]{:S(2)}, u32[]{:S(2)}) collective-permute-start(bf16[32,2,32,128]{3,2,1,0:T(8,128)(2,1)S(1)} %collective-permute-done.1.refs_2_), channel_id=1, source_target_pairs={{0,14},{2,0},{4,2},{6,4},{8,6},{10,8},{12,10},{14,12},{1,15},{3,1}... | collective-permute-start | bytes 1572872 | tf_op jit(solution)/shard_map/ppermute | solution.py:23
  72.3 0.8 copy-start.5
  73.1 21.8 %copy-start.6 = (bf16[32,2,32,128]{3,2,1,0:T(8,128)(2,1)}, bf16[32,2,32,128]{3,2,1,0:T(8,128)(2,1)S(1)}, u32[]{:S(2)}) copy-start(bf16[32,2,32,128]{3,2,1,0:T(8,128)(2,1)S(1)} %collective-permute-done.7.refs_4_) | copy-start | bytes 1572868
  73.1 21.8 %collective-permute-start.10 = (bf16[32,2,32,128]{3,2,1,0:T(8,128)(2,1)S(1)}, bf16[32,2,32,128]{3,2,1,0:T(8,128)(2,1)}, u32[]{:S(2)}, u32[]{:S(2)}) collective-permute-start(bf16[32,2,32,128]{3,2,1,0:T(8,128)(2,1)S(1)} %collective-permute-done.6.refs_3_), channel_id=1, source_target_pairs={{0,2},{2,4},{4,6},{6,8},{8,10},{10,12},{12,14},{14,0},{1,3},{3,5},... | collective-permute-start | bytes 1572872 | tf_op jit(solution)/shard_map/ppermute | solution.py:23
  73.1 21.8 %collective-permute-start.11 = (bf16[32,2,32,128]{3,2,1,0:T(8,128)(2,1)S(1)}, bf16[32,2,32,128]{3,2,1,0:T(8,128)(2,1)S(1)}, u32[]{:S(2)}, u32[]{:S(2)}) collective-permute-start(bf16[32,2,32,128]{3,2,1,0:T(8,128)(2,1)S(1)} %collective-permute-done.7.refs_4_), channel_id=1, source_target_pairs={{0,14},{2,0},{4,2},{6,4},{8,6},{10,8},{12,10},{14,12},{1,15},{3,1}... | collective-permute-start | bytes 1572872 | tf_op jit(solution)/shard_map/ppermute | solution.py:23
  83.5 22.5 %copy-start.10 = (bf16[32,2,32,128]{3,2,1,0:T(8,128)(2,1)}, bf16[32,2,32,128]{3,2,1,0:T(8,128)(2,1)S(1)}, u32[]{:S(2)}) copy-start(bf16[32,2,32,128]{3,2,1,0:T(8,128)(2,1)S(1)} %collective-permute-done.4.refs_3_) | copy-start | bytes 1572868
  83.5 24.9 %copy-start.11 = (bf16[32,2,32,128]{3,2,1,0:T(8,128)(2,1)}, bf16[32,2,32,128]{3,2,1,0:T(8,128)(2,1)S(1)}, u32[]{:S(2)}) copy-start(bf16[32,2,32,128]{3,2,1,0:T(8,128)(2,1)S(1)} %collective-permute-done.5.refs_4_) | copy-start | bytes 1572868
  83.5 22.5 %collective-permute-start.8 = (bf16[32,2,32,128]{3,2,1,0:T(8,128)(2,1)S(1)}, bf16[32,2,32,128]{3,2,1,0:T(8,128)(2,1)S(1)}, u32[]{:S(2)}, u32[]{:S(2)}) collective-permute-start(bf16[32,2,32,128]{3,2,1,0:T(8,128)(2,1)S(1)} %collective-permute-done.4.refs_3_), channel_id=1, source_target_pairs={{0,2},{2,4},{4,6},{6,8},{8,10},{10,12},{12,14},{14,0},{1,3},{3,5},... | collective-permute-start | bytes 1572872 | tf_op jit(solution)/shard_map/ppermute | solution.py:23
  83.8 22.2 %collective-permute-start.9 = (bf16[32,2,32,128]{3,2,1,0:T(8,128)(2,1)S(1)}, bf16[32,2,32,128]{3,2,1,0:T(8,128)(2,1)}, u32[]{:S(2)}, u32[]{:S(2)}) collective-permute-start(bf16[32,2,32,128]{3,2,1,0:T(8,128)(2,1)S(1)} %collective-permute-done.5.refs_4_), channel_id=1, source_target_pairs={{0,14},{2,0},{4,2},{6,4},{8,6},{10,8},{12,10},{14,12},{1,15},{3,1}... | collective-permute-start | bytes 1572872 | tf_op jit(solution)/shard_map/ppermute | solution.py:23
  94.9 0.8 copy-start.7
  95.7 21.7 %collective-permute-start.13 = (bf16[32,2,32,128]{3,2,1,0:T(8,128)(2,1)}, bf16[32,2,32,128]{3,2,1,0:T(8,128)(2,1)}, u32[]{:S(2)}, u32[]{:S(2)}) collective-permute-start(bf16[32,2,32,128]{3,2,1,0:T(8,128)(2,1)} %collective-permute-done.10.refs_5_), channel_id=1, source_target_pairs={{0,2},{2,4},{4,6},{6,8},{8,10},{10,12},{12,14},{14,0},{1,3},{3,5},... | collective-permute-start | bytes 1572872 | tf_op jit(solution)/shard_map/ppermute | solution.py:23
  106.0 2.5 %copy-start.12 = (bf16[32,2,32,128]{3,2,1,0:T(8,128)(2,1)}, bf16[32,2,32,128]{3,2,1,0:T(8,128)(2,1)S(1)}, u32[]{:S(2)}) copy-start(bf16[32,2,32,128]{3,2,1,0:T(8,128)(2,1)S(1)} %collective-permute-done.8.refs_5_) | copy-start | bytes 1572868
  106.0 17.0 %collective-permute-start.12 = (bf16[32,2,32,128]{3,2,1,0:T(8,128)(2,1)}, bf16[32,2,32,128]{3,2,1,0:T(8,128)(2,1)}, u32[]{:S(2)}, u32[]{:S(2)}) collective-permute-start(bf16[32,2,32,128]{3,2,1,0:T(8,128)(2,1)} %collective-permute-done.9.refs_6_), channel_id=1, source_target_pairs={{0,14},{2,0},{4,2},{6,4},{8,6},{10,8},{12,10},{14,12},{1,15},{3,1}... | collective-permute-start | bytes 1572872 | tf_op jit(solution)/shard_map/ppermute | solution.py:23
  108.5 8.9 %copy-start.4 = (bf16[32,8,32,128]{3,2,1,0:T(8,128)(2,1)}, bf16[32,8,32,128]{3,2,1,0:T(8,128)(2,1)S(1)}, u32[]{:S(2)}) copy-start(bf16[32,8,32,128]{3,2,1,0:T(8,128)(2,1)S(1)} %all-to-all-done.1) | copy-start | bytes 6291460

commit v7 on v6

--- a/solution.py
+++ b/solution.py
@@ -8,8 +8,10 @@
 from jax.sharding import Mesh, PartitionSpec as P
 
 PLANE = ("y", "xh", "xl", "c")
+CHIPS = ("y", "xh", "xl")
 GROUPS = 32
 SLABS = 8
+OFFSETS = (0, 7, 1, 6, 2, 5, 3, 4)
 STEP_ROWS = 64
 VMEM_LIMIT = 32 * 1024 * 1024
 PRODUCT_LIMIT = 58 * 1024 * 1024
@@ -160,93 +162,106 @@
     )(pair, back, gain, bias, ordered)
 
 
-def product_kernel(half, slab_ref, sides_hbm, *refs):
-    block_hbm = refs[:SLABS]
-    out_hbm, sides, blocks, out, grads, sems, out_sems = refs[SLABS + half :]
-    here = pl.ds(2 * half, 2)
+def product_kernel(slab_ref, sides_hbm, *refs):
+    block_hbm = refs[: 2 * SLABS]
+    out_hbm, sides, blocks, out, grads, sems, side_sems, out_sems = refs[2 * SLABS :]
     loads = [
         pltpu.make_async_copy(ref, blocks.at[n], sems.at[n]) for n, ref in enumerate(block_hbm)
     ]
-    loads.append(pltpu.make_async_copy(sides_hbm.at[:, here], sides, sems.at[SLABS]))
-    for load in loads:
-        load.start()
-
-    def place(channel, offset, piece):
-        where = lax.rem(slab_ref[0] + offset, SLABS)
+    side_loads = [
+        pltpu.make_async_copy(
+            sides_hbm.at[:, pl.ds(2 * half, 2)], sides.at[half], side_sems.at[half]
+        )
+        for half in range(2)
+    ]
+    for half in range(2):
+        for load in loads[SLABS * half : SLABS * half + SLABS]:
+            load.start()
+        side_loads[half].start()
+
+    def place(channel, n):
+        where = lax.rem(slab_ref[0] + OFFSETS[n % SLABS], SLABS)
         for x in range(2):
             rows = pl.ds(pl.multiple_of(512 * x + 64 * where, 64), 64)
             for r in range(8):
                 grads[channel, rows, 128 * r : 128 * r + 128] = jnp.concatenate(
-                    [piece(4 * r + 2 * x), piece(4 * r + 2 * x + 1)], axis=0
+                    [blocks[n, 4 * r + 2 * x, channel], blocks[n, 4 * r + 2 * x + 1, channel]],
+                    axis=0,
                 )
 
-    def whole(channel, side):
+    def whole(half, channel, side):
         return jnp.concatenate(
             [
-                jnp.concatenate([sides[4 * r + c, side, channel] for c in range(4)], axis=0)
+                jnp.concatenate(
+                    [sides[half, 4 * r + c, side, channel] for c in range(4)], axis=0
+                )
                 for r in range(8)
             ],
             axis=1,
         )
 
-    for n, offset in enumerate((0, 7, 1, 6, 2, 5, 3, 4)):
-        loads[n].wait()
+    stores = []
+    for half in range(2):
+        for n in range(SLABS * half, SLABS * half + SLABS):
+            loads[n].wait()
+            for channel in range(2):
+                place(channel, n)
+        side_loads[half].wait()
         for channel in range(2):
-            place(channel, offset, lambda d: blocks[n, d, channel])
-    loads[SLABS].wait()
-    stores = []
-    for channel in range(2):
-        first = jnp.dot(whole(channel, 1), grads[channel], preferred_element_type=jnp.float32)
-        second = lax.dot_general(
-            whole(channel, 0),
-            grads[channel],
-            (((1,), (1,)), ((), ())),
-            preferred_element_type=jnp.float32,
-        )
-        for side, value in enumerate((first, second)):
-            value = value.astype(jnp.bfloat16)
-            for r in range(8):
-                for c in range(4):
-                    out[channel, 4 * r + c, side] = value[
-                        32 * c : 32 * c + 32, 128 * r : 128 * r + 128
-                    ]
-        stores.append(
-            pltpu.make_async_copy(
-                out.at[channel], out_hbm.at[:, here, channel], out_sems.at[channel]
-            )
-        )
-        stores[-1].start()
+            first = jnp.dot(
+                whole(half, channel, 1), grads[channel], preferred_element_type=jnp.float32
+            )
+            second = lax.dot_general(
+                whole(half, channel, 0),
+                grads[channel],
+                (((1,), (1,)), ((), ())),
+                preferred_element_type=jnp.float32,
+            )
+            at = 2 * half + channel
+            for side, value in enumerate((first, second)):
+                value = value.astype(jnp.bfloat16)
+                for r in range(8):
+                    for c in range(4):
+                        out[at, 4 * r + c, side] = value[
+                            32 * c : 32 * c + 32, 128 * r : 128 * r + 128
+                        ]
+            stores.append(
+                pltpu.make_async_copy(
+                    out.at[at], out_hbm.at[:, pl.ds(2 * half, 2), channel], out_sems.at[at]
+                )
+            )
+            stores[-1].start()
     for store in stores:
         store.wait()
 
 
-def products(slab, sides, half, blocks, earlier=None):
+def products(slab, sides, blocks):
     groups, pairs, depth, width = sides.shape
     channels = pairs // 4
     sides = sides.reshape(groups, 4, channels, depth, width)
-    operands = [slab, sides, *blocks] + ([] if earlier is None else [earlier])
     bf16 = lambda *shape: pltpu.VMEM(shape, jnp.bfloat16)
-    return pl.pallas_call(
-        functools.partial(product_kernel, half),
+    out = pl.pallas_call(
+        product_kernel,
         in_specs=[pl.BlockSpec(memory_space=pltpu.SMEM)]
-        + [pl.BlockSpec(memory_space=pltpu.HBM)] * (len(operands) - 1),
-        out_specs=pl.BlockSpec(memory_space=pltpu.HBM),
+        + [pl.BlockSpec(memory_space=pl.ANY)] * (1 + len(blocks)),
+        out_specs=pl.BlockSpec(memory_space=pl.ANY),
         out_shape=jax.ShapeDtypeStruct(sides.shape, jnp.bfloat16),
         scratch_shapes=[
-            bf16(groups, 2, channels, depth, width),
-            bf16(SLABS, groups, channels, depth, width),
-            bf16(channels, groups, 2, depth, width),
+            bf16(2, groups, 2, channels, depth, width),
+            bf16(2 * SLABS, groups, channels, depth, width),
+            bf16(2 * channels, groups, 2, depth, width),
             bf16(channels, 1024, 1024),
-            pltpu.SemaphoreType.DMA((SLABS + 1,)),
+            pltpu.SemaphoreType.DMA((2 * SLABS,)),
             pltpu.SemaphoreType.DMA((2,)),
-        ],
-        input_output_aliases={} if earlier is None else {len(operands) - 1: 0},
+            pltpu.SemaphoreType.DMA((4,)),
+        ],
         compiler_params=pltpu.CompilerParams(vmem_limit_bytes=PRODUCT_LIMIT),
         cost_estimate=pl.CostEstimate(
-            flops=4 * channels * 128 * 1024 * 1024, bytes_accessed=12 << 20, transcendentals=0
+            flops=16 * 128 * 1024 * 1024, bytes_accessed=12 << 20, transcendentals=0
         ),
         name="triangle_products",
-    )(*operands)
+    )(slab, sides, *blocks)
+    return out.reshape(groups, pairs, depth, width)
 
 
 def sum_of_all(x):
@@ -268,7 +283,8 @@
     after = lambda wanted, done: barrier((wanted, done))[0]
     own = all_to_all(split(product_grad), PLANE)
     sides, ordered = pre(pair, gain, bias, proj_weight)
-    a0, b0, sides = barrier((own[:, :2], own[:, 2:], split(sides)))
+    a0, own = barrier((own[:, :2], own))
+    b0, sides = barrier((own[:, 2:], split(sides)))
     sides = all_to_all(sides, PLANE)
     a1 = both((a0, a0))
     b1 = both((b0, b0))
@@ -284,9 +300,8 @@
     a4 = shift(a3[0], 1)
     b3 = after(b3, a3)
     b4 = shift(b3[1], -1)
-    back = products(slab, sides, 0, [a0, *a1, *a2, *a3, a4])
-    back = products(slab, sides, 1, [b0, *b1, *b2, *b3, b4], back)
-    back = all_to_all(back.reshape(sides.shape), PLANE)
+    blocks = [a0, *a1, *a2, *a3, a4, b0, *b1, *b2, *b3, b4]
+    back = all_to_all(products(slab, sides, blocks), PLANE)
 
     total_rows = 24 * GROUPS
     pairwise_gradient, total = post(

time: 216 us -> 216 us (level)
    pallas_call x2 -> x1, Pallas kernels: 11.3 us -> 9.75 us  [products(): pl.pallas_call(product_kernel, in_specs=[pl.BlockSpec(memory_space=pltpu....]
  transfers between devices with their start and end apart: 16 -> 16, of which waited for: 8 -> 10; matrix products, arithmetic and copies ran while one was open for 2% -> 3% of each run, Pallas kernels for 4% -> 2%
where the time goes in v7:
time: 216 us
  blocking collectives  75.7 us (35%)
  waiting for transfers between devices  69.4 us (32%)
  starting transfers between devices  33.2 us (15%)
  Pallas kernels  19 us (9%)
  local copies, waits for them, and re-layouts  16.9 us (8%)
    all_to_all x4, blocking collectives, all_to_all(): return lax.all_to_all(x, axes, split_axis=0, concat_axis=0, tiled=True)  75.7 us
    ppermute x14, waiting for transfers between devices, shift(): return lax.ppermute(x, 'z', [(i, (i + by) % SLABS) for i in range(SLABS)])  59.5 us
    ppermute x14, starting transfers between devices, shift(): return lax.ppermute(x, 'z', [(i, (i + by) % SLABS) for i in range(SLABS)])  19.7 us
    all_to_all x2, starting transfers between devices, all_to_all(): return lax.all_to_all(x, axes, split_axis=0, concat_axis=0, tiled=True)  13.5 us
    all_to_all x2, waiting for transfers between devices, all_to_all(): return lax.all_to_all(x, axes, split_axis=0, concat_axis=0, tiled=True)  9.9 us
    pallas_call x1, Pallas kernels, products(): pl.pallas_call(product_kernel, in_specs=[pl.BlockSpec(memory_space=pltpu....  9.75 us
    transpose x2, local copies, waits for them, and re-layouts, per_device(): jnp.transpose(x, (2, 1, 0)).reshape(GROUPS, -1, cols, rows)  7.25 us
    pallas_call x1, Pallas kernels, post(): pl.pallas_call(post_kernel, grid=(rows // STEP_ROWS,), in_specs=[tile, pl...  5.98 us
  transfers between devices with their start and end apart: 16, of which 10 were waited for; matrix products, arithmetic and copies ran while one was open for 3% of the time, Pallas kernels for 2%

profile of v7, /device:TPU:1, one launch (start us, length us, event | category | flops | bytes accessed | tf_op | source)
XLA Modules:
  0.0 215.8 jit_solution(1945710760568800622)
XLA Ops:
  0.7 3.3 %copy.16 = bf16[128,32,128]{2,1,0:T(8,128)(2,1)} copy(bf16[128,32,128]{0,1,2:T(8,128)(2,1)} %bitcast.33) | data formatting | bytes 2097152 | tf_op jit(solution)/shard_map/transpose | solution.py:276
  3.9 8.6 %all-to-all-start = ((bf16[32,4,32,128]{3,2,1,0:T(8,128)(2,1)}), bf16[32,4,32,128]{3,2,1,0:T(8,128)(2,1)}, u32[]{:S(2)}, u32[]{:S(2)}) async-start(bf16[32,4,32,128]{3,2,1,0:T(8,128)(2,1)} %bitcast.2), calls=%async_computation | async-start | bytes 2097152 | tf_op jit(solution)/shard_map/all_to_all | solution.py:21
  12.6 3.3 %gated_projections.1 = (bf16[128,32,256]{2,1,0:T(8,128)(2,1)S(1)}, bf16[128,512]{1,0:T(8,128)(2,1)S(1)}) custom-call(bf16[128,32,128]{2,1,0:T(8,128)(2,1)S(1)} %copy-done, f32[1,128]{1,0:T(1,128)S(1)} %bitcast.23, f32[1,128]{1,0:T(1,128)S(1)} %bitcast.25, bf16[128,512]{1,0:T(8,128)(2,1)S(1)} %copy-done.1), custom_call_target="tpu_custom_call" | custom-call | flops 536870912 | bytes 12582912 | tf_op jit(solution)/shard_map/gated_projections/pallas_call | solution.py:68
  15.9 4.0 %copy.17 = bf16[256,32,128]{2,1,0:T(8,128)(2,1)} copy(bf16[256,32,128]{0,1,2:T(8,128)(2,1)S(1)} %bitcast.21) | data formatting | bytes 4194304 | tf_op jit(solution)/shard_map/transpose | solution.py:276
  19.9 9.9 %all-to-all-done = bf16[32,4,32,128]{3,2,1,0:T(8,128)(2,1)} async-done(((bf16[32,4,32,128]{3,2,1,0:T(8,128)(2,1)}), bf16[32,4,32,128]{3,2,1,0:T(8,128)(2,1)}, u32[]{:S(2)}, u32[]{:S(2)}) %all-to-all-start) | async-done | bytes 1048608 | tf_op jit(solution)/shard_map/all_to_all | solution.py:21
  29.8 1.9 slice.20.refs_0_
  31.7 5.6 %collective-permute-start.1 = (bf16[32,2,32,128]{3,2,1,0:T(8,128)(2,1)}, bf16[32,2,32,128]{3,2,1,0:T(8,128)(2,1)}, u32[]{:S(2)}, u32[]{:S(2)}) collective-permute-start(bf16[32,2,32,128]{3,2,1,0:T(8,128)(2,1)} %slice.20.refs_0_), channel_id=1, source_target_pairs={{0,14},{2,0},{4,2},{6,4},{8,6},{10,8},{12,10},{14,12},{1,15},{3,1}... | collective-permute-start | bytes 1572872 | tf_op jit(solution)/shard_map/ppermute | solution.py:25
  37.3 1.9 slice.16.refs_8_
  39.2 2.7 %collective-permute-start.5 = (bf16[32,2,32,128]{3,2,1,0:T(8,128)(2,1)}, bf16[32,2,32,128]{3,2,1,0:T(8,128)(2,1)}, u32[]{:S(2)}, u32[]{:S(2)}) collective-permute-start(bf16[32,2,32,128]{3,2,1,0:T(8,128)(2,1)} %slice.16.refs_8_), channel_id=1, source_target_pairs={{0,14},{2,0},{4,2},{6,4},{8,6},{10,8},{12,10},{14,12},{1,15},{3,1}... | collective-permute-start | bytes 1572872 | tf_op jit(solution)/shard_map/ppermute | solution.py:25
  41.8 4.9 %all-to-all-start.1 = ((bf16[32,8,32,128]{3,2,1,0:T(8,128)(2,1)}), bf16[32,8,32,128]{3,2,1,0:T(8,128)(2,1)S(1)}, u32[]{:S(2)}, u32[]{:S(2)}) async-start(bf16[32,8,32,128]{3,2,1,0:T(8,128)(2,1)} %bitcast.29), calls=%async_computation.1 | async-start | bytes 4194304 | tf_op jit(solution)/shard_map/all_to_all | solution.py:21
  46.7 1.8 collective-permute-done.1.refs_2_
  48.5 3.1 %collective-permute-done.refs_1_ = bf16[32,2,32,128]{3,2,1,0:T(8,128)(2,1)} collective-permute-done((bf16[32,2,32,128]{3,2,1,0:T(8,128)(2,1)}, bf16[32,2,32,128]{3,2,1,0:T(8,128)(2,1)}, u32[]{:S(2)}, u32[]{:S(2)}) %collective-permute-start) | collective-permute-done | bytes 524320 | tf_op jit(solution)/shard_map/ppermute | solution.py:25
  51.6 2.7 %collective-permute-start.3 = (bf16[32,2,32,128]{3,2,1,0:T(8,128)(2,1)}, bf16[32,2,32,128]{3,2,1,0:T(8,128)(2,1)S(1)}, u32[]{:S(2)}, u32[]{:S(2)}) collective-permute-start(bf16[32,2,32,128]{3,2,1,0:T(8,128)(2,1)} %collective-permute-done.1.refs_2_), channel_id=1, source_target_pairs={{0,14},{2,0},{4,2},{6,4},{8,6},{10,8},{12,10},{14,12},{1,15},{3,1}... | collective-permute-start | bytes 1572872 | tf_op jit(solution)/shard_map/ppermute | solution.py:25
  54.3 5.5 %collective-permute-done.5.refs_10_ = bf16[32,2,32,128]{3,2,1,0:T(8,128)(2,1)} collective-permute-done((bf16[32,2,32,128]{3,2,1,0:T(8,128)(2,1)}, bf16[32,2,32,128]{3,2,1,0:T(8,128)(2,1)}, u32[]{:S(2)}, u32[]{:S(2)}) %collective-permute-start.5) | collective-permute-done | bytes 524320 | tf_op jit(solution)/shard_map/ppermute | solution.py:25
  59.7 3.1 %collective-permute-done.4.refs_9_ = bf16[32,2,32,128]{3,2,1,0:T(8,128)(2,1)} collective-permute-done((bf16[32,2,32,128]{3,2,1,0:T(8,128)(2,1)}, bf16[32,2,32,128]{3,2,1,0:T(8,128)(2,1)}, u32[]{:S(2)}, u32[]{:S(2)}) %collective-permute-start.4) | collective-permute-done | bytes 524320 | tf_op jit(solution)/shard_map/ppermute | solution.py:25
  62.8 2.7 %collective-permute-start.9 = (bf16[32,2,32,128]{3,2,1,0:T(8,128)(2,1)}, bf16[32,2,32,128]{3,2,1,0:T(8,128)(2,1)S(1)}, u32[]{:S(2)}, u32[]{:S(2)}) collective-permute-start(bf16[32,2,32,128]{3,2,1,0:T(8,128)(2,1)} %collective-permute-done.5.refs_10_), channel_id=1, source_target_pairs={{0,14},{2,0},{4,2},{6,4},{8,6},{10,8},{12,10},{14,12},{1,15},{3,1}... | collective-permute-start | bytes 1572872 | tf_op jit(solution)/shard_map/ppermute | solution.py:25
  65.5 8.5 %collective-permute-done.2.refs_3_ = bf16[32,2,32,128]{3,2,1,0:T(8,128)(2,1)S(1)} collective-permute-done((bf16[32,2,32,128]{3,2,1,0:T(8,128)(2,1)}, bf16[32,2,32,128]{3,2,1,0:T(8,128)(2,1)S(1)}, u32[]{:S(2)}, u32[]{:S(2)}) %collective-permute-start.2) | collective-permute-done | bytes 524320 | tf_op jit(solution)/shard_map/ppermute | solution.py:25
  74.0 0.8 copy-done.5
  74.8 2.7 %collective-permute-start.7 = (bf16[32,2,32,128]{3,2,1,0:T(8,128)(2,1)S(1)}, bf16[32,2,32,128]{3,2,1,0:T(8,128)(2,1)S(1)}, u32[]{:S(2)}, u32[]{:S(2)}) collective-permute-start(bf16[32,2,32,128]{3,2,1,0:T(8,128)(2,1)S(1)} %collective-permute-done.3.refs_4_), channel_id=1, source_target_pairs={{0,14},{2,0},{4,2},{6,4},{8,6},{10,8},{12,10},{14,12},{1,15},{3,1}... | collective-permute-start | bytes 1572872 | tf_op jit(solution)/shard_map/ppermute | solution.py:25
  77.4 7.8 %collective-permute-done.8.refs_11_ = bf16[32,2,32,128]{3,2,1,0:T(8,128)(2,1)S(1)} collective-permute-done((bf16[32,2,32,128]{3,2,1,0:T(8,128)(2,1)}, bf16[32,2,32,128]{3,2,1,0:T(8,128)(2,1)S(1)}, u32[]{:S(2)}, u32[]{:S(2)}) %collective-permute-start.8) | collective-permute-done | bytes 524320 | tf_op jit(solution)/shard_map/ppermute | solution.py:25
  85.5 2.7 %collective-permute-start.12 = (bf16[32,2,32,128]{3,2,1,0:T(8,128)(2,1)S(1)}, bf16[32,2,32,128]{3,2,1,0:T(8,128)(2,1)}, u32[]{:S(2)}, u32[]{:S(2)}) collective-permute-start(bf16[32,2,32,128]{3,2,1,0:T(8,128)(2,1)S(1)} %collective-permute-done.9.refs_12_), channel_id=1, source_target_pairs={{0,14},{2,0},{4,2},{6,4},{8,6},{10,8},{12,10},{14,12},{1,15},{3,1}... | collective-permute-start | bytes 1572872 | tf_op jit(solution)/shard_map/ppermute | solution.py:25
  88.1 8.4 %collective-permute-done.6.refs_5_ = bf16[32,2,32,128]{3,2,1,0:T(8,128)(2,1)} collective-permute-done((bf16[32,2,32,128]{3,2,1,0:T(8,128)(2,1)S(1)}, bf16[32,2,32,128]{3,2,1,0:T(8,128)(2,1)}, u32[]{:S(2)}, u32[]{:S(2)}) %collective-permute-start.6) | collective-permute-done | bytes 524320 | tf_op jit(solution)/shard_map/ppermute | solution.py:25
  96.6 11.0 %collective-permute-done.11.refs_13_ = bf16[32,2,32,128]{3,2,1,0:T(8,128)(2,1)S(1)} collective-permute-done((bf16[32,2,32,128]{3,2,1,0:T(8,128)(2,1)S(1)}, bf16[32,2,32,128]{3,2,1,0:T(8,128)(2,1)S(1)}, u32[]{:S(2)}, u32[]{:S(2)}) %collective-permute-start.11) | collective-permute-done | bytes 524320 | tf_op jit(solution)/shard_map/ppermute | solution.py:25
  108.5 10.5 %collective-permute-done.10.refs_7_ = bf16[32,2,32,128]{3,2,1,0:T(8,128)(2,1)} collective-permute-done((bf16[32,2,32,128]{3,2,1,0:T(8,128)(2,1)}, bf16[32,2,32,128]{3,2,1,0:T(8,128)(2,1)}, u32[]{:S(2)}, u32[]{:S(2)}) %collective-permute-start.10) | collective-permute-done | bytes 524320 | tf_op jit(solution)/shard_map/ppermute | solution.py:25
  119.0 9.8 %triangle_products.1 = bf16[32,4,2,32,128]{4,3,2,1,0:T(8,128)(2,1)} custom-call(s32[1]{0:T(128)} %bitcast.slab_ref, bf16[32,4,2,32,128]{4,3,2,1,0:T(8,128)(2,1)} %bitcast.27, bf16[32,2,32,128]{3,2,1,0:T(8,128)(2,1)} %slice.20.refs_0_, bf16[32,2,32,128]{3,2,1,0:T(8,128)(2,1)} %collective-permute-done.refs_1_, ...), custom_call_target="tpu_custom_call" | custom-call | flops 2147483648 | bytes 12582912 | tf_op jit(solution)/shard_map/triangle_products/pallas_call | solution.py:243
  128.8 36.5 %all_to_all.30 = bf16[32,8,32,128]{3,2,1,0:T(8,128)(2,1)} all-to-all(bf16[32,8,32,128]{3,2,1,0:T(8,128)(2,1)} %bitcast.28), channel_id=1, replica_groups=mesh['y'=4,'xh'=2,'xl'=2,'z'=8,'c'=2] {'y','xh','xl','c'}, dimensions={0} | all-to-all | bytes 4194304 | tf_op jit(solution)/shard_map/all_to_all | solution.py:21
  165.3 3.9 %copy.18 = bf16[256,32,128]{0,1,2:T(8,128)(2,1)S(1)} copy(bf16[256,32,128]{2,1,0:T(8,128)(2,1)} %bitcast.30) | data formatting | bytes 4194304 | tf_op jit(solution)/shard_map/reshape | solution.py:277
  169.2 6.0 %input_gradients.1 = (bf16[128,32,128]{2,1,0:T(8,128)(2,1)}, f32[768,128]{1,0:T(8,128)S(1)}) custom-call(bf16[128,32,128]{2,1,0:T(8,128)(2,1)S(1)} %copy-done, bf16[128,32,256]{2,1,0:T(8,128)(2,1)S(1)} %bitcast.20, f32[1,128]{1,0:T(1,128)S(1)} %bitcast.24, f32[1,128]{1,0:T(1,128)S(1)} %bitcast.26, bf16[128,512]{1,0:T(8,128)(2,1)S(1)} %get-tuple-element.40.ordered_ref), custom_call_target="tpu_custom_call" | custom-call | flops 1610612736 | bytes 20971520 | tf_op jit(solution)/shard_map/input_gradients/pallas_call | solution.py:141
  175.2 13.7 %all_to_all.31 = f32[32,24,128]{2,1,0:T(8,128)S(1)} all-to-all(f32[32,24,128]{2,1,0:T(8,128)S(1)} %bitcast.22), channel_id=1, replica_groups=mesh['y'=4,'xh'=2,'xl'=2,'z'=8,'c'=2] {'y','xh','xl','c'}, dimensions={0} | all-to-all | bytes 786432 | tf_op jit(solution)/shard_map/all_to_all | solution.py:21
  188.9 10.0 %all_to_all.32 = f32[8,24,128]{2,1,0:T(8,128)S(1)} all-to-all(f32[8,24,128]{2,1,0:T(8,128)S(1)} %broadcast_in_dim.6), channel_id=1, replica_groups=mesh['y'=4,'xh'=2,'xl'=2,'z'=8,'c'=2] {'z'}, dimensions={0} | all-to-all | bytes 196608 | tf_op jit(solution)/shard_map/all_to_all | solution.py:21
  199.0 15.4 %all_to_all.33 = f32[32,24,128]{2,1,0:T(8,128)S(1)} all-to-all(f32[32,24,128]{2,1,0:T(8,128)S(1)} %broadcast_in_dim.7), channel_id=1, replica_groups=mesh['y'=4,'xh'=2,'xl'=2,'z'=8,'c'=2] {'y','xh','xl','c'}, dimensions={0} | all-to-all | bytes 786432 | tf_op jit(solution)/shard_map/all_to_all | solution.py:21
  214.5 0.7 copy.22
  (43 shorter events, 1.9 us)
Async XLA Ops:
  0.6 12.0 %copy-start = (bf16[128,32,128]{2,1,0:T(8,128)(2,1)S(1)}, bf16[128,32,128]{2,1,0:T(8,128)(2,1)}, u32[]{:S(2)}) copy-start(bf16[128,32,128]{2,1,0:T(8,128)(2,1)} %pair_ref.3) | copy-start | bytes 3145732
  0.6 12.0 %copy-start.1 = (bf16[128,512]{1,0:T(8,128)(2,1)S(1)}, bf16[128,512]{1,0:T(8,128)(2,1)}, u32[]{:S(2)}) copy-start(bf16[128,512]{1,0:T(8,128)(2,1)} %weight_ref.1) | copy-start | bytes 393220
  0.7 12.0 %copy-start.2 = (f32[128]{0:T(128)S(1)}, f32[128]{0:T(128)}, u32[]{:S(2)}) copy-start(f32[128]{0:T(128)} %param.6) | copy-start | bytes 1540
  0.7 12.0 %copy-start.3 = (f32[128]{0:T(128)S(1)}, f32[128]{0:T(128)}, u32[]{:S(2)}) copy-start(f32[128]{0:T(128)} %param.7) | copy-start | bytes 1540
  3.9 25.9 %all-to-all-start = ((bf16[32,4,32,128]{3,2,1,0:T(8,128)(2,1)}), bf16[32,4,32,128]{3,2,1,0:T(8,128)(2,1)}, u32[]{:S(2)}, u32[]{:S(2)}) async-start(bf16[32,4,32,128]{3,2,1,0:T(8,128)(2,1)} %bitcast.2), calls=%async_computation | async-start | bytes 2097152 | tf_op jit(solution)/shard_map/all_to_all | solution.py:21
  31.7 16.8 %collective-permute-start.1 = (bf16[32,2,32,128]{3,2,1,0:T(8,128)(2,1)}, bf16[32,2,32,128]{3,2,1,0:T(8,128)(2,1)}, u32[]{:S(2)}, u32[]{:S(2)}) collective-permute-start(bf16[32,2,32,128]{3,2,1,0:T(8,128)(2,1)} %slice.20.refs_0_), channel_id=1, source_target_pairs={{0,14},{2,0},{4,2},{6,4},{8,6},{10,8},{12,10},{14,12},{1,15},{3,1}... | collective-permute-start | bytes 1572872 | tf_op jit(solution)/shard_map/ppermute | solution.py:25
  37.3 14.3 %collective-permute-start = (bf16[32,2,32,128]{3,2,1,0:T(8,128)(2,1)}, bf16[32,2,32,128]{3,2,1,0:T(8,128)(2,1)}, u32[]{:S(2)}, u32[]{:S(2)}) collective-permute-start(bf16[32,2,32,128]{3,2,1,0:T(8,128)(2,1)} %slice.20.refs_0_), channel_id=1, source_target_pairs={{0,2},{2,4},{4,6},{6,8},{8,10},{10,12},{12,14},{14,0},{1,3},{3,5},... | collective-permute-start | bytes 1572872 | tf_op jit(solution)/shard_map/ppermute | solution.py:25
  39.2 20.6 %collective-permute-start.5 = (bf16[32,2,32,128]{3,2,1,0:T(8,128)(2,1)}, bf16[32,2,32,128]{3,2,1,0:T(8,128)(2,1)}, u32[]{:S(2)}, u32[]{:S(2)}) collective-permute-start(bf16[32,2,32,128]{3,2,1,0:T(8,128)(2,1)} %slice.16.refs_8_), channel_id=1, source_target_pairs={{0,14},{2,0},{4,2},{6,4},{8,6},{10,8},{12,10},{14,12},{1,15},{3,1}... | collective-permute-start | bytes 1572872 | tf_op jit(solution)/shard_map/ppermute | solution.py:25
  41.8 21.0 %collective-permute-start.4 = (bf16[32,2,32,128]{3,2,1,0:T(8,128)(2,1)}, bf16[32,2,32,128]{3,2,1,0:T(8,128)(2,1)}, u32[]{:S(2)}, u32[]{:S(2)}) collective-permute-start(bf16[32,2,32,128]{3,2,1,0:T(8,128)(2,1)} %slice.16.refs_8_), channel_id=1, source_target_pairs={{0,2},{2,4},{4,6},{6,8},{8,10},{10,12},{12,14},{14,0},{1,3},{3,5},... | collective-permute-start | bytes 1572872 | tf_op jit(solution)/shard_map/ppermute | solution.py:25
  41.8 66.7 %all-to-all-start.1 = ((bf16[32,8,32,128]{3,2,1,0:T(8,128)(2,1)}), bf16[32,8,32,128]{3,2,1,0:T(8,128)(2,1)S(1)}, u32[]{:S(2)}, u32[]{:S(2)}) async-start(bf16[32,8,32,128]{3,2,1,0:T(8,128)(2,1)} %bitcast.29), calls=%async_computation.1 | async-start | bytes 4194304 | tf_op jit(solution)/shard_map/all_to_all | solution.py:21
  51.6 22.4 %collective-permute-start.2 = (bf16[32,2,32,128]{3,2,1,0:T(8,128)(2,1)}, bf16[32,2,32,128]{3,2,1,0:T(8,128)(2,1)S(1)}, u32[]{:S(2)}, u32[]{:S(2)}) collective-permute-start(bf16[32,2,32,128]{3,2,1,0:T(8,128)(2,1)} %collective-permute-done.refs_1_), channel_id=1, source_target_pairs={{0,2},{2,4},{4,6},{6,8},{8,10},{10,12},{12,14},{14,0},{1,3},{3,5},... | collective-permute-start | bytes 1572872 | tf_op jit(solution)/shard_map/ppermute | solution.py:25
  51.6 22.4 %collective-permute-start.3 = (bf16[32,2,32,128]{3,2,1,0:T(8,128)(2,1)}, bf16[32,2,32,128]{3,2,1,0:T(8,128)(2,1)S(1)}, u32[]{:S(2)}, u32[]{:S(2)}) collective-permute-start(bf16[32,2,32,128]{3,2,1,0:T(8,128)(2,1)} %collective-permute-done.1.refs_2_), channel_id=1, source_target_pairs={{0,14},{2,0},{4,2},{6,4},{8,6},{10,8},{12,10},{14,12},{1,15},{3,1}... | collective-permute-start | bytes 1572872 | tf_op jit(solution)/shard_map/ppermute | solution.py:25
  62.8 22.4 %collective-permute-start.8 = (bf16[32,2,32,128]{3,2,1,0:T(8,128)(2,1)}, bf16[32,2,32,128]{3,2,1,0:T(8,128)(2,1)S(1)}, u32[]{:S(2)}, u32[]{:S(2)}) collective-permute-start(bf16[32,2,32,128]{3,2,1,0:T(8,128)(2,1)} %collective-permute-done.4.refs_9_), channel_id=1, source_target_pairs={{0,2},{2,4},{4,6},{6,8},{8,10},{10,12},{12,14},{14,0},{1,3},{3,5},... | collective-permute-start | bytes 1572872 | tf_op jit(solution)/shard_map/ppermute | solution.py:25
  62.8 22.4 %collective-permute-start.9 = (bf16[32,2,32,128]{3,2,1,0:T(8,128)(2,1)}, bf16[32,2,32,128]{3,2,1,0:T(8,128)(2,1)S(1)}, u32[]{:S(2)}, u32[]{:S(2)}) collective-permute-start(bf16[32,2,32,128]{3,2,1,0:T(8,128)(2,1)} %collective-permute-done.5.refs_10_), channel_id=1, source_target_pairs={{0,14},{2,0},{4,2},{6,4},{8,6},{10,8},{12,10},{14,12},{1,15},{3,1}... | collective-permute-start | bytes 1572872 | tf_op jit(solution)/shard_map/ppermute | solution.py:25
  73.9 0.8 copy-start.5
  74.7 21.8 %copy-start.6 = (bf16[32,2,32,128]{3,2,1,0:T(8,128)(2,1)}, bf16[32,2,32,128]{3,2,1,0:T(8,128)(2,1)S(1)}, u32[]{:S(2)}) copy-start(bf16[32,2,32,128]{3,2,1,0:T(8,128)(2,1)S(1)} %collective-permute-done.3.refs_4_) | copy-start | bytes 1572868
  74.8 21.8 %collective-permute-start.6 = (bf16[32,2,32,128]{3,2,1,0:T(8,128)(2,1)S(1)}, bf16[32,2,32,128]{3,2,1,0:T(8,128)(2,1)}, u32[]{:S(2)}, u32[]{:S(2)}) collective-permute-start(bf16[32,2,32,128]{3,2,1,0:T(8,128)(2,1)S(1)} %collective-permute-done.2.refs_3_), channel_id=1, source_target_pairs={{0,2},{2,4},{4,6},{6,8},{8,10},{10,12},{12,14},{14,0},{1,3},{3,5},... | collective-permute-start | bytes 1572872 | tf_op jit(solution)/shard_map/ppermute | solution.py:25
  74.8 21.8 %collective-permute-start.7 = (bf16[32,2,32,128]{3,2,1,0:T(8,128)(2,1)S(1)}, bf16[32,2,32,128]{3,2,1,0:T(8,128)(2,1)S(1)}, u32[]{:S(2)}, u32[]{:S(2)}) collective-permute-start(bf16[32,2,32,128]{3,2,1,0:T(8,128)(2,1)S(1)} %collective-permute-done.3.refs_4_), channel_id=1, source_target_pairs={{0,14},{2,0},{4,2},{6,4},{8,6},{10,8},{12,10},{14,12},{1,15},{3,1}... | collective-permute-start | bytes 1572872 | tf_op jit(solution)/shard_map/ppermute | solution.py:25
  85.2 11.3 %copy-start.7 = (bf16[32,2,32,128]{3,2,1,0:T(8,128)(2,1)}, bf16[32,2,32,128]{3,2,1,0:T(8,128)(2,1)S(1)}, u32[]{:S(2)}) copy-start(bf16[32,2,32,128]{3,2,1,0:T(8,128)(2,1)S(1)} %collective-permute-done.8.refs_11_) | copy-start | bytes 1572868
  85.2 22.5 %copy-start.8 = (bf16[32,2,32,128]{3,2,1,0:T(8,128)(2,1)}, bf16[32,2,32,128]{3,2,1,0:T(8,128)(2,1)S(1)}, u32[]{:S(2)}) copy-start(bf16[32,2,32,128]{3,2,1,0:T(8,128)(2,1)S(1)} %collective-permute-done.9.refs_12_) | copy-start | bytes 1572868
  85.2 22.5 %collective-permute-start.11 = (bf16[32,2,32,128]{3,2,1,0:T(8,128)(2,1)S(1)}, bf16[32,2,32,128]{3,2,1,0:T(8,128)(2,1)S(1)}, u32[]{:S(2)}, u32[]{:S(2)}) collective-permute-start(bf16[32,2,32,128]{3,2,1,0:T(8,128)(2,1)S(1)} %collective-permute-done.8.refs_11_), channel_id=1, source_target_pairs={{0,2},{2,4},{4,6},{6,8},{8,10},{10,12},{12,14},{14,0},{1,3},{3,5},... | collective-permute-start | bytes 1572872 | tf_op jit(solution)/shard_map/ppermute | solution.py:25
  85.5 22.2 %collective-permute-start.12 = (bf16[32,2,32,128]{3,2,1,0:T(8,128)(2,1)S(1)}, bf16[32,2,32,128]{3,2,1,0:T(8,128)(2,1)}, u32[]{:S(2)}, u32[]{:S(2)}) collective-permute-start(bf16[32,2,32,128]{3,2,1,0:T(8,128)(2,1)S(1)} %collective-permute-done.9.refs_12_), channel_id=1, source_target_pairs={{0,14},{2,0},{4,2},{6,4},{8,6},{10,8},{12,10},{14,12},{1,15},{3,1}... | collective-permute-start | bytes 1572872 | tf_op jit(solution)/shard_map/ppermute | solution.py:25
  96.5 11.1 %copy-start.9 = (bf16[32,2,32,128]{3,2,1,0:T(8,128)(2,1)}, bf16[32,2,32,128]{3,2,1,0:T(8,128)(2,1)S(1)}, u32[]{:S(2)}) copy-start(bf16[32,2,32,128]{3,2,1,0:T(8,128)(2,1)S(1)} %collective-permute-done.7.refs_6_) | copy-start | bytes 1572868
  96.5 22.4 %collective-permute-start.10 = (bf16[32,2,32,128]{3,2,1,0:T(8,128)(2,1)}, bf16[32,2,32,128]{3,2,1,0:T(8,128)(2,1)}, u32[]{:S(2)}, u32[]{:S(2)}) collective-permute-start(bf16[32,2,32,128]{3,2,1,0:T(8,128)(2,1)} %collective-permute-done.6.refs_5_), channel_id=1, source_target_pairs={{0,2},{2,4},{4,6},{6,8},{8,10},{10,12},{12,14},{14,0},{1,3},{3,5},... | collective-permute-start | bytes 1572872 | tf_op jit(solution)/shard_map/ppermute | solution.py:25
  107.7 0.8 copy-start.10
  107.7 11.3 %collective-permute-start.13 = (bf16[32,2,32,128]{3,2,1,0:T(8,128)(2,1)}, bf16[32,2,32,128]{3,2,1,0:T(8,128)(2,1)}, u32[]{:S(2)}, u32[]{:S(2)}) collective-permute-start(bf16[32,2,32,128]{3,2,1,0:T(8,128)(2,1)} %collective-permute-done.12.refs_14_), channel_id=1, source_target_pairs={{0,14},{2,0},{4,2},{6,4},{8,6},{10,8},{12,10},{14,12},{1,15},{3,1}... | collective-permute-start | bytes 1572872 | tf_op jit(solution)/shard_map/ppermute | solution.py:25
  108.5 10.5 %copy-start.4 = (bf16[32,8,32,128]{3,2,1,0:T(8,128)(2,1)}, bf16[32,8,32,128]{3,2,1,0:T(8,128)(2,1)S(1)}, u32[]{:S(2)}) copy-start(bf16[32,8,32,128]{3,2,1,0:T(8,128)(2,1)S(1)} %all-to-all-done.1) | copy-start | bytes 6291460
